TPU v7x, 32 devices: a whole 2x2x4 slice. The times are simulated.
32 devices in a mesh: dp: 8 (over z, y), mp: 4 (over x, core).
Axes of the slice: x: 2, y: 2, z: 4, core: 2. Of those that a mesh axis runs over, the one named last changes fastest.
Arguments:
- patches: bfloat16 [32, 197, 768], P(('dp', 'mp')), may hold values from -6 to 6
- row_mask: int32 [32, 197], P(('dp', 'mp')), may hold values from 0 to 1, as said below
- out_grad: bfloat16 [32, 197, 768], P(('dp', 'mp')), may hold values from -6 to 6
- rel_index: int32 [197, 197], replicated, may hold values from 0 to 731
- mask_token: float32 [768], replicated, may hold values from -6 to 6
- ln1_gain: float32 [768], replicated, may hold values from 0.5 to 1.5
- ln1_bias: float32 [768], replicated, may hold values from -4 to 4
- qkv_weight: bfloat16 [768, 2304], replicated, may hold values from -0.21875 to 0.21875
- query_bias: float32 [768], replicated, may hold values from -6 to 6
- value_bias: float32 [768], replicated, may hold values from -6 to 6
- rel_table: float32 [732, 12], replicated, may hold values from -6 to 6
- proj_weight: bfloat16 [768, 768], replicated, may hold values from -0.625 to 0.625
- proj_bias: float32 [768], replicated, may hold values from -4 to 4
- gamma1: float32 [768], replicated, may hold values from 0.5 to 1.5
- ln2_gain: float32 [768], replicated, may hold values from 0.5 to 1.5
- ln2_bias: float32 [768], replicated, may hold values from -4 to 4
- fc1_weight: bfloat16 [768, 3072], P(None, 'mp'), may hold values from -0.21875 to 0.21875
- fc1_bias: bfloat16 [3072], P('mp'), may hold values from -6 to 6
- fc2_weight: bfloat16 [3072, 768], P('mp'), may hold values from -0.109375 to 0.109375
- fc2_bias: float32 [768], replicated, may hold values from -4 to 4
- gamma2: float32 [768], replicated, may hold values from 0.5 to 1.5
Outputs:
- layer_out: bfloat16 [32, 197, 768], P(('dp', 'mp'))
- patch_grad: float32 [32, 197, 768], P(('dp', 'mp'))
- mask_token_grad: float32 [768], replicated
- ln1_gain_grad: float32 [768], replicated
- ln1_bias_grad: float32 [768], replicated
- qkv_weight_grad: float32 [768, 2304], P('dp')
- query_bias_grad: float32 [768], replicated
- value_bias_grad: float32 [768], replicated
- rel_table_grad: float32 [732, 12], replicated
- proj_weight_grad: float32 [768, 768], P('dp')
- proj_bias_grad: float32 [768], replicated
- gamma1_grad: float32 [768], replicated
- ln2_gain_grad: float32 [768], replicated
- ln2_bias_grad: float32 [768], replicated
- fc1_weight_grad: float32 [768, 3072], P('dp', 'mp')
- fc1_bias_grad: float32 [3072], P('mp')
- fc2_weight_grad: float32 [3072, 768], P('mp', 'dp')
- fc2_bias_grad: float32 [768], replicated
- gamma2_grad: float32 [768], replicated
Inputs may be any that keep to these rules, and one draw needn't show every extreme that they name: `row_mask`: row 0 of every image (the class row) is never masked. The number of masked rows differs widely from image to image, and in some images every one of the 196 patch rows is masked.
All inputs are finite; a program needn't handle non-finite values.
Results may differ from a plain program's by a relative error of at most 0.015.
Values may be sent and summed in bfloat16 or wider, within the bound.
No kernel may reach another device: no remote copies, remote signals or barrier semaphores. Data moves between devices by JAX's collectives and lax.ppermute only.
A program may use at most 128 MiB of HBM per device.

v0:
```python
import jax
import jax.numpy as jnp
from jax import lax
from jax.sharding import PartitionSpec as P


def norm_rows(values, gain, shift):
    middle = jnp.mean(values, axis=-1, keepdims=True)
    centred = values - middle
    spread = jnp.mean(centred * centred, axis=-1, keepdims=True)
    return centred * lax.rsqrt(spread + 1e-06) * gain + shift


def gelu_exact(values):
    return jax.nn.gelu(values, approximate=False)


def contract_rows(left_side, right_side):
    return lax.dot_general(
        left_side, right_side, (((0,), (0,)), ((), ())), preferred_element_type=jnp.float32
    )


def contract_cols(left_side, right_side):
    return lax.dot_general(
        left_side, right_side, (((1,), (1,)), ((), ())), preferred_element_type=jnp.float32
    )


def on_device(
    patches,
    row_mask,
    out_grad,
    rel_index,
    mask_token,
    ln1_gain,
    ln1_bias,
    qkv_weight,
    query_bias,
    value_bias,
    rel_table,
    proj_weight,
    proj_bias,
    gamma1,
    ln2_gain,
    ln2_bias,
    fc1_weight,
    fc1_bias,
    fc2_weight,
    fc2_bias,
    gamma2,
):
    images_here, seq_rows, model_width = patches.shape
    head_count = rel_table.shape[1]
    head_size = model_width // head_count
    score_scale = head_size ** (-0.5)
    row_count = images_here * seq_rows
    shaped = (images_here, seq_rows, head_count, head_size)
    picked = (row_mask > 0).reshape(row_count, 1)
    start = jnp.where(
        picked, mask_token, patches.astype(jnp.float32).reshape(row_count, model_width)
    )
    normed_f, pull_first = jax.vjp(norm_rows, start, ln1_gain, ln1_bias)
    normed = normed_f.astype(jnp.bfloat16)
    bias_row = jnp.concatenate([query_bias, jnp.zeros_like(query_bias), value_bias])
    qkv = jnp.dot(normed, qkv_weight, preferred_element_type=jnp.float32) + bias_row
    query_rows = (qkv[:, :model_width] * score_scale).astype(jnp.bfloat16).reshape(shaped)
    key_rows = qkv[:, model_width : 2 * model_width].astype(jnp.bfloat16).reshape(shaped)
    value_rows = qkv[:, 2 * model_width :].astype(jnp.bfloat16).reshape(shaped)
    rel_bias = jnp.transpose(rel_table[rel_index], (2, 0, 1))
    scores = (
        jnp.einsum("bqhe,bkhe->bhqk", query_rows, key_rows, preferred_element_type=jnp.float32)
        + rel_bias
    )
    row_max = jnp.max(scores, axis=-1, keepdims=True)
    row_total = jnp.sum(jnp.exp(scores - row_max), axis=-1, keepdims=True)
    log_total = row_max + jnp.log(row_total)
    probs_b = jnp.exp(scores - log_total).astype(jnp.bfloat16)
    mixed = jnp.einsum("bhqk,bkhe->bqhe", probs_b, value_rows, preferred_element_type=jnp.float32)
    mixed = mixed.astype(jnp.bfloat16).reshape(row_count, model_width)
    attended = jnp.dot(mixed, proj_weight, preferred_element_type=jnp.float32) + proj_bias
    hidden = start + gamma1 * attended
    inner_f, pull_second = jax.vjp(norm_rows, hidden, ln2_gain, ln2_bias)
    inner = inner_f.astype(jnp.bfloat16)
    cotangent = out_grad.astype(jnp.float32).reshape(row_count, model_width) * picked.astype(
        jnp.float32
    )
    d_branch = (gamma2 * cotangent).astype(jnp.bfloat16)
    fc2_bias_grad = jnp.sum(d_branch.astype(jnp.float32), axis=0)
    everyone = lax.all_gather(inner, "mp", axis=0, tiled=True)
    pre = jnp.dot(everyone, fc1_weight, preferred_element_type=jnp.float32) + fc1_bias
    act_f, pull_gelu = jax.vjp(gelu_exact, pre)
    act = act_f.astype(jnp.bfloat16)
    part = act
    branch = (
        lax.psum_scatter(
            jnp.dot(part, fc2_weight, preferred_element_type=jnp.float32).astype(jnp.bfloat16),
            "mp",
            scatter_dimension=0,
            tiled=True,
        ).astype(jnp.float32)
        + fc2_bias
    )
    d_branch_all = lax.all_gather(d_branch, "mp", axis=0, tiled=True)
    fc2_grad = contract_rows(act, d_branch_all)
    d_act = contract_cols(d_branch_all, fc2_weight)
    d_pre = pull_gelu(d_act)[0].astype(jnp.bfloat16)
    fc1_bias_grad = jnp.sum(d_pre.astype(jnp.float32), axis=0)
    fc1_grad = contract_rows(everyone, d_pre)
    part = d_pre
    d_inner = lax.psum_scatter(
        contract_cols(part, fc1_weight), "mp", scatter_dimension=0, tiled=True
    )
    layer_out = (
        (hidden + gamma2 * branch).astype(jnp.bfloat16).reshape(images_here, seq_rows, model_width)
    )
    gamma2_grad = jnp.sum(cotangent * branch, axis=0)
    d_hidden_norm, ln2_gain_grad, ln2_bias_grad = pull_second(d_inner)
    d_hidden = cotangent + d_hidden_norm
    gamma1_grad = jnp.sum(d_hidden * attended, axis=0)
    d_attended = (gamma1 * d_hidden).astype(jnp.bfloat16)
    proj_bias_grad = jnp.sum(d_attended.astype(jnp.float32), axis=0)
    proj_grad = contract_rows(mixed, d_attended)
    d_mixed = contract_cols(d_attended, proj_weight).astype(jnp.bfloat16).reshape(shaped)
    again = (
        jnp.einsum("bqhe,bkhe->bhqk", query_rows, key_rows, preferred_element_type=jnp.float32)
        + rel_bias
    )
    probs_f = jnp.exp(again - log_total)
    probs_again = probs_f.astype(jnp.bfloat16)
    d_probs = jnp.einsum("bqhe,bkhe->bhqk", d_mixed, value_rows, preferred_element_type=jnp.float32)
    d_scores = probs_f * (d_probs - jnp.sum(probs_f * d_probs, axis=-1, keepdims=True))
    d_scores = d_scores.astype(jnp.bfloat16)
    d_query = (
        jnp.einsum("bhqk,bkhe->bqhe", d_scores, key_rows, preferred_element_type=jnp.float32)
        * score_scale
    )
    d_key = jnp.einsum("bhqk,bqhe->bkhe", d_scores, query_rows, preferred_element_type=jnp.float32)
    d_value = jnp.einsum(
        "bhqk,bqhe->bkhe", probs_again, d_mixed, preferred_element_type=jnp.float32
    )
    rel_pairs = jnp.transpose(jnp.sum(d_scores.astype(jnp.float32), axis=0), (1, 2, 0))
    rel_grad = jax.ops.segment_sum(
        rel_pairs.reshape(seq_rows * seq_rows, head_count),
        rel_index.reshape(-1),
        num_segments=rel_table.shape[0],
    )
    d_qkv = jnp.concatenate(
        [
            d_query.reshape(row_count, model_width),
            d_key.reshape(row_count, model_width),
            d_value.reshape(row_count, model_width),
        ],
        axis=1,
    ).astype(jnp.bfloat16)
    d_qkv_f = d_qkv.astype(jnp.float32)
    query_bias_grad = jnp.sum(d_qkv_f[:, :model_width], axis=0)
    value_bias_grad = jnp.sum(d_qkv_f[:, 2 * model_width :], axis=0)
    qkv_grad = contract_rows(normed, d_qkv)
    d_normed = contract_cols(d_qkv, qkv_weight)
    d_start_norm, ln1_gain_grad, ln1_bias_grad = pull_first(d_normed)
    d_start = d_hidden + d_start_norm
    patch_grad = jnp.where(picked, 0.0, d_start).reshape(images_here, seq_rows, model_width)
    mask_token_grad = jnp.sum(jnp.where(picked, d_start, 0.0), axis=0)
    big = (
        lax.psum_scatter(qkv_grad, "dp", scatter_dimension=0, tiled=True),
        lax.psum_scatter(proj_grad, "dp", scatter_dimension=0, tiled=True),
        lax.psum_scatter(fc1_grad, "dp", scatter_dimension=0, tiled=True),
        lax.psum_scatter(fc2_grad, "dp", scatter_dimension=1, tiled=True),
    )
    small = lax.psum(
        (
            fc1_bias_grad,
            mask_token_grad,
            ln1_gain_grad,
            ln1_bias_grad,
            query_bias_grad,
            value_bias_grad,
            rel_grad,
            proj_bias_grad,
            gamma1_grad,
            ln2_gain_grad,
            ln2_bias_grad,
            fc2_bias_grad,
            gamma2_grad,
        ),
        "dp",
    )
    whole = (
        lax.psum(big[0].astype(jnp.bfloat16), "mp").astype(jnp.float32),
        lax.psum(big[1].astype(jnp.bfloat16), "mp").astype(jnp.float32),
        lax.psum(small[1].astype(jnp.bfloat16), "mp").astype(jnp.float32),
        lax.psum(small[2].astype(jnp.bfloat16), "mp").astype(jnp.float32),
        lax.psum(small[3].astype(jnp.bfloat16), "mp").astype(jnp.float32),
        lax.psum(small[4].astype(jnp.bfloat16), "mp").astype(jnp.float32),
        lax.psum(small[5].astype(jnp.bfloat16), "mp").astype(jnp.float32),
        lax.psum(small[6].astype(jnp.bfloat16), "mp").astype(jnp.float32),
        lax.psum(small[7].astype(jnp.bfloat16), "mp").astype(jnp.float32),
        lax.psum(small[8].astype(jnp.bfloat16), "mp").astype(jnp.float32),
        lax.psum(small[9].astype(jnp.bfloat16), "mp").astype(jnp.float32),
        lax.psum(small[10].astype(jnp.bfloat16), "mp").astype(jnp.float32),
        lax.psum(small[11].astype(jnp.bfloat16), "mp").astype(jnp.float32),
        lax.psum(small[12].astype(jnp.bfloat16), "mp").astype(jnp.float32),
    )
    return (
        layer_out,
        patch_grad,
        whole[2],
        whole[3],
        whole[4],
        whole[0],
        whole[5],
        whole[6],
        whole[7],
        whole[1],
        whole[8],
        whole[9],
        whole[10],
        whole[11],
        big[2],
        small[0],
        big[3],
        whole[12],
        whole[13],
    )


def solution(mesh):
    placed = (
        P(("dp", "mp"), None, None),
        P(("dp", "mp"), None),
        P(("dp", "mp"), None, None),
        P(),
        P(),
        P(),
        P(),
        P(),
        P(),
        P(),
        P(),
        P(),
        P(),
        P(),
        P(),
        P(),
        P(None, "mp"),
        P("mp"),
        P("mp", None),
        P(),
        P(),
    )
    return jax.shard_map(
        on_device,
        mesh=mesh,
        in_specs=placed,
        out_specs=(
            P(("dp", "mp"), None, None),
            P(("dp", "mp"), None, None),
            P(),
            P(),
            P(),
            P("dp", None),
            P(),
            P(),
            P(),
            P("dp", None),
            P(),
            P(),
            P(),
            P(),
            P("dp", "mp"),
            P("mp"),
            P("mp", "dp"),
            P(),
            P(),
        ),
        check_vma=False,
    )
```

profile of v0, /device:TPU:0, one launch (start us, length us, event | category | flops | bytes accessed | tf_op | source)
XLA Modules:
  0.0 866.2 jit_solution(9534973505054352059)
XLA Ops:
  18.9 3.2 fusion.56
  30.5 142.0 %gather_fusion = f32[38809,12]{1,0:T(8,128)} fusion(f32[732,12]{1,0:T(8,128)} %copy.73, s32[38912]{0:T(1024)} %pad_clamp_fusion), kind=kCustom, calls=%fused_computation | custom fusion | bytes 3880900 | tf_op jit(solution)/shard_map/gather | solution.py:70
  172.5 12.1 %copy.74 = f32[38809,12]{0,1:T(8,128)} copy(f32[38809,12]{1,0:T(8,128)} %gather_fusion) | data formatting | bytes 3725664 | tf_op jit(solution)/shard_map/gather | solution.py:70
  184.6 4.1 reshape.265
  188.7 3.3 copy.75
  192.0 3.9 fusion.54
  206.6 16.0 %all-gather.5.cloned.1.call-done = bf16[4,197,768]{2,1,0:T(8,128)(2,1)} async-done(((bf16[1,197,768]{2,1,0:T(8,128)(2,1)}), bf16[4,197,768]{2,1,0:T(8,128)(2,1)}) %all-gather.5.cloned.1.call-update) | async-done | bytes 1210384 | tf_op jit(solution)/shard_map/all_gather | solution.py:90
  222.5 2.6 reshape.284
  225.2 4.2 fusion.57
  229.3 13.1 %all-gather.7.cloned.1.call-done = bf16[4,197,768]{2,1,0:T(8,128)(2,1)} async-done(((bf16[1,197,768]{2,1,0:T(8,128)(2,1)}), bf16[4,197,768]{2,1,0:T(8,128)(2,1)}) %all-gather.7.cloned.1.call-update) | async-done | bytes 1210384 | tf_op jit(solution)/shard_map/all_gather | solution.py:104
  242.4 2.7 reshape.286
  245.1 9.6 %convert_reduce_fusion = (f32[768]{0:T(1024)}, bf16[788,768]{1,0:T(8,128)(2,1)S(1)}, f32[788,768]{1,0:T(8,128)S(1)}) fusion(f32[788,768]{1,0:T(8,128)} %fusion.57, f32[768]{0:T(1024)} %convert_element_type.176, bf16[788,768]{1,0:T(8,128)(2,1)} %reshape.286, bf16[768,768]{1,0:T(8,128)(2,1)} %param.39), kind=kOutput, calls=%fused_computation.16 | convolution fusion | flops 974950656 | bytes 8448000 | tf_op jit(solution)/shard_map/dot_general | solution.py:25
  258.7 2.6 fusion.58
  261.2 26.3 %fusion.1 = f32[200,768]{1,0:T(8,128)} fusion(f32[788,768]{1,0:T(8,128)} %fusion.58), kind=kCustom, calls=%all-reduce-scatter.1 | all-reduce-scatter fusion | flops 614401 | bytes 3035648
  290.9 17.7 %fusion = bf16[200,768]{1,0:T(8,128)(2,1)} fusion(bf16[788,768]{1,0:T(8,128)(2,1)} %convolution_convert_fusion), kind=kCustom, calls=%all-reduce-scatter | all-reduce-scatter fusion | flops 614401 | bytes 1518080
  313.7 4.0 concatenate.9
  317.7 4.3 concatenate.10
  332.0 2.6 convolution_convert_fusion.4
  336.5 2.8 multiply_reduce_fusion
  343.2 4.3 fusion.45
  347.5 55.4 %reduce-scatter.11.cloned.1.call-done = f32[96,768]{1,0:T(8,128)} async-done(((f32[768,768]{1,0:T(8,128)}), f32[96,768]{1,0:T(8,128)}) %reduce-scatter.11.cloned.1.call-update) | async-done | bytes 294928 | tf_op jit(solution)/shard_map/reduce_scatter | solution.py:167
  404.5 130.0 %reduce-scatter.9.cloned.1.call-done = f32[96,2304]{1,0:T(8,128)} async-done(((f32[768,2304]{1,0:T(8,128)}), f32[96,2304]{1,0:T(8,128)}) %reduce-scatter.9.cloned.1.call-update) | async-done | bytes 884752 | tf_op jit(solution)/shard_map/reduce_scatter | solution.py:166
  536.5 4.5 fusion.61
  541.1 4.6 fusion.60
  547.7 5.2 fusion.14
  552.9 3.3 copy.82
  556.2 3.9 reshape.276
  560.2 3.6 fusion.32
  566.8 11.0 %copy.83 = f32[38809,12]{1,0:T(8,128)} copy(f32[38809,12]{0,1:T(8,128)} %reshape.276) | data formatting | bytes 3725664 | tf_op jit(solution)/shard_map/reshape | solution.py:144
  577.8 208.0 %scatter_custom_fusion = f32[732,12]{1,0:T(8,128)} fusion(s32[38809]{0:T(1024)} %reshape.274, f32[38809,12]{1,0:T(8,128)} %copy.83, f32[]{:T(128)} %constant.39.clone.1), kind=kCustom, calls=%fused_computation.87 | custom fusion | flops 465708 | bytes 35648 | tf_op jit(solution)/shard_map/scatter-add | solution.py:143
  788.2 41.1 %all-reduce.4 = (bf16[732,12]{1,0:T(8,128)(2,1)}, bf16[768]{0:T(1024)(128)(2,1)}, bf16[768]{0:T(1024)(128)(2,1)}, bf16[768]{0:T(1024)(128)(2,1)}, bf16[768]{0:T(...) all-reduce(f32[732,12]{1,0:T(8,128)} %scatter_custom_fusion, ...), channel_id=1, replica_groups=mesh['dp'=8,'mp'=4] {'dp'}, use_global_device_ids=true, to_apply=%region_31.32 | all-reduce | flops 18000 | bytes 109536 | tf_op jit(solution)/shard_map/psum | solution.py:171
  829.3 13.4 %all-reduce.5 = (bf16[732,12]{1,0:T(8,128)(2,1)}, bf16[768]{0:T(1024)(128)(2,1)}, bf16[768]{0:T(1024)(128)(2,1)}, bf16[768]{0:T(1024)(128)(2,1)}, bf16[768]{0:T(...) all-reduce(bf16[732,12]{1,0:T(8,128)(2,1)} %get-tuple-element.88, ...), channel_id=1, replica_groups=mesh['dp'=8,'mp'=4] {'mp'}, use_global_device_ids=true, to_apply=%region_32.33 | all-reduce | flops 17232 | bytes 68928 | tf_op jit(solution)/shard_map/psum | solution.py:197
  (226 shorter events, 85.5 us)
Async XLA Ops:
  7.2 11.7 %copy-start = (bf16[768,2304]{1,0:T(8,128)(2,1)S(1)}, bf16[768,2304]{1,0:T(8,128)(2,1)}, u32[]{:S(2)}) copy-start(bf16[768,2304]{1,0:T(8,128)(2,1)} %param.28) | copy-start | bytes 10616836
  7.2 215.3 %all-gather.5.cloned.1.call-start = ((), (), s32[]{:S(2)}) async-start(), calls=%async_computation.8 | async-start | bytes 1536000 | tf_op jit(solution)/shard_map/all_gather | solution.py:90
  8.1 14.0 %copy-start.39 = (pred[197]{0:T(512)(128)(4,1)}, pred[197]{0:T(512)(128)(4,1)S(1)}, u32[]{:S(2)}) copy-start(pred[197]{0:T(512)(128)(4,1)S(1)} %compare_reduce_fusion) | copy-start | bytes 595
  9.5 12.7 %copy-start.36 = (f32[197]{0:T(256)}, f32[197]{0:T(256)S(1)}, u32[]{:S(2)}) copy-start(f32[197]{0:T(256)S(1)} %broadcast_multiply_fusion.1) | copy-start | bytes 2368
  11.3 10.8 %copy-start.44 = (f32[197]{0:T(256)}, f32[197]{0:T(256)S(1)}, u32[]{:S(2)}) copy-start(f32[197]{0:T(256)S(1)} %fusion.42) | copy-start | bytes 2368
  201.9 40.5 %all-gather.7.cloned.1.call-start = ((), (), s32[]{:S(2)}) async-start(), calls=%async_computation.9 | async-start | bytes 1536000 | tf_op jit(solution)/shard_map/all_gather | solution.py:104
  205.1 197.8 %reduce-scatter.11.cloned.1.call-start = ((), (), s32[]{:S(2)}) async-start(), calls=%async_computation.5 | async-start | bytes 2654208 | tf_op jit(solution)/shard_map/reduce_scatter | solution.py:167
  245.1 9.6 %copy-start.25 = (f32[788,768]{1,0:T(8,128)S(1)}, f32[788,768]{1,0:T(8,128)}, u32[]{:S(2)}) copy-start(f32[788,768]{1,0:T(8,128)} %fusion.57) | copy-start | bytes 7262212
  245.1 9.6 %copy-start.51 = (f32[768]{0:T(1024)S(1)}, f32[768]{0:T(1024)}, u32[]{:S(2)}) copy-start(f32[768]{0:T(1024)} %convert_element_type.176) | copy-start | bytes 9220
  254.7 3.9 copy-start.68
  289.0 28.7 %collective-permute-start.1 = (f32[9,768]{1,0:T(8,128)}, f32[9,768]{1,0:T(8,128)}, u32[]{:S(2)}, u32[]{:S(2)}) collective-permute-start(f32[9,768]{1,0:T(8,128)} %slice.30), channel_id=1, source_target_pairs={{0,1},{1,2},{2,3},{4,5},{5,6},{6,7},{8,9},{9,10},{10,11},{12,13},{... | collective-permute-start | bytes 82952
  309.9 3.8 collective-permute-start
  322.0 6.3 copy-start.21
  322.0 6.3 copy-start.49
  322.0 6.3 copy-start.57
  322.0 7.8 copy-start.17
  331.7 202.7 %reduce-scatter.9.cloned.1.call-start = ((), (), s32[]{:S(2)}) async-start(), calls=%async_computation.4 | async-start | bytes 7962624 | tf_op jit(solution)/shard_map/reduce_scatter | solution.py:166
  347.5 508.3 %all-reduce.9.cloned.1.call-start = ((), (), s32[]{:S(2)}) async-start(), calls=%async_computation.10 | async-start | bytes 1179648 | tf_op jit(solution)/shard_map/psum | solution.py:190
  536.5 322.9 %reduce-scatter.15.cloned.1.call-start = ((), (), s32[]{:S(2)}) async-start(), calls=%async_computation.7 | async-start | bytes 2654208 | tf_op jit(solution)/shard_map/reduce_scatter | solution.py:169
  541.0 318.3 %reduce-scatter.13.cloned.1.call-start = ((), (), s32[]{:S(2)}) async-start(), calls=%async_computation.6 | async-start | bytes 2654208 | tf_op jit(solution)/shard_map/reduce_scatter | solution.py:168
  556.2 3.9 copy-start.29
  556.2 3.9 copy-start.32
  556.2 3.9 copy-start.38
  556.2 3.9 copy-start.42
  560.1 4.1 copy-start.9
  560.1 4.1 copy-start.22
  560.1 4.1 copy-start.23
  560.1 4.1 copy-start.24
  560.2 4.1 copy-start.35
  560.2 4.1 copy-start.50
  560.2 4.1 copy-start.58
  560.2 4.1 copy-start.60
  (46 other events, 84.0 us)
Sparse Core Ops, SparseCore 0:
  202.1 20.4 all-gather.4
  224.6 17.7 all-gather.6
  331.8 70.9 reduce-scatter.10
  406.4 128.0 reduce-scatter.8
  536.9 32.6 all-reduce.8
  574.0 68.9 reduce-scatter.14
  647.5 67.9 reduce-scatter.12
where the time goes:
time: 871 us; the launch traced here: 866 us
  other arithmetic  257 us (30%)
  local copies, waits for them, and re-layouts  223 us (26%)
  waiting for transfers between devices  214 us (25%)
  blocking collectives  98.6 us (11%)
  matrix products  53.2 us (6%)
  between operations  15.4 us (2%)
    scatter-add x1, other arithmetic, on_device(): jax.ops.segment_sum(rel_pairs.reshape(seq_rows * seq_rows, head_count), r...  208 us
    gather x4, local copies, waits for them, and re-layouts, on_device(): rel_bias = jnp.transpose(rel_table[rel_index], (2, 0, 1))  162 us
    reduce_scatter x1, waiting for transfers between devices, on_device(): lax.psum_scatter(qkv_grad, 'dp', scatter_dimension=0, tiled=True)  130 us
    reduce_scatter x1, waiting for transfers between devices, on_device(): lax.psum_scatter(proj_grad, 'dp', scatter_dimension=0, tiled=True)  55.4 us
    unnamed x2, blocking collectives  44 us
    psum x1, blocking collectives, on_device(): lax.psum((fc1_bias_grad, mask_token_grad, ln1_gain_grad, ln1_bias_grad, q...  41.1 us
    unnamed x148, local copies, waits for them, and re-layouts  30.7 us
    dot_general x4, matrix products, contract_cols(): lax.dot_general(left_side, right_side, (((1,), (1,)), ((), ())), preferre...  18.5 us
  transfers between devices with their start and end apart: 9, of which 4 were waited for; matrix products, arithmetic and copies ran while one was open for 37% of the time, Pallas kernels for 0%

commit v1 on v0

v1 whole, which is shorter than its diff:
```python
import functools

import jax
import jax.numpy as jnp
from jax import lax
from jax.experimental import pallas as pl
from jax.experimental.pallas import tpu as pltpu
from jax.sharding import PartitionSpec as P

F32 = jnp.float32
BF16 = jnp.bfloat16
EPS = 1e-06
LANES = 128
VMEM_LIMIT = 56 * 1024 * 1024


def round_up(value, step):
    return -(-value // step) * step


def dot_nn(left, right):
    return lax.dot_general(left, right, (((1,), (0,)), ((), ())), preferred_element_type=F32)


def dot_nt(left, right):
    return lax.dot_general(left, right, (((1,), (1,)), ((), ())), preferred_element_type=F32)


def dot_tn(left, right):
    return lax.dot_general(left, right, (((0,), (0,)), ((), ())), preferred_element_type=F32)


def row_of(ref):
    return ref[...].reshape(1, ref.shape[0])


def norm_stats(values):
    middle = jnp.mean(values, axis=-1, keepdims=True)
    centred = values - middle
    spread = jnp.mean(centred * centred, axis=-1, keepdims=True)
    root = lax.rsqrt(spread + EPS)
    return centred * root, root


def norm_back(d_out, xhat, root, gain):
    t = d_out * gain
    mean_t = jnp.mean(t, axis=-1, keepdims=True)
    mean_tx = jnp.mean(t * xhat, axis=-1, keepdims=True)
    return root * (t - mean_t - xhat * mean_tx)


def call(body, outs, scratch=(), flops=0, moved=0):
    return pl.pallas_call(
        body,
        out_shape=outs,
        scratch_shapes=list(scratch),
        compiler_params=pltpu.CompilerParams(vmem_limit_bytes=VMEM_LIMIT),
        cost_estimate=pl.CostEstimate(flops=flops, bytes_accessed=moved, transcendentals=0),
    )


def shape(dims, kind):
    return jax.ShapeDtypeStruct(dims, kind)


def load_padded(source_ref, pad_ref):
    rows = source_ref.shape[1]
    tail = (rows // 8) * 8
    pad_ref[tail:, :] = jnp.zeros_like(pad_ref[tail:, :])
    pad_ref[0:rows, :] = source_ref[0].astype(F32)
    return pad_ref[...]


def forward_body(
    heads,
    patches_ref,
    mask_ref,
    index_ref,
    token_ref,
    gain1_ref,
    bias1_ref,
    wqkv_ref,
    qbias_ref,
    vbias_ref,
    table_ref,
    wproj_ref,
    pbias_ref,
    gamma1_ref,
    gain2_ref,
    bias2_ref,
    normed_ref,
    q_ref,
    k_ref,
    v_ref,
    probs_ref,
    mixed_ref,
    attended_ref,
    hidden_ref,
    inner_ref,
    pad_s,
    index_s,
    table_s,
    tablet_s,
):
    rows = patches_ref.shape[1]
    width = patches_ref.shape[2]
    pad = normed_ref.shape[0]
    keys = k_ref.shape[0]
    head_size = width // heads
    picked = mask_ref[...] > 0
    start = jnp.where(picked, row_of(token_ref), load_padded(patches_ref, pad_s))
    xhat, _ = norm_stats(start)
    normed = (xhat * row_of(gain1_ref) + row_of(bias1_ref)).astype(BF16)
    normed_ref[...] = normed
    qkv = dot_nn(normed, wqkv_ref[...])
    scale = head_size ** (-0.5)
    q_ref[...] = ((qkv[:, :width] + row_of(qbias_ref)) * scale).astype(BF16)
    k_ref[0:pad, :] = qkv[:, width : 2 * width].astype(BF16)
    k_ref[pad:, :] = jnp.zeros_like(k_ref[pad:, :])
    v_ref[0:pad, :] = (qkv[:, 2 * width :] + row_of(vbias_ref)).astype(BF16)
    v_ref[pad:, :] = jnp.zeros_like(v_ref[pad:, :])

    index_s[...] = jnp.zeros_like(index_s)
    index_s[0:rows, 0:rows] = index_ref[...]
    table_s[...] = jnp.zeros_like(table_s)
    table_s[0 : table_ref.shape[0], 0:heads] = table_ref[...]
    chunks = table_s.shape[0] // LANES
    for chunk in range(chunks):
        part = slice(chunk * LANES, (chunk + 1) * LANES)
        flipped = table_s[part, :].T
        for head in range(heads):
            tablet_s[head, :, part] = flipped[head : head + 1, :]
    lane = lax.broadcasted_iota(jnp.int32, (1, LANES), 1)
    first = lane < head_size
    key_lane = lax.broadcasted_iota(jnp.int32, (1, keys), 1)

    def rel_bias(head):
        halves = []
        for half in range(keys // LANES):
            at = index_s[:, half * LANES : (half + 1) * LANES]
            low = lax.rem(at, LANES)
            high = lax.div(at, LANES)
            value = jnp.zeros((pad, LANES), F32)
            for chunk in range(chunks):
                line = tablet_s[head, :, chunk * LANES : (chunk + 1) * LANES]
                found = jnp.take_along_axis(
                    jnp.broadcast_to(line, (pad, LANES)), low, axis=1, mode="promise_in_bounds"
                )
                value = jnp.where(high == chunk, found, value)
            halves.append(value)
        return jnp.where(key_lane < rows, jnp.concatenate(halves, axis=1), -1e30)

    def pair_step(pair, carry):
        at = pl.ds(pl.multiple_of(pair * LANES, LANES), LANES)
        query = q_ref[:, at]
        key = k_ref[:, at]
        value = v_ref[:, at]
        outs = []
        for side in range(2):
            head = pair * 2 + side
            own = first if side == 0 else jnp.logical_not(first)
            scores = dot_nt(jnp.where(own, query, jnp.zeros_like(query)), key) + rel_bias(head)
            top = jnp.max(scores, axis=-1, keepdims=True)
            grown = jnp.exp(scores - top)
            probs = (grown / jnp.sum(grown, axis=-1, keepdims=True)).astype(BF16)
            probs_ref[head] = probs
            outs.append(dot_nn(probs, value))
        mixed_ref[:, at] = jnp.where(first, outs[0], outs[1]).astype(BF16)
        return carry

    lax.fori_loop(0, heads // 2, pair_step, 0)
    attended = dot_nn(mixed_ref[...], wproj_ref[...]) + row_of(pbias_ref)
    attended_ref[...] = attended
    hidden = start + row_of(gamma1_ref) * attended
    hidden_ref[...] = hidden
    xhat2, _ = norm_stats(hidden)
    inner_ref[...] = (xhat2 * row_of(gain2_ref) + row_of(bias2_ref)).astype(BF16)


def forward(heads, patches, mask_col, rel_index, token, gain1, bias1, wqkv, qbias, vbias, table,
            wproj, pbias, gamma1, gain2, bias2):
    rows, width = patches.shape[1:]
    pad = mask_col.shape[0]
    keys = round_up(pad, LANES)
    entries = round_up(table.shape[0], LANES)
    outs = (
        shape((pad, width), BF16),
        shape((pad, width), BF16),
        shape((keys, width), BF16),
        shape((keys, width), BF16),
        shape((heads, pad, keys), BF16),
        shape((pad, width), BF16),
        shape((pad, width), F32),
        shape((pad, width), F32),
        shape((pad, width), BF16),
    )
    return call(
        functools.partial(forward_body, heads),
        outs,
        (
            pltpu.VMEM((pad, width), F32),
            pltpu.VMEM((pad, keys), jnp.int32),
            pltpu.VMEM((entries, LANES), F32),
            pltpu.VMEM((heads, 1, entries), F32),
        ),
        flops=10**10,
        moved=2 * 10**7,
    )(patches, mask_col, rel_index, token, gain1, bias1, wqkv, qbias, vbias, table, wproj, pbias,
      gamma1, gain2, bias2)


def mlp_body(
    inner_ref, dbranch_ref, w1a_ref, w1b_ref, w2a_ref, w2b_ref, b1a_ref, b1b_ref,
    acta_ref, actb_ref, dprea_ref, dpreb_ref, branch_ref, dinner_ref, sums_ref,
):
    inner = inner_ref[...]
    dbranch = dbranch_ref[...]
    branch = None
    dinner = None
    for at, (w1, w2, b1, act_out, dpre_out) in enumerate((
        (w1a_ref, w2a_ref, b1a_ref, acta_ref, dprea_ref),
        (w1b_ref, w2b_ref, b1b_ref, actb_ref, dpreb_ref),
    )):
        pre = dot_nn(inner, w1[...]) + row_of(b1).astype(F32)
        phi = 0.5 + 0.5 * lax.erf(pre * (0.5**0.5))
        act = (pre * phi).astype(BF16)
        act_out[...] = act
        slope = phi + pre * (jnp.exp(-0.5 * pre * pre) * 0.3989422804014327)
        dact = dot_nt(dbranch, w2[...])
        dpre = (dact * slope).astype(BF16)
        dpre_out[...] = dpre
        sums_ref[at : at + 1, :] = jnp.sum(dpre.astype(F32), axis=0, keepdims=True)
        this_branch = dot_nn(act, w2[...])
        this_dinner = dot_nt(dpre, w1[...])
        branch = this_branch if branch is None else branch + this_branch
        dinner = this_dinner if dinner is None else dinner + this_dinner
    branch_ref[...] = branch.astype(branch_ref.dtype)
    dinner_ref[...] = dinner.astype(dinner_ref.dtype)


def mlp(inner, dbranch, w1a, w1b, w2a, w2b, b1a, b1b, kind):
    pad, width = inner.shape
    ff = w1a.shape[1]
    outs = (
        shape((pad, ff), BF16),
        shape((pad, ff), BF16),
        shape((pad, ff), BF16),
        shape((pad, ff), BF16),
        shape((pad, width), kind),
        shape((pad, width), kind),
        shape((8, ff), F32),
    )
    return call(mlp_body, outs, flops=10**10, moved=10**7)(
        inner, dbranch, w1a, w1b, w2a, w2b, b1a, b1b
    )


def mlp_grad_body(add, inner0, inner1, dpre0, dpre1, act0, act1, dbr0, dbr1, *rest):
    out_ref = rest[-1]
    for at, (left0, left1, right0, right1) in enumerate(
        ((inner0, inner1, dpre0, dpre1), (dbr0, dbr1, act0, act1))
    ):
        total = dot_tn(left0[...], right0[...]) + dot_tn(left1[...], right1[...])
        if add:
            total = total + rest[0][at].astype(F32)
        out_ref[at] = total.astype(BF16)


def mlp_grad(inner0, inner1, dpre0, dpre1, act0, act1, dbr0, dbr1, other=None):
    width = inner0.shape[1]
    ff = act0.shape[1]
    extra = () if other is None else (other,)
    return call(
        functools.partial(mlp_grad_body, other is not None),
        shape((2, width, ff), BF16),
        flops=10**10,
        moved=10**7,
    )(inner0, inner1, dpre0, dpre1, act0, act1, dbr0, dbr1, *extra)


def backward_body(
    heads,
    rows,
    where_ref,
    dinner0_ref,
    dinner1_ref,
    hidden_ref,
    attended_ref,
    outgrad_ref,
    mask_ref,
    gain2_ref,
    gamma1_ref,
    wproj_ref,
    q_ref,
    k_ref,
    v_ref,
    probs_ref,
    dhidden_ref,
    dattsend_ref,
    dattkeep_ref,
    dqkv_ref,
    dqkvsend_ref,
    dscores_ref,
    sums_ref,
    pad_s,
    dmixed_s,
):
    pad, width = hidden_ref.shape
    head_size = width // heads
    cotangent = load_padded(outgrad_ref, pad_s) * mask_ref[...]
    xhat, root = norm_stats(hidden_ref[...])
    dinner = dinner0_ref[...].astype(F32) + dinner1_ref[...].astype(F32)
    dhidden = cotangent + norm_back(dinner, xhat, root, row_of(gain2_ref))
    dhidden_ref[...] = dhidden
    datt = (row_of(gamma1_ref) * dhidden).astype(BF16)
    high = where_ref[0] > 0
    half = width // 2
    dattsend_ref[...] = jnp.where(high, datt[:, :half], datt[:, half:])
    dattkeep_ref[...] = jnp.where(high, datt[:, half:], datt[:, :half])
    dmixed_s[...] = dot_nt(datt, wproj_ref[...]).astype(BF16)
    sums_ref[0:1, :] = jnp.sum(dinner * xhat, axis=0, keepdims=True)
    sums_ref[1:2, :] = jnp.sum(dinner, axis=0, keepdims=True)
    sums_ref[2:3, :] = jnp.sum(dhidden * attended_ref[...], axis=0, keepdims=True)
    sums_ref[3:4, :] = jnp.sum(datt.astype(F32), axis=0, keepdims=True)

    lane = lax.broadcasted_iota(jnp.int32, (1, LANES), 1)
    first = lane < head_size
    scale = head_size ** (-0.5)

    def pair_step(pair, carry):
        start = pl.multiple_of(pair * LANES, LANES)
        at = pl.ds(start, LANES)
        query = q_ref[:, at]
        key = k_ref[:, at]
        value = v_ref[:, at]
        dmixed = dmixed_s[:, at]
        dq, dk, dv = [], [], []
        for side in range(2):
            head = pair * 2 + side
            own = first if side == 0 else jnp.logical_not(first)
            probs_b = probs_ref[head]
            probs = probs_b.astype(F32)
            dprobs = dot_nt(jnp.where(own, dmixed, jnp.zeros_like(dmixed)), value)
            inside = jnp.sum(probs * dprobs, axis=-1, keepdims=True)
            dscores = (probs * (dprobs - inside)).astype(BF16)
            dscores_ref[head] = dscores
            dq.append(dot_nn(dscores, key))
            dk.append(dot_tn(dscores, query))
            dv.append(dot_tn(probs_b, dmixed))
        dqkv_ref[:, at] = (jnp.where(first, dq[0], dq[1]) * scale).astype(BF16)
        dqkv_ref[:, pl.ds(pl.multiple_of(start + width, LANES), LANES)] = (
            jnp.where(first, dk[0], dk[1])[:pad].astype(BF16)
        )
        dqkv_ref[:, pl.ds(pl.multiple_of(start + 2 * width, LANES), LANES)] = (
            jnp.where(first, dv[0], dv[1])[:pad].astype(BF16)
        )
        return carry

    lax.fori_loop(0, heads // 2, pair_step, 0)
    three = 3 * width // 2
    dqkvsend_ref[...] = jnp.where(high, dqkv_ref[:, :three], dqkv_ref[:, three:])
    sums_ref[4:5, :] = jnp.sum(dqkv_ref[:, :width].astype(F32), axis=0, keepdims=True)
    sums_ref[5:6, :] = jnp.sum(dqkv_ref[:, 2 * width :].astype(F32), axis=0, keepdims=True)
    sums_ref[6:8, :] = jnp.zeros((2, width), F32)


def with_scalars(body, outs, scratch, n_in, flops=10**10, moved=10**7):
    return pl.pallas_call(
        body,
        out_shape=outs,
        in_specs=[pl.BlockSpec(memory_space=pltpu.SMEM)]
        + [pl.BlockSpec(memory_space=pltpu.VMEM)] * n_in,
        scratch_shapes=list(scratch),
        compiler_params=pltpu.CompilerParams(vmem_limit_bytes=VMEM_LIMIT),
        cost_estimate=pl.CostEstimate(flops=flops, bytes_accessed=moved, transcendentals=0),
    )


def backward(heads, where, dinner0, dinner1, hidden, attended, out_grad, mask_col, gain2, gamma1,
             wproj, q, k, v, probs):
    pad, width = hidden.shape
    keys = k.shape[0]
    half, three = width // 2, 3 * width // 2
    outs = (
        shape((pad, width), F32),
        shape((pad, half), BF16),
        shape((pad, half), BF16),
        shape((pad, 3 * width), BF16),
        shape((pad, three), BF16),
        shape((heads, pad, keys), BF16),
        shape((8, width), F32),
    )
    scratch = (pltpu.VMEM((pad, width), F32), pltpu.VMEM((pad, width), BF16))
    return with_scalars(
        functools.partial(backward_body, heads, out_grad.shape[1]), outs, scratch, 13
    )(where, dinner0, dinner1, hidden, attended, out_grad, mask_col, gain2, gamma1, wproj, q, k, v,
      probs)


def first_norm_body(
    patches_ref, mask_ref, token_ref, gain1_ref, dqkv_ref, wqkv_ref, dhidden_ref,
    patchgrad_ref, sums_ref, pad_s,
):
    rows, width = patches_ref.shape[1:]
    mask = mask_ref[...]
    picked = mask > 0
    start = jnp.where(picked, row_of(token_ref), load_padded(patches_ref, pad_s))
    xhat, root = norm_stats(start)
    dnormed = dot_nt(dqkv_ref[...], wqkv_ref[...])
    dstart = dhidden_ref[...] + norm_back(dnormed, xhat, root, row_of(gain1_ref))
    patchgrad_ref[0] = jnp.where(picked, 0.0, dstart)[0:rows]
    sums_ref[0:1, :] = jnp.sum(jnp.where(picked, dstart, 0.0), axis=0, keepdims=True)
    sums_ref[1:2, :] = jnp.sum(dnormed * xhat, axis=0, keepdims=True)
    sums_ref[2:3, :] = jnp.sum(dnormed, axis=0, keepdims=True)
    sums_ref[3:8, :] = jnp.zeros((5, width), F32)


def first_norm(patches, mask_col, token, gain1, dqkv, wqkv, dhidden):
    rows, width = patches.shape[1:]
    pad = mask_col.shape[0]
    outs = (shape((1, rows, width), F32), shape((8, width), F32))
    return call(
        first_norm_body, outs, (pltpu.VMEM((pad, width), F32),), flops=10**9, moved=10**7
    )(patches, mask_col, token, gain1, dqkv, wqkv, dhidden)


def layer_end_body(
    hidden_ref, branch0_ref, branch1_ref, bias_ref, gamma2_ref, outgrad_ref, mask_ref, dbranch_ref,
    out_ref, sums_ref, pad_s,
):
    rows, width = outgrad_ref.shape[1:]
    branch = branch0_ref[...].astype(F32) + branch1_ref[...].astype(F32) + row_of(bias_ref)
    layer = hidden_ref[...] + row_of(gamma2_ref) * branch
    out_ref[0] = layer[0:rows].astype(BF16)
    cotangent = load_padded(outgrad_ref, pad_s) * mask_ref[...]
    sums_ref[0:1, :] = jnp.sum(dbranch_ref[...].astype(F32), axis=0, keepdims=True)
    sums_ref[1:2, :] = jnp.sum(cotangent * branch, axis=0, keepdims=True)
    sums_ref[2:8, :] = jnp.zeros((6, width), F32)


def layer_end(hidden, branch0, branch1, bias, gamma2, out_grad, mask_col, dbranch):
    rows, width = out_grad.shape[1:]
    pad = hidden.shape[0]
    outs = (shape((1, rows, width), BF16), shape((8, width), F32))
    return call(
        layer_end_body, outs, (pltpu.VMEM((pad, width), F32),), flops=10**8, moved=10**7
    )(hidden, branch0, branch1, bias, gamma2, out_grad, mask_col, dbranch)


def table_grad_body(index_ref, ds_ref, out_ref, index_s):
    rows = index_ref.shape[0]
    high_count, head_pad, _ = out_ref.shape
    pad, keys = index_s.shape
    index_s[...] = jnp.zeros_like(index_s)
    index_s[0:rows, 0:rows] = index_ref[...]
    out_ref[...] = jnp.zeros_like(out_ref)
    below = lax.broadcasted_iota(jnp.int32, (LANES, keys), 0)

    def step(group, carry):
        base = pl.multiple_of(group * 8, 8)
        lines = index_s[pl.ds(base, 8), :]
        low = lax.rem(lines, LANES)
        high = lax.div(lines, LANES)
        total = jnp.zeros((high_count * head_pad, LANES), F32)
        for i in range(8):
            onehot = jnp.where(below == low[i : i + 1], 1.0, 0.0).astype(BF16)
            ds = ds_ref[base + i].astype(F32)
            left = jnp.concatenate(
                [jnp.where(high[i : i + 1] == at, ds, 0.0).astype(BF16) for at in range(high_count)],
                axis=0,
            )
            total = total + dot_nt(left, onehot)
        out_ref[...] += total.reshape(high_count, head_pad, LANES)
        return carry

    lax.fori_loop(0, pad // 8, step, 0)


def table_grad(rel_index, dscores, entries):
    pad, head_pad, keys = dscores.shape
    high_count = round_up(entries, LANES) // LANES
    return call(
        table_grad_body,
        shape((high_count, head_pad, LANES), F32),
        (pltpu.VMEM((pad, keys), jnp.int32),),
        flops=10**10,
        moved=10**7,
    )(rel_index, dscores)


def late_grad_body(
    add, where_ref, normed0, normed1, mixed0, mixed1, dqkv_ref, dqkv1_ref, datt0, datt1, *rest
):
    out_ref = rest[-1]
    width = normed0.shape[1]
    half, three = width // 2, 3 * width // 2
    high = where_ref[0] > 0
    core = where_ref[1] > 0
    second = core if add else jnp.logical_not(core)
    own = jnp.where(high, dqkv_ref[:, three:], dqkv_ref[:, :three])
    total0, total1 = None, None
    for normed_ref, mixed_ref, part, datt_ref in (
        (normed0, mixed0, own, datt0),
        (normed1, mixed1, dqkv1_ref[...], datt1),
    ):
        normed = normed_ref[...]
        right0 = jnp.where(second, part[:, width:], part[:, :half])
        left1 = jnp.where(second, mixed_ref[...], normed)
        right1 = jnp.where(second, datt_ref[...], part[:, half:width])
        this0 = dot_tn(normed, right0)
        this1 = dot_tn(left1, right1)
        total0 = this0 if total0 is None else total0 + this0
        total1 = this1 if total1 is None else total1 + this1
    if add:
        total0 = total0 + rest[0][:, :half].astype(F32)
        total1 = total1 + rest[0][:, half:].astype(F32)
    out_ref[:, :half] = total0.astype(BF16)
    out_ref[:, half:] = total1.astype(BF16)


def late_grad(where, normed0, normed1, mixed0, mixed1, dqkv, dqkv1, datt0, datt1, other=None):
    width = normed0.shape[1]
    extra = () if other is None else (other,)
    return with_scalars(
        functools.partial(late_grad_body, other is not None),
        shape((width, width), BF16),
        (),
        8 + len(extra),
    )(where, normed0, normed1, mixed0, mixed1, dqkv, dqkv1, datt0, datt1, *extra)


def on_device(
    dp,
    patches,
    row_mask,
    out_grad,
    rel_index,
    mask_token,
    ln1_gain,
    ln1_bias,
    qkv_weight,
    query_bias,
    value_bias,
    rel_table,
    proj_weight,
    proj_bias,
    gamma1,
    ln2_gain,
    ln2_bias,
    fc1_weight,
    fc1_bias,
    fc2_weight,
    fc2_bias,
    gamma2,
):
    rows, width = patches.shape[1:]
    entries, heads = rel_table.shape
    pad = round_up(rows, 16)
    mp_at = lax.axis_index("mp")
    dp_at = lax.axis_index("dp")
    x_at, core_at, low_at = mp_at // 2, mp_at % 2, dp_at % 2
    where = jnp.stack([x_at, core_at]).astype(jnp.int32)

    def swap(axis, bit):
        count = 4 if axis == "mp" else dp
        pairs = [(at, at ^ bit) for at in range(count)]
        return lambda value: lax.ppermute(value, axis, pairs)

    over_core, over_x = swap("mp", 1), swap("mp", 2)

    mask_col = jnp.pad(
        (row_mask > 0).astype(F32).reshape(rows, 1), ((0, pad - rows), (0, 0))
    )
    dbranch = jnp.pad(
        (gamma2 * (out_grad[0].astype(F32) * mask_col[:rows])).astype(BF16),
        ((0, pad - rows), (0, 0)),
    )
    dbranch1 = over_x(dbranch)
    w1b, w2b, b1b = over_core(fc1_weight), over_core(fc2_weight), over_core(fc1_bias)

    normed, q, k, v, probs, mixed, attended, hidden, inner = forward(
        heads, patches, mask_col, rel_index, mask_token, ln1_gain, ln1_bias, qkv_weight,
        query_bias, value_bias, rel_table, proj_weight, proj_bias, gamma1, ln2_gain, ln2_bias,
    )
    inner1 = over_x(inner)
    weights = (fc1_weight, w1b, fc2_weight, w2b, fc1_bias, b1b)
    acta0, actb0, dprea0, dpreb0, branch0, dinner0, sums0 = mlp(inner, dbranch, *weights, F32)
    acta1, actb1, dprea1, dpreb1, branch1, dinner1, sums1 = mlp(inner1, dbranch1, *weights, BF16)
    dinner_in = over_x(dinner1)
    mixed1 = over_x(mixed)
    normed1 = over_x(normed)
    branch_in = over_x(branch1)

    other = over_core(
        mlp_grad(inner, inner1, dpreb0, dpreb1, actb0, actb1, dbranch, dbranch1)
    )
    fc_grad = mlp_grad(inner, inner1, dprea0, dprea1, acta0, acta1, dbranch, dbranch1, other)

    dhidden, datt_send, datt_keep, dqkv, dqkv_send, dscores, sums_b = backward(
        heads, where, dinner0, dinner_in, hidden, attended, out_grad, mask_col, ln2_gain, gamma1,
        proj_weight, q, k, v, probs,
    )
    datt1 = over_x(datt_send)
    dqkv1 = over_x(dqkv_send)

    patch_grad, sums_n = first_norm(
        patches, mask_col, mask_token, ln1_gain, dqkv, qkv_weight, dhidden
    )
    layer_out, sums_e = layer_end(
        hidden, branch0, branch_in, fc2_bias, gamma2, out_grad, mask_col, dbranch
    )

    late_args = (where, normed, normed1, mixed, mixed1, dqkv, dqkv1, datt_keep, datt1)
    late_other = over_core(late_grad(*late_args))
    late = late_grad(*late_args, late_other)

    block = width // dp
    halves = dp // 2
    over_low = swap("dp", 1)

    def scatter_low(value):
        parts = value.reshape(-1, halves, 2, block, value.shape[-1])
        send = lax.dynamic_index_in_dim(parts, 1 - low_at, 2, False)
        keep = lax.dynamic_index_in_dim(parts, low_at, 2, False)
        return (keep.astype(F32) + over_low(send).astype(F32)).astype(BF16)

    high_at = dp_at // 2

    def scatter_high(value):
        total = lax.dynamic_index_in_dim(value, high_at, 1, False).astype(F32)
        for step in range(1, halves):
            part = lax.dynamic_index_in_dim(value, high_at ^ step, 1, False)
            total = total + swap("dp", 2 * step)(part).astype(F32)
        return total

    fc_own = scatter_high(scatter_low(fc_grad))
    late_own = scatter_high(scatter_low(late))[0].astype(BF16)

    fc1_weight_grad = fc_own[0]
    fc2_weight_grad = fc_own[1].T

    late_x = over_x(late_own)
    pair_core = over_core(jnp.stack([late_own, late_x]))
    on_core = core_at > 0
    on_x = x_at > 0
    mine = jnp.stack([late_own, late_x])
    core0 = jnp.where(on_core, pair_core, mine)
    core1 = jnp.where(on_core, mine, pair_core)
    low0 = jnp.where(on_x, core0[1], core0[0])
    high0 = jnp.where(on_x, core0[0], core0[1])
    low1 = jnp.where(on_x, core1[1], core1[0])
    high1 = jnp.where(on_x, core1[0], core1[1])
    half = width // 2
    qkv_weight_grad = jnp.concatenate(
        [low0, low1[:, :half], high0, high1[:, :half]], axis=1
    ).astype(F32)
    proj_weight_grad = jnp.concatenate([low1[:, half:], high1[:, half:]], axis=1).astype(F32)

    head_pad = 16
    ds = jnp.pad(jnp.transpose(dscores, (1, 0, 2)), ((0, 0), (0, head_pad - heads), (0, 0)))
    table = table_grad(rel_index, ds, entries)

    table_rows = table.reshape(-1, width)
    shared = jnp.concatenate([table_rows, sums_b[:6], sums_n[:3], sums_e[:2]], axis=0)
    shared_rows = shared.shape[0]
    sums = sums0 + sums1
    met = over_core(jnp.concatenate([shared, sums[1:2]], axis=0))
    shared = shared + met[:shared_rows]
    bias_row = sums[0:1] + met[shared_rows:]
    shared = shared + over_x(shared)
    both = jnp.concatenate([shared, bias_row], axis=0)
    bit = 1
    while bit < dp:
        both = both + swap("dp", bit)(both)
        bit *= 2
    n = table_rows.shape[0]
    rel_grad = both[:n].reshape(-1, head_pad, LANES)
    rel_grad = jnp.transpose(rel_grad, (0, 2, 1)).reshape(-1, head_pad)[:entries, :heads]
    (ln2_gain_grad, ln2_bias_grad, gamma1_grad, proj_bias_grad, query_bias_grad, value_bias_grad,
     mask_token_grad, ln1_gain_grad, ln1_bias_grad, fc2_bias_grad, gamma2_grad,
     fc1_bias_grad) = [both[n + at] for at in range(12)]
    return (
        layer_out,
        patch_grad,
        mask_token_grad,
        ln1_gain_grad,
        ln1_bias_grad,
        qkv_weight_grad,
        query_bias_grad,
        value_bias_grad,
        rel_grad,
        proj_weight_grad,
        proj_bias_grad,
        gamma1_grad,
        ln2_gain_grad,
        ln2_bias_grad,
        fc1_weight_grad,
        fc1_bias_grad,
        fc2_weight_grad,
        fc2_bias_grad,
        gamma2_grad,
    )


def solution(mesh):
    rows3 = P(("dp", "mp"), None, None)
    placed = (
        (rows3, P(("dp", "mp"), None), rows3)
        + (P(),) * 13
        + (P(None, "mp"), P("mp"), P("mp", None), P(), P())
    )
    return jax.shard_map(
        functools.partial(on_device, mesh.shape["dp"]),
        mesh=mesh,
        in_specs=placed,
        out_specs=(
            rows3,
            rows3,
            P(),
            P(),
            P(),
            P("dp", None),
            P(),
            P(),
            P(),
            P("dp", None),
            P(),
            P(),
            P(),
            P(),
            P("dp", "mp"),
            P("mp"),
            P("mp", "dp"),
            P(),
            P(),
        ),
        check_vma=False,
    )
```

time: 871 us -> 247 us (0.28)
  other arithmetic: 257 us -> 4.05 us
  local copies, waits for them, and re-layouts: 223 us -> 19.2 us
  waiting for transfers between devices: 214 us -> 115 us
  blocking collectives: 98.6 us -> 0 us
  Pallas kernels: 0 us -> 78.7 us
  matrix products: 53.2 us -> 0 us
  starting transfers between devices: 4.48 us -> 28.7 us
  between operations: 15.4 us -> 1.03 us
    scatter-add x1 -> x0, other arithmetic: 208 us -> none  [on_device(): jax.ops.segment_sum(rel_pairs.reshape(seq_rows * seq_rows, head_count), r...]
    reduce_scatter x4 -> x0, waiting for transfers between devices: 185 us -> none  [the longest x1 130 us: on_device(): lax.psum_scatter(qkv_grad, 'dp', scatter_dimension=0, tiled=True)]
    gather x4 -> x0, local copies, waits for them, and re-layouts: 162 us -> none  [on_device(): rel_bias = jnp.transpose(rel_table[rel_index], (2, 0, 1))]
    ppermute x0 -> x28, waiting for transfers between devices: none -> 115 us  [swap(): return lambda value: lax.ppermute(value, axis, pairs)]
    pallas_call x0 -> x11, Pallas kernels: none -> 78.7 us  [the longest x1 19.8 us: forward(): call(functools.partial(forward_body, heads), outs, (pltpu.VMEM((pad, widt...]
    psum x2 -> x0, blocking collectives: 54.6 us -> none  [the longest x1 41.1 us: on_device(): lax.psum((fc1_bias_grad, mask_token_grad, ln1_gain_grad, ln1_bias_grad, q...]
    dot_general x18 -> x0, matrix products: 53.2 us -> none  [the longest x4 18.5 us: contract_cols(): lax.dot_general(left_side, right_side, (((1,), (1,)), ((), ())), preferre...]
    unnamed x2 -> x0, blocking collectives: 44 us -> none
  transfers between devices with their start and end apart: 9 -> 28, of which waited for: 4 -> 15; matrix products, arithmetic and copies ran while one was open for 37% -> 7% of each run, Pallas kernels for 0% -> 25%
where the time goes in v1:
time: 247 us
  waiting for transfers between devices  115 us (47%)
  Pallas kernels  78.7 us (32%)
  starting transfers between devices  28.7 us (12%)
  local copies, waits for them, and re-layouts  19.2 us (8%)
  other arithmetic  4.05 us (2%)
    ppermute x28, waiting for transfers between devices, swap(): return lambda value: lax.ppermute(value, axis, pairs)  115 us
    ppermute x28, starting transfers between devices, swap(): return lambda value: lax.ppermute(value, axis, pairs)  28.7 us
    pallas_call x1, Pallas kernels, forward(): call(functools.partial(forward_body, heads), outs, (pltpu.VMEM((pad, widt...  19.8 us
    pallas_call x2, Pallas kernels, mlp(): call(mlp_body, outs, flops=10 ** 10, moved=10 ** 7)  11.6 us
    pallas_call x1, Pallas kernels, backward(): with_scalars(functools.partial(backward_body, heads, out_grad.shape[1]),...  11.1 us
    pallas_call x1, Pallas kernels, table_grad(): call(table_grad_body, shape((high_count, head_pad, LANES), F32), (pltpu.V...  10.5 us
    pallas_call x2, Pallas kernels, mlp_grad(): call(functools.partial(mlp_grad_body, other is not None), shape((2, width...  9.96 us
    unnamed x53, local copies, waits for them, and re-layouts  9.26 us
  transfers between devices with their start and end apart: 28, of which 15 were waited for; matrix products, arithmetic and copies ran while one was open for 7% of the time, Pallas kernels for 25%

profile of v1, /device:TPU:0, one launch (start us, length us, event | category | flops | bytes accessed | tf_op | source)
XLA Modules:
  0.0 246.6 jit_solution(2366378852447053089)
XLA Ops:
  2.1 1.7 copy.48.table_ref
  4.4 19.8 %shard_map.348 = (bf16[208,768]{1,0:T(8,128)(2,1)}, bf16[208,768]{1,0:T(8,128)(2,1)}, bf16[256,768]{1,0:T(8,128)(2,1)}, bf16[256,768]{1,0:T(8,128)(2,1)}, bf16[1...) custom-call(bf16[1,197,768]{2,1,0:T(8,128)(2,1)} %patches_ref.3, ...), custom_call_target="tpu_custom_call" | custom-call | flops 10000000000 | bytes 20000000 | tf_op jit(solution)/shard_map/pallas_call | solution.py:197
  24.3 3.0 %collective-permute-start.3 = (bf16[208,768]{1,0:T(8,128)(2,1)}, bf16[208,768]{1,0:T(8,128)(2,1)S(1)}, u32[]{:S(2)}, u32[]{:S(2)}) collective-permute-start(bf16[208,768]{1,0:T(8,128)(2,1)} %get-tuple-element.54.inner_ref.inner0), channel_id=1, source_target_pairs={{0,2},{1,3},{2,0},{3,1},{4,6},{5,7},{6,4},{7,5},{8,10},{9,11},{10,... | collective-permute-start | bytes 958472 | tf_op jit(solution)/shard_map/ppermute | solution.py:567
  28.8 7.0 %collective-permute-done.3.inner_ref.inner1 = bf16[208,768]{1,0:T(8,128)(2,1)S(1)} collective-permute-done((bf16[208,768]{1,0:T(8,128)(2,1)}, bf16[208,768]{1,0:T(8,128)(2,1)S(1)}, u32[]{:S(2)}, u32[]{:S(2)}) %collective-permute-start.3) | collective-permute-done | bytes 319520 | tf_op jit(solution)/shard_map/ppermute | solution.py:567
  35.8 6.3 %collective-permute-done.4.dbranch_ref.dbr1 = bf16[208,768]{1,0:T(8,128)(2,1)S(1)} collective-permute-done((bf16[208,768]{1,0:T(8,128)(2,1)S(1)}, bf16[208,768]{1,0:T(8,128)(2,1)S(1)}, u32[]{:S(2)}, u32[]{:S(2)}) %collective-permute-start.4) | collective-permute-done | bytes 319520 | tf_op jit(solution)/shard_map/ppermute | solution.py:567
  44.2 5.8 %shard_map.350 = (bf16[208,768]{1,0:T(8,128)(2,1)}, bf16[208,768]{1,0:T(8,128)(2,1)}, bf16[208,768]{1,0:T(8,128)(2,1)}, bf16[208,768]{1,0:T(8,128)(2,1)}, bf16[2...) custom-call(bf16[208,768]{1,0:T(8,128)(2,1)} %copy-done.14, bf16[208,768]{1,0:T(8,128)(2,1)} %copy-done.15, ...), custom_call_target="tpu_custom_call" | custom-call | flops 10000000000 | bytes 10000000 | tf_op jit(solution)/shard_map/pallas_call | solution.py:253
  50.0 1.7 collective-permute-start.6
  51.7 5.9 %shard_map.349 = (bf16[208,768]{1,0:T(8,128)(2,1)}, bf16[208,768]{1,0:T(8,128)(2,1)}, bf16[208,768]{1,0:T(8,128)(2,1)}, bf16[208,768]{1,0:T(8,128)(2,1)}, f32[20...) custom-call(bf16[208,768]{1,0:T(8,128)(2,1)} %get-tuple-element.54.inner_ref.inner0, ...), custom_call_target="tpu_custom_call" | custom-call | flops 10000000000 | bytes 10000000 | tf_op jit(solution)/shard_map/pallas_call | solution.py:253
  57.6 1.6 collective-permute-done.6.dinner1_ref
  59.9 11.1 %shard_map.352 = (f32[208,768]{1,0:T(8,128)}, bf16[208,384]{1,0:T(8,128)(2,1)}, bf16[208,384]{1,0:T(8,128)(2,1)}, bf16[208,2304]{1,0:T(8,128)(2,1)}, bf16[208,11...) custom-call(s32[2]{0:T(128)} %pad_add_fusion.where_ref, ...), custom_call_target="tpu_custom_call" | custom-call | flops 10000000000 | bytes 10000000 | tf_op jit(solution)/shard_map/pallas_call | solution.py:394
  76.5 15.5 %collective-permute-done.12.normed1 = bf16[208,768]{1,0:T(8,128)(2,1)S(1)} collective-permute-done((bf16[208,768]{1,0:T(8,128)(2,1)S(1)}, bf16[208,768]{1,0:T(8,128)(2,1)S(1)}, u32[]{:S(2)}, u32[]{:S(2)}) %collective-permute-start.12) | collective-permute-done | bytes 319520 | tf_op jit(solution)/shard_map/ppermute | solution.py:567
  92.0 6.8 %collective-permute-done.13.mixed1 = bf16[208,768]{1,0:T(8,128)(2,1)S(1)} collective-permute-done((bf16[208,768]{1,0:T(8,128)(2,1)S(1)}, bf16[208,768]{1,0:T(8,128)(2,1)S(1)}, u32[]{:S(2)}, u32[]{:S(2)}) %collective-permute-start.13) | collective-permute-done | bytes 319520 | tf_op jit(solution)/shard_map/ppermute | solution.py:567
  98.8 3.4 %collective-permute-done.15.datt1 = bf16[208,384]{1,0:T(8,128)(2,1)S(1)} collective-permute-done((bf16[208,384]{1,0:T(8,128)(2,1)}, bf16[208,384]{1,0:T(8,128)(2,1)S(1)}, u32[]{:S(2)}, u32[]{:S(2)}) %collective-permute-start.15) | collective-permute-done | bytes 159776 | tf_op jit(solution)/shard_map/ppermute | solution.py:567
  103.0 3.9 %shard_map.355 = bf16[768,768]{1,0:T(8,128)(2,1)} custom-call(s32[2]{0:T(128)} %pad_add_fusion.where_ref, bf16[208,768]{1,0:T(8,128)(2,1)} %get-tuple-element.74.normed0, bf16[208,768]{1,0:T(8,128)(2,1)} %copy-done.19, bf16[208,768]{1,0:T(8,128)(2,1)} %get-tuple-element.75.mixed0, bf16[208,768]{1,0:T(8,128)(2,1)} %copy-done.20, ...), custom_call_target="tpu_custom_call" | custom-call | flops 10000000000 | bytes 10000000 | tf_op jit(solution)/shard_map/pallas_call | solution.py:524
  106.9 4.6 %shard_map.357 = bf16[2,768,768]{2,1,0:T(8,128)(2,1)} custom-call(bf16[208,768]{1,0:T(8,128)(2,1)} %get-tuple-element.54.inner_ref.inner0, bf16[208,768]{1,0:T(8,128)(2,1)} %copy-done.14, bf16[208,768]{1,0:T(8,128)(2,1)} %get-tuple-element.83.dpre0, bf16[208,768]{1,0:T(8,128)(2,1)} %get-tuple-element.84.dpre1, bf16[208,768]{1,0:T(8,128)(2,1)} %get-tuple-element.85.act0, ...), custom_call_target="tpu_custom_call" | custom-call | flops 10000000000 | bytes 10000000 | tf_op jit(solution)/shard_map/pallas_call | solution.py:273
  114.1 10.5 %shard_map.354 = f32[6,16,128]{2,1,0:T(8,128)} custom-call(s32[197,197]{1,0:T(8,128)} %index_ref.3, bf16[208,16,256]{2,1,0:T(8,128)(2,1)} %pad.14.ds_ref), custom_call_target="tpu_custom_call" | custom-call | flops 10000000000 | bytes 10000000 | tf_op jit(solution)/shard_map/pallas_call | solution.py:482
  125.4 5.0 %shard_map.353 = (f32[1,197,768]{2,1,0:T(8,128)}, f32[8,768]{1,0:T(8,128)}) custom-call(bf16[1,197,768]{2,1,0:T(8,128)(2,1)} %patches_ref.3, f32[208,1]{1,0:T(8,128)} %pad.12.mask_ref, f32[768]{0:T(1024)} %token_ref.3, f32[768]{0:T(1024)} %gain1_ref.3, bf16[208,2304]{1,0:T(8,128)(2,1)} %get-tuple-element.65.dqkv_ref, bf16[768,2304]{1,0:T(8,128)(2,1)} %wqkv_ref.3, ...), custom_call_target="tpu_custom_call" | custom-call | flops 1000000000 | bytes 10000000 | tf_op jit(solution)/shard_map/pallas_call | solution.py:422
  131.9 2.5 %shard_map.351 = (bf16[1,197,768]{2,1,0:T(8,128)(2,1)}, f32[8,768]{1,0:T(8,128)}) custom-call(f32[208,768]{1,0:T(8,128)} %get-tuple-element.53.hidden_ref, f32[208,768]{1,0:T(8,128)} %get-tuple-element.55.branch0_ref, bf16[208,768]{1,0:T(8,128)(2,1)} %copy-done.5, f32[768]{0:T(1024)} %bias_ref.1, f32[768]{0:T(1024)} %gamma2_ref.1, ...), custom_call_target="tpu_custom_call" | custom-call | flops 100000000 | bytes 10000000 | tf_op jit(solution)/shard_map/pallas_call | solution.py:445
  136.4 4.3 %shard_map.356 = bf16[768,768]{1,0:T(8,128)(2,1)} custom-call(s32[2]{0:T(128)} %pad_add_fusion.where_ref, bf16[208,768]{1,0:T(8,128)(2,1)} %get-tuple-element.74.normed0, bf16[208,768]{1,0:T(8,128)(2,1)} %copy-done.19, bf16[208,768]{1,0:T(8,128)(2,1)} %get-tuple-element.75.mixed0, bf16[208,768]{1,0:T(8,128)(2,1)} %copy-done.20, ...), custom_call_target="tpu_custom_call" | custom-call | flops 10000000000 | bytes 10000000 | tf_op jit(solution)/shard_map/pallas_call | solution.py:524
  145.0 3.4 %collective-permute-done.8 = f32[27,768]{1,0:T(8,128)S(1)} collective-permute-done((f32[27,768]{1,0:T(8,128)S(1)}, f32[27,768]{1,0:T(8,128)S(1)}, u32[]{:S(2)}, u32[]{:S(2)}) %collective-permute-start.8) | collective-permute-done | bytes 82976 | tf_op jit(solution)/shard_map/ppermute | solution.py:567
  149.1 9.0 %collective-permute-done.17 = bf16[1,4,96,768]{3,2,1,0:T(8,128)(2,1)S(1)} collective-permute-done((bf16[1,4,96,768]{3,2,1,0:T(8,128)(2,1)S(1)}, bf16[1,4,96,768]{3,2,1,0:T(8,128)(2,1)S(1)}, u32[]{:S(2)}, u32[]{:S(2)}) %collective-permute-start.17) | collective-permute-done | bytes 589856 | tf_op jit(solution)/shard_map/ppermute | solution.py:567
  158.3 3.6 %collective-permute-start.20 = (bf16[1,96,768]{2,1,0:T(8,128)(2,1)S(1)}, bf16[1,96,768]{2,1,0:T(8,128)(2,1)S(1)}, u32[]{:S(2)}, u32[]{:S(2)}) collective-permute-start(bf16[1,96,768]{2,1,0:T(8,128)(2,1)S(1)} %get-tuple-element.147), channel_id=1, source_target_pairs={{0,24},{4,28},{8,16},{12,20},{16,8},{20,12},{24,0},{28,4},{1,25},{... | collective-permute-start | bytes 442376 | tf_op jit(solution)/shard_map/ppermute | solution.py:567
  164.0 2.9 %collective-permute-done.20 = bf16[1,96,768]{2,1,0:T(8,128)(2,1)S(1)} collective-permute-done((bf16[1,96,768]{2,1,0:T(8,128)(2,1)S(1)}, bf16[1,96,768]{2,1,0:T(8,128)(2,1)S(1)}, u32[]{:S(2)}, u32[]{:S(2)}) %collective-permute-start.20) | collective-permute-done | bytes 147488 | tf_op jit(solution)/shard_map/ppermute | solution.py:567
  167.0 6.9 %collective-permute-done.19 = bf16[1,96,768]{2,1,0:T(8,128)(2,1)S(1)} collective-permute-done((bf16[1,96,768]{2,1,0:T(8,128)(2,1)S(1)}, bf16[1,96,768]{2,1,0:T(8,128)(2,1)S(1)}, u32[]{:S(2)}, u32[]{:S(2)}) %collective-permute-start.19) | collective-permute-done | bytes 147488 | tf_op jit(solution)/shard_map/ppermute | solution.py:567
  173.9 1.6 collective-permute-start.21
  177.1 5.0 %collective-permute-done.11 = f32[28,768]{1,0:T(8,128)S(1)} collective-permute-done((f32[28,768]{1,0:T(8,128)S(1)}, f32[28,768]{1,0:T(8,128)S(1)}, u32[]{:S(2)}, u32[]{:S(2)}) %collective-permute-start.11) | collective-permute-done | bytes 86048 | tf_op jit(solution)/shard_map/ppermute | solution.py:567
  182.9 5.3 %shard_map.358 = bf16[2,768,768]{2,1,0:T(8,128)(2,1)} custom-call(bf16[208,768]{1,0:T(8,128)(2,1)} %get-tuple-element.54.inner_ref.inner0, bf16[208,768]{1,0:T(8,128)(2,1)} %copy-done.14, bf16[208,768]{1,0:T(8,128)(2,1)} %get-tuple-element.79.dpre0, bf16[208,768]{1,0:T(8,128)(2,1)} %get-tuple-element.80.dpre1, bf16[208,768]{1,0:T(8,128)(2,1)} %get-tuple-element.81.act0, ...), custom_call_target="tpu_custom_call" | custom-call | flops 10000000000 | bytes 10000000 | tf_op jit(solution)/shard_map/pallas_call | solution.py:273
  188.3 1.8 constant_dynamic-slice_fusion.1
  193.3 25.3 %collective-permute-done.24 = bf16[2,4,96,768]{3,2,0,1:T(8,128)(2,1)S(1)} collective-permute-done((bf16[2,4,96,768]{3,2,0,1:T(8,128)(2,1)S(1)}, bf16[2,4,96,768]{3,2,0,1:T(8,128)(2,1)S(1)}, u32[]{:S(2)}, u32[]{:S(2)}) %collective-permute-start.24) | collective-permute-done | bytes 1179680 | tf_op jit(solution)/shard_map/ppermute | solution.py:567
  220.5 2.9 %collective-permute-start.25 = (bf16[2,96,768]{2,1,0:T(8,128)(2,1)S(1)}, bf16[2,96,768]{2,1,0:T(8,128)(2,1)S(1)}, u32[]{:S(2)}, u32[]{:S(2)}) collective-permute-start(bf16[2,96,768]{2,1,0:T(8,128)(2,1)S(1)} %get-tuple-element.139), channel_id=1, source_target_pairs={{0,8},{4,12},{8,0},{12,4},{16,24},{20,28},{24,16},{28,20},{1,9},{5... | collective-permute-start | bytes 884744 | tf_op jit(solution)/shard_map/ppermute | solution.py:567
  224.4 6.5 %collective-permute-done.27 = bf16[2,96,768]{2,1,0:T(8,128)(2,1)S(1)} collective-permute-done((bf16[2,96,768]{2,1,0:T(8,128)(2,1)S(1)}, bf16[2,96,768]{2,1,0:T(8,128)(2,1)S(1)}, u32[]{:S(2)}, u32[]{:S(2)}) %collective-permute-start.27) | collective-permute-done | bytes 294944 | tf_op jit(solution)/shard_map/ppermute | solution.py:567
  230.8 14.8 %collective-permute-done.26 = bf16[2,96,768]{2,1,0:T(8,128)(2,1)S(1)} collective-permute-done((bf16[2,96,768]{2,1,0:T(8,128)(2,1)S(1)}, bf16[2,96,768]{2,1,0:T(8,128)(2,1)S(1)}, u32[]{:S(2)}, u32[]{:S(2)}) %collective-permute-start.26) | collective-permute-done | bytes 294944 | tf_op jit(solution)/shard_map/ppermute | solution.py:567
  (130 shorter events, 36.3 us)
Async XLA Ops:
  0.7 41.4 %collective-permute-start = (bf16[768,768]{1,0:T(8,128)(2,1)}, bf16[768,768]{1,0:T(8,128)(2,1)S(1)}, u32[]{:S(2)}, u32[]{:S(2)}) collective-permute-start(bf16[768,768]{1,0:T(8,128)(2,1)} %w1a_ref.3), channel_id=1, source_target_pairs={{0,1},{1,0},{2,3},{3,2},{4,5},{5,4},{6,7},{7,6},{8,9},{9,8},{10,11... | collective-permute-start | bytes 3538952 | tf_op jit(solution)/shard_map/ppermute | solution.py:567
  1.2 40.9 %collective-permute-start.1 = (bf16[768,768]{1,0:T(8,128)(2,1)}, bf16[768,768]{1,0:T(8,128)(2,1)S(1)}, u32[]{:S(2)}, u32[]{:S(2)}) collective-permute-start(bf16[768,768]{1,0:T(8,128)(2,1)} %w2a_ref.3), channel_id=1, source_target_pairs={{0,1},{1,0},{2,3},{3,2},{4,5},{5,4},{6,7},{7,6},{8,9},{9,8},{10,11... | collective-permute-start | bytes 3538952 | tf_op jit(solution)/shard_map/ppermute | solution.py:567
  4.4 22.8 %copy-start.2 = (bf16[1,197,768]{2,1,0:T(8,128)(2,1)S(1)}, bf16[1,197,768]{2,1,0:T(8,128)(2,1)}, u32[]{:S(2)}) copy-start(bf16[1,197,768]{2,1,0:T(8,128)(2,1)} %outgrad_ref.3) | copy-start | bytes 907780
  4.4 22.8 %copy-start.9 = (f32[768]{0:T(1024)S(1)}, f32[768]{0:T(1024)}, u32[]{:S(2)}) copy-start(f32[768]{0:T(1024)} %gamma2_ref.1) | copy-start | bytes 9220
  24.3 11.5 %collective-permute-start.3 = (bf16[208,768]{1,0:T(8,128)(2,1)}, bf16[208,768]{1,0:T(8,128)(2,1)S(1)}, u32[]{:S(2)}, u32[]{:S(2)}) collective-permute-start(bf16[208,768]{1,0:T(8,128)(2,1)} %get-tuple-element.54.inner_ref.inner0), channel_id=1, source_target_pairs={{0,2},{1,3},{2,0},{3,1},{4,6},{5,7},{6,4},{7,5},{8,10},{9,11},{10,... | collective-permute-start | bytes 958472 | tf_op jit(solution)/shard_map/ppermute | solution.py:567
  27.5 22.5 %copy-start.1 = (bf16[208,768]{1,0:T(8,128)(2,1)}, bf16[208,768]{1,0:T(8,128)(2,1)S(1)}, u32[]{:S(2)}) copy-start(bf16[208,768]{1,0:T(8,128)(2,1)S(1)} %pad.13.dbranch_ref.dbr0) | copy-start | bytes 958468
  27.5 14.6 %collective-permute-start.4 = (bf16[208,768]{1,0:T(8,128)(2,1)S(1)}, bf16[208,768]{1,0:T(8,128)(2,1)S(1)}, u32[]{:S(2)}, u32[]{:S(2)}) collective-permute-start(bf16[208,768]{1,0:T(8,128)(2,1)S(1)} %pad.13.dbranch_ref.dbr0), channel_id=1, source_target_pairs={{0,2},{1,3},{2,0},{3,1},{4,6},{5,7},{6,4},{7,5},{8,10},{9,11},{10,... | collective-permute-start | bytes 958472 | tf_op jit(solution)/shard_map/ppermute | solution.py:567
  27.6 1.2 collective-permute-start.2
  50.0 9.2 %collective-permute-start.6 = (bf16[208,768]{1,0:T(8,128)(2,1)}, bf16[208,768]{1,0:T(8,128)(2,1)S(1)}, u32[]{:S(2)}, u32[]{:S(2)}) collective-permute-start(bf16[208,768]{1,0:T(8,128)(2,1)} %get-tuple-element.59), channel_id=1, source_target_pairs={{0,2},{1,3},{2,0},{3,1},{4,6},{5,7},{6,4},{7,5},{8,10},{9,11},{10,... | collective-permute-start | bytes 958472 | tf_op jit(solution)/shard_map/ppermute | solution.py:567
  71.0 31.2 %collective-permute-start.14 = (bf16[208,1152]{1,0:T(8,128)(2,1)}, bf16[208,1152]{1,0:T(8,128)(2,1)S(1)}, u32[]{:S(2)}, u32[]{:S(2)}) collective-permute-start(bf16[208,1152]{1,0:T(8,128)(2,1)} %get-tuple-element.76), channel_id=1, source_target_pairs={{0,2},{1,3},{2,0},{3,1},{4,6},{5,7},{6,4},{7,5},{8,10},{9,11},{10,... | collective-permute-start | bytes 1437704 | tf_op jit(solution)/shard_map/ppermute | solution.py:567
  72.4 19.5 %collective-permute-start.12 = (bf16[208,768]{1,0:T(8,128)(2,1)S(1)}, bf16[208,768]{1,0:T(8,128)(2,1)S(1)}, u32[]{:S(2)}, u32[]{:S(2)}) collective-permute-start(bf16[208,768]{1,0:T(8,128)(2,1)S(1)} %copy-done.16), channel_id=1, source_target_pairs={{0,2},{1,3},{2,0},{3,1},{4,6},{5,7},{6,4},{7,5},{8,10},{9,11},{10,... | collective-permute-start | bytes 958472 | tf_op jit(solution)/shard_map/ppermute | solution.py:567
  73.0 25.8 %collective-permute-start.13 = (bf16[208,768]{1,0:T(8,128)(2,1)S(1)}, bf16[208,768]{1,0:T(8,128)(2,1)S(1)}, u32[]{:S(2)}, u32[]{:S(2)}) collective-permute-start(bf16[208,768]{1,0:T(8,128)(2,1)S(1)} %copy-done.17), channel_id=1, source_target_pairs={{0,2},{1,3},{2,0},{3,1},{4,6},{5,7},{6,4},{7,5},{8,10},{9,11},{10,... | collective-permute-start | bytes 958472 | tf_op jit(solution)/shard_map/ppermute | solution.py:567
  74.4 27.8 %collective-permute-start.15 = (bf16[208,384]{1,0:T(8,128)(2,1)}, bf16[208,384]{1,0:T(8,128)(2,1)S(1)}, u32[]{:S(2)}, u32[]{:S(2)}) collective-permute-start(bf16[208,384]{1,0:T(8,128)(2,1)} %get-tuple-element.78), channel_id=1, source_target_pairs={{0,2},{1,3},{2,0},{3,1},{4,6},{5,7},{6,4},{7,5},{8,10},{9,11},{10,... | collective-permute-start | bytes 479240 | tf_op jit(solution)/shard_map/ppermute | solution.py:567
  75.1 56.1 %collective-permute-start.5 = (bf16[208,768]{1,0:T(8,128)(2,1)S(1)}, bf16[208,768]{1,0:T(8,128)(2,1)S(1)}, u32[]{:S(2)}, u32[]{:S(2)}) collective-permute-start(bf16[208,768]{1,0:T(8,128)(2,1)S(1)} %copy-done.18), channel_id=1, source_target_pairs={{0,2},{1,3},{2,0},{3,1},{4,6},{5,7},{6,4},{7,5},{8,10},{9,11},{10,... | collective-permute-start | bytes 958472 | tf_op jit(solution)/shard_map/ppermute | solution.py:567
  106.9 28.5 %collective-permute-start.16 = (bf16[768,768]{1,0:T(8,128)(2,1)}, bf16[768,768]{1,0:T(8,128)(2,1)S(1)}, u32[]{:S(2)}, u32[]{:S(2)}) collective-permute-start(bf16[768,768]{1,0:T(8,128)(2,1)} %shard_map.355), channel_id=1, source_target_pairs={{0,1},{1,0},{2,3},{3,2},{4,5},{5,4},{6,7},{7,6},{8,9},{9,8},{10,11... | collective-permute-start | bytes 3538952 | tf_op jit(solution)/shard_map/ppermute | solution.py:567
  111.6 71.3 %collective-permute-start.23 = (bf16[2,768,768]{2,1,0:T(8,128)(2,1)}, bf16[2,768,768]{2,1,0:T(8,128)(2,1)}, u32[]{:S(2)}, u32[]{:S(2)}) collective-permute-start(bf16[2,768,768]{2,1,0:T(8,128)(2,1)} %shard_map.357), channel_id=1, source_target_pairs={{0,1},{1,0},{2,3},{3,2},{4,5},{5,4},{6,7},{7,6},{8,9},{9,8},{10,11... | collective-permute-start | bytes 7077896 | tf_op jit(solution)/shard_map/ppermute | solution.py:567
  135.3 8.1 %collective-permute-start.7 = (f32[28,768]{1,0:T(8,128)S(1)}, f32[28,768]{1,0:T(8,128)S(1)}, u32[]{:S(2)}, u32[]{:S(2)}) collective-permute-start(f32[28,768]{1,0:T(8,128)S(1)} %concatenate.17), channel_id=1, source_target_pairs={{0,1},{1,0},{2,3},{3,2},{4,5},{5,4},{6,7},{7,6},{8,9},{9,8},{10,11... | collective-permute-start | bytes 258056 | tf_op jit(solution)/shard_map/ppermute | solution.py:567
  140.7 17.4 %copy-start.3 = (bf16[768,768]{1,0:T(8,128)(2,1)S(1)}, bf16[768,768]{1,0:T(8,128)(2,1)}, u32[]{:S(2)}) copy-start(bf16[768,768]{1,0:T(8,128)(2,1)} %shard_map.356) | copy-start | bytes 3538948
  141.9 16.2 %collective-permute-start.17 = (bf16[1,4,96,768]{3,2,1,0:T(8,128)(2,1)S(1)}, bf16[1,4,96,768]{3,2,1,0:T(8,128)(2,1)S(1)}, u32[]{:S(2)}, u32[]{:S(2)}) collective-permute-start(bf16[1,4,96,768]{3,2,1,0:T(8,128)(2,1)S(1)} %dynamic-slice_bitcast_fusion), channel_id=1, source_target_pairs={{0,4},{4,0},{8,12},{12,8},{16,20},{20,16},{24,28},{28,24},{1,5},{5... | collective-permute-start | bytes 1769480 | tf_op jit(solution)/shard_map/ppermute | solution.py:567
  143.4 5.0 %collective-permute-start.8 = (f32[27,768]{1,0:T(8,128)S(1)}, f32[27,768]{1,0:T(8,128)S(1)}, u32[]{:S(2)}, u32[]{:S(2)}) collective-permute-start(f32[27,768]{1,0:T(8,128)S(1)} %slice_add_fusion), channel_id=1, source_target_pairs={{0,2},{1,3},{2,0},{3,1},{4,6},{5,7},{6,4},{7,5},{8,10},{9,11},{10,... | collective-permute-start | bytes 248840 | tf_op jit(solution)/shard_map/ppermute | solution.py:567
  148.5 14.3 %collective-permute-start.9 = (f32[28,768]{1,0:T(8,128)S(1)}, f32[28,768]{1,0:T(8,128)S(1)}, u32[]{:S(2)}, u32[]{:S(2)}) collective-permute-start(f32[28,768]{1,0:T(8,128)S(1)} %pad_maximum_fusion.1), channel_id=1, source_target_pairs={{0,4},{4,0},{8,12},{12,8},{16,20},{20,16},{24,28},{28,24},{1,5},{5... | collective-permute-start | bytes 258056 | tf_op jit(solution)/shard_map/ppermute | solution.py:567
  158.3 8.7 %collective-permute-start.20 = (bf16[1,96,768]{2,1,0:T(8,128)(2,1)S(1)}, bf16[1,96,768]{2,1,0:T(8,128)(2,1)S(1)}, u32[]{:S(2)}, u32[]{:S(2)}) collective-permute-start(bf16[1,96,768]{2,1,0:T(8,128)(2,1)S(1)} %get-tuple-element.147), channel_id=1, source_target_pairs={{0,24},{4,28},{8,16},{12,20},{16,8},{20,12},{24,0},{28,4},{1,25},{... | collective-permute-start | bytes 442376 | tf_op jit(solution)/shard_map/ppermute | solution.py:567
  161.9 11.9 %collective-permute-start.19 = (bf16[1,96,768]{2,1,0:T(8,128)(2,1)S(1)}, bf16[1,96,768]{2,1,0:T(8,128)(2,1)S(1)}, u32[]{:S(2)}, u32[]{:S(2)}) collective-permute-start(bf16[1,96,768]{2,1,0:T(8,128)(2,1)S(1)} %get-tuple-element.148), channel_id=1, source_target_pairs={{0,16},{4,20},{8,24},{12,28},{16,0},{20,4},{24,8},{28,12},{1,17},{... | collective-permute-start | bytes 442376 | tf_op jit(solution)/shard_map/ppermute | solution.py:567
  161.9 11.9 %collective-permute-start.18 = (bf16[1,96,768]{2,1,0:T(8,128)(2,1)S(1)}, bf16[1,96,768]{2,1,0:T(8,128)(2,1)S(1)}, u32[]{:S(2)}, u32[]{:S(2)}) collective-permute-start(bf16[1,96,768]{2,1,0:T(8,128)(2,1)S(1)} %get-tuple-element.146), channel_id=1, source_target_pairs={{0,8},{4,12},{8,0},{12,4},{16,24},{20,28},{24,16},{28,20},{1,9},{5... | collective-permute-start | bytes 442376 | tf_op jit(solution)/shard_map/ppermute | solution.py:567
  162.8 12.7 %collective-permute-start.10 = (f32[28,768]{1,0:T(8,128)S(1)}, f32[28,768]{1,0:T(8,128)S(1)}, u32[]{:S(2)}, u32[]{:S(2)}) collective-permute-start(f32[28,768]{1,0:T(8,128)S(1)} %fusion.12), channel_id=1, source_target_pairs={{0,8},{4,12},{8,0},{12,4},{16,24},{20,28},{24,16},{28,20},{1,9},{5... | collective-permute-start | bytes 258056 | tf_op jit(solution)/shard_map/ppermute | solution.py:567
  173.9 8.9 %collective-permute-start.21 = (bf16[96,768]{1,0:T(8,128)(2,1)S(1)}, bf16[96,768]{1,0:T(8,128)(2,1)S(1)}, u32[]{:S(2)}, u32[]{:S(2)}) collective-permute-start(bf16[96,768]{1,0:T(8,128)(2,1)S(1)} %bitcast.73), channel_id=1, source_target_pairs={{0,2},{1,3},{2,0},{3,1},{4,6},{5,7},{6,4},{7,5},{8,10},{9,11},{10,... | collective-permute-start | bytes 442376 | tf_op jit(solution)/shard_map/ppermute | solution.py:567
  175.5 6.6 %collective-permute-start.11 = (f32[28,768]{1,0:T(8,128)S(1)}, f32[28,768]{1,0:T(8,128)S(1)}, u32[]{:S(2)}, u32[]{:S(2)}) collective-permute-start(f32[28,768]{1,0:T(8,128)S(1)} %add.95), channel_id=1, source_target_pairs={{0,16},{4,20},{8,24},{12,28},{16,0},{20,4},{24,8},{28,12},{1,17},{... | collective-permute-start | bytes 258056 | tf_op jit(solution)/shard_map/ppermute | solution.py:567
  182.8 9.6 %collective-permute-start.22 = (bf16[2,96,768]{2,1,0:T(8,128)(2,1)S(1)}, bf16[2,96,768]{2,1,0:T(8,128)(2,1)S(1)}, u32[]{:S(2)}, u32[]{:S(2)}) collective-permute-start(bf16[2,96,768]{2,1,0:T(8,128)(2,1)S(1)} %pad_maximum_fusion), channel_id=1, source_target_pairs={{0,1},{1,0},{2,3},{3,2},{4,5},{5,4},{6,7},{7,6},{8,9},{9,8},{10,11... | collective-permute-start | bytes 884744 | tf_op jit(solution)/shard_map/ppermute | solution.py:567
  190.1 28.4 %collective-permute-start.24 = (bf16[2,4,96,768]{3,2,0,1:T(8,128)(2,1)S(1)}, bf16[2,4,96,768]{3,2,0,1:T(8,128)(2,1)S(1)}, u32[]{:S(2)}, u32[]{:S(2)}) collective-permute-start(bf16[2,4,96,768]{3,2,0,1:T(8,128)(2,1)S(1)} %bitcast.74), channel_id=1, source_target_pairs={{0,4},{4,0},{8,12},{12,8},{16,20},{20,16},{24,28},{28,24},{1,5},{5... | collective-permute-start | bytes 3538952 | tf_op jit(solution)/shard_map/ppermute | solution.py:567
  219.0 11.9 %collective-permute-start.27 = (bf16[2,96,768]{2,1,0:T(8,128)(2,1)S(1)}, bf16[2,96,768]{2,1,0:T(8,128)(2,1)S(1)}, u32[]{:S(2)}, u32[]{:S(2)}) collective-permute-start(bf16[2,96,768]{2,1,0:T(8,128)(2,1)S(1)} %get-tuple-element.140), channel_id=1, source_target_pairs={{0,24},{4,28},{8,16},{12,20},{16,8},{20,12},{24,0},{28,4},{1,25},{... | collective-permute-start | bytes 884744 | tf_op jit(solution)/shard_map/ppermute | solution.py:567
  220.5 25.1 %collective-permute-start.26 = (bf16[2,96,768]{2,1,0:T(8,128)(2,1)S(1)}, bf16[2,96,768]{2,1,0:T(8,128)(2,1)S(1)}, u32[]{:S(2)}, u32[]{:S(2)}) collective-permute-start(bf16[2,96,768]{2,1,0:T(8,128)(2,1)S(1)} %get-tuple-element.141), channel_id=1, source_target_pairs={{0,16},{4,20},{8,24},{12,28},{16,0},{20,4},{24,8},{28,12},{1,17},{... | collective-permute-start | bytes 884744 | tf_op jit(solution)/shard_map/ppermute | solution.py:567
  220.5 25.1 %collective-permute-start.25 = (bf16[2,96,768]{2,1,0:T(8,128)(2,1)S(1)}, bf16[2,96,768]{2,1,0:T(8,128)(2,1)S(1)}, u32[]{:S(2)}, u32[]{:S(2)}) collective-permute-start(bf16[2,96,768]{2,1,0:T(8,128)(2,1)S(1)} %get-tuple-element.139), channel_id=1, source_target_pairs={{0,8},{4,12},{8,0},{12,4},{16,24},{20,28},{24,16},{28,20},{1,9},{5... | collective-permute-start | bytes 884744 | tf_op jit(solution)/shard_map/ppermute | solution.py:567
  (21 other events, 120.1 us)

commit v2 on v1

v2 whole, which is shorter than its diff:
```python
import functools

import jax
import jax.numpy as jnp
from jax import lax
from jax.experimental import pallas as pl
from jax.experimental.pallas import tpu as pltpu
from jax.sharding import PartitionSpec as P

F32 = jnp.float32
BF16 = jnp.bfloat16
EPS = 1e-06
LANES = 128
COST = dict(pair=0.7, keep=1.5, back=9, norm=4, late=2.6, table=6, mlp=4, end=2, spread=0.7, total=0.5)
UNROLL_F = 6
UNROLL_B = 6
VMEM_LIMIT = 16 * 1024 * 1024


def round_up(value, step):
    return -(-value // step) * step


def dot_nn(left, right):
    return lax.dot_general(left, right, (((1,), (0,)), ((), ())), preferred_element_type=F32)


def dot_nt(left, right):
    return lax.dot_general(left, right, (((1,), (1,)), ((), ())), preferred_element_type=F32)


def dot_tn(left, right):
    return lax.dot_general(left, right, (((0,), (0,)), ((), ())), preferred_element_type=F32)


def row_of(ref):
    return ref[...].reshape(1, ref.shape[0])


def norm_stats(values):
    middle = jnp.mean(values, axis=-1, keepdims=True)
    centred = values - middle
    spread = jnp.mean(centred * centred, axis=-1, keepdims=True)
    root = lax.rsqrt(spread + EPS)
    return centred * root, root


def norm_back(d_out, xhat, root, gain):
    t = d_out * gain
    mean_t = jnp.mean(t, axis=-1, keepdims=True)
    mean_tx = jnp.mean(t * xhat, axis=-1, keepdims=True)
    return root * (t - mean_t - xhat * mean_tx)


SPACES = {
    "h": (pltpu.HBM, pltpu.VMEM),
    "v": (None, pltpu.VMEM),
    "s": (None, pltpu.SMEM),
    "a": (pltpu.HBM, pl.ANY),
}


def call(body, outs, kinds, values, scratch=(), cost=1, deps=(), carry=()):
    specs, given = [], []
    for kind, value in zip(kinds, values, strict=True):
        keep, space = SPACES[kind]
        specs.append(pl.BlockSpec(memory_space=space))
        given.append(value if keep is None else pltpu.with_memory_space_constraint(value, keep))
    outs = outs if isinstance(outs, tuple) else (outs,)
    n_in, n_more, n_out = len(given), len(deps) + len(carry), len(outs)

    def inner(*refs):
        rest = refs[n_in + n_more :]
        body(*refs[:n_in], *rest[:n_out], *rest[n_out + len(carry) :])

    anywhere = pl.BlockSpec(memory_space=pl.ANY)
    out = pl.pallas_call(
        inner,
        name=getattr(body, "func", body).__name__,
        out_shape=outs + tuple(jax.ShapeDtypeStruct(c.shape, c.dtype) for c in carry),
        in_specs=specs + [anywhere] * n_more,
        out_specs=tuple(pl.BlockSpec(memory_space=pltpu.VMEM) for _ in outs)
        + (anywhere,) * len(carry),
        input_output_aliases={n_in + len(deps) + at: n_out + at for at in range(len(carry))},
        scratch_shapes=list(scratch),
        compiler_params=pltpu.CompilerParams(vmem_limit_bytes=VMEM_LIMIT),
        cost_estimate=pl.CostEstimate(
            flops=int(cost * 1e9), bytes_accessed=1000, transcendentals=0
        ),
    )(*given, *deps, *carry)
    return out if len(out) > 1 else out[0]


def shape(dims, kind):
    return pltpu.VMEM(dims, kind)


def shape_out(dims, kind):
    return pltpu.HBM(dims, kind)


def load_padded(source_ref, pad_ref):
    rows = source_ref.shape[1]
    tail = (rows // 8) * 8
    pad_ref[tail:, :] = jnp.zeros_like(pad_ref[tail:, :])
    pad_ref[0:rows, :] = source_ref[0].astype(F32)
    return pad_ref[...]


def mask_column(mask_ref, wide_ref, pad):
    rows = mask_ref.shape[1]
    wide_ref[...] = jnp.zeros_like(wide_ref)
    line = jnp.where(mask_ref[...] > 0, 1.0, 0.0)
    wide_ref[:, 0:rows] = jnp.broadcast_to(line, (LANES, rows))
    return wide_ref[...].T[:pad]


def forward_body(
    heads,
    patches_ref,
    mask_ref,
    index_ref,
    token_ref,
    gain1_ref,
    bias1_ref,
    qbias_ref,
    vbias_ref,
    table_ref,
    pbias_ref,
    gamma1_ref,
    gain2_ref,
    bias2_ref,
    wqkv_hbm,
    wproj_hbm,
    mask_out,
    normed_ref,
    q_ref,
    k_ref,
    v_ref,
    probs_ref,
    mixed_ref,
    attended_ref,
    hidden_ref,
    inner_ref,
    pad_s,
    wide_s,
    index_s,
    table_s,
    bias_s,
    wqkv_ref,
    wproj_ref,
    sems,
):
    rows, width = patches_ref.shape[1:]
    pad = normed_ref.shape[0]
    keys = k_ref.shape[0]
    head_size = width // heads
    copy_qkv = pltpu.make_async_copy(wqkv_hbm, wqkv_ref, sems.at[0])
    copy_qkv.start()
    copy_proj = pltpu.make_async_copy(wproj_hbm, wproj_ref, sems.at[1])
    copy_proj.start()

    index_s[...] = jnp.zeros_like(index_s)
    index_s[0:rows, 0:rows] = index_ref[...]
    entries = table_ref.shape[1]
    chunks = table_s.shape[2] // LANES
    top = jnp.max(jnp.abs(table_ref[...]))
    grow = 32767.0 / jnp.maximum(top, 1e-30)
    shrink = jnp.maximum(top, 1e-30) / 32767.0
    whole = jnp.round(table_ref[...] * grow).astype(jnp.int32)
    table_s[...] = jnp.zeros_like(table_s)
    for pair in range(heads // 2):
        both = whole[2 * pair : 2 * pair + 1] * 65536 + (whole[2 * pair + 1 : 2 * pair + 2] & 65535)
        table_s[pair, :, 0:entries] = jnp.broadcast_to(both, (8, entries))
    key_lane = lax.broadcasted_iota(jnp.int32, (1, LANES), 1)

    def gather_step(tile, carry):
        at_rows = pl.ds(pl.multiple_of(tile * 8, 8), 8)
        for half in range(keys // LANES):
            lanes = slice(half * LANES, (half + 1) * LANES)
            at = index_s[at_rows, lanes]
            low = at & (LANES - 1)
            high = at >> 7
            marks = [high == chunk for chunk in range(chunks)]
            real = key_lane + half * LANES < rows
            for pair in range(heads // 2):
                value = None
                for chunk in range(chunks):
                    line = table_s[pair, :, chunk * LANES : (chunk + 1) * LANES]
                    found = jnp.take_along_axis(line, low, axis=1, mode="promise_in_bounds")
                    value = found if value is None else jnp.where(marks[chunk], found, value)
                one = (value >> 16).astype(F32) * shrink
                two = ((value << 16) >> 16).astype(F32) * shrink
                if (half + 1) * LANES > rows:
                    one = jnp.where(real, one, -1e30)
                    two = jnp.where(real, two, -1e30)
                bias_s[2 * pair, at_rows, lanes] = one
                bias_s[2 * pair + 1, at_rows, lanes] = two
        return carry

    lax.fori_loop(0, pad // 8, gather_step, 0, unroll=2)

    column = mask_column(mask_ref, wide_s, pad)
    mask_out[...] = column
    picked = column[:, 0:1] > 0
    start = jnp.where(picked, row_of(token_ref), load_padded(patches_ref, pad_s))
    pad_s[...] = start
    xhat, _ = norm_stats(start)
    normed = (xhat * row_of(gain1_ref) + row_of(bias1_ref)).astype(BF16)
    normed_ref[...] = normed
    copy_qkv.wait()
    scale = head_size ** (-0.5)
    q_ref[...] = ((dot_nn(normed, wqkv_ref[:, :width]) + row_of(qbias_ref)) * scale).astype(BF16)
    k_ref[0:pad, :] = dot_nn(normed, wqkv_ref[:, width : 2 * width]).astype(BF16)
    k_ref[pad:, :] = jnp.zeros_like(k_ref[pad:, :])
    v_ref[0:pad, :] = (dot_nn(normed, wqkv_ref[:, 2 * width :]) + row_of(vbias_ref)).astype(BF16)
    v_ref[pad:, :] = jnp.zeros_like(v_ref[pad:, :])

    lane = lax.broadcasted_iota(jnp.int32, (1, LANES), 1)
    first = lane < head_size

    def pair_step(pair, carry):
        at = pl.ds(pl.multiple_of(pair * LANES, LANES), LANES)
        query = q_ref[:, at]
        key = k_ref[:, at]
        value = v_ref[:, at]
        outs = []
        for side in range(2):
            head = pair * 2 + side
            own = first if side == 0 else jnp.logical_not(first)
            scores = dot_nt(jnp.where(own, query, jnp.zeros_like(query)), key) + bias_s[head]
            top = jnp.max(scores, axis=-1, keepdims=True)
            grown = jnp.exp(scores - top)
            probs = (grown * (1.0 / jnp.sum(grown, axis=-1, keepdims=True))).astype(BF16)
            probs_ref[head] = probs
            outs.append(dot_nn(probs, value))
        mixed_ref[:, at] = jnp.where(first, outs[0], outs[1]).astype(BF16)
        return carry

    lax.fori_loop(0, heads // 2, pair_step, 0, unroll=UNROLL_F)
    copy_proj.wait()
    attended = dot_nn(mixed_ref[...], wproj_ref[...]) + row_of(pbias_ref)
    attended_ref[...] = attended
    hidden = pad_s[...] + row_of(gamma1_ref) * attended
    hidden_ref[...] = hidden
    xhat2, _ = norm_stats(hidden)
    inner_ref[...] = (xhat2 * row_of(gain2_ref) + row_of(bias2_ref)).astype(BF16)


def forward(heads, pad, patches, row_mask, rel_index, token, gain1, bias1, qbias, vbias, table_t,
            pbias, gamma1, gain2, bias2, wqkv, wproj):
    rows, width = patches.shape[1:]
    keys = round_up(pad, LANES)
    entries = round_up(table_t.shape[1], LANES)
    outs = (
        shape_out((pad, LANES), F32),
        shape_out((pad, width), BF16),
        shape_out((pad, width), BF16),
        shape_out((keys, width), BF16),
        shape_out((keys, width), BF16),
        shape_out((heads, pad, keys), BF16),
        shape_out((pad, width), BF16),
        shape_out((pad, width), F32),
        shape_out((pad, width), F32),
        shape((pad, width), BF16),
    )
    return call(
        functools.partial(forward_body, heads),
        outs,
        "hhhhhhhhhhhhhaa",
        (patches, row_mask, rel_index, token, gain1, bias1, qbias, vbias, table_t, pbias, gamma1,
         gain2, bias2, wqkv, wproj),
        (
            pltpu.VMEM((pad, width), F32),
            pltpu.VMEM((LANES, keys), F32),
            pltpu.VMEM((pad, keys), jnp.int32),
            pltpu.VMEM((heads // 2, 8, entries), jnp.int32),
            pltpu.VMEM((heads, pad, keys), F32),
            pltpu.VMEM(wqkv.shape, BF16),
            pltpu.VMEM(wproj.shape, BF16),
            pltpu.SemaphoreType.DMA((2,)),
        ),
        cost=12,
    )


def mlp_body(
    first, inner_ref, b1a_ref, b1b_ref, w1a_ref, w1b_ref, w2a_ref, w2b_ref, bias_ref, *rest
):
    if first:
        grads, masks, gamma2_ref = rest[0:2], rest[2:4], rest[4]
        rest = rest[5:]
        dbranches, rest = rest[0:2], rest[2:]
        cot_out, rest = rest[0], rest[1:]
        pad_s, wide_s = rest[-2:]
        rest = rest[:-2]
        pad = inner_ref.shape[0]
        for grad_ref, mask_ref, out_ref in zip(grads, masks, dbranches):
            column = mask_column(mask_ref, wide_s, pad)[:, 0:1]
            cotangent = load_padded(grad_ref, pad_s) * column
            out_ref[...] = (row_of(gamma2_ref) * cotangent).astype(BF16)
            if out_ref is dbranches[0]:
                own_cotangent = cotangent
            else:
                cot_out[...] = cotangent
        dbranch = dbranches[0][...]
        cotangent = own_cotangent
    else:
        dbranch, cotangent = rest[0][...], rest[1][...]
        rest = rest[2:]
    acta_ref, actb_ref, dprea_ref, dpreb_ref, branch_ref, dinner_ref, sums_ref = rest
    inner = inner_ref[...]
    branch = None
    dinner = None
    for at, (w1, w2, b1, act_out, dpre_out) in enumerate((
        (w1a_ref, w2a_ref, b1a_ref, acta_ref, dprea_ref),
        (w1b_ref, w2b_ref, b1b_ref, actb_ref, dpreb_ref),
    )):
        pre = dot_nn(inner, w1[...]) + row_of(b1).astype(F32)
        phi = 0.5 + 0.5 * lax.erf(pre * (0.5**0.5))
        act = (pre * phi).astype(BF16)
        act_out[...] = act
        slope = phi + pre * (jnp.exp(-0.5 * pre * pre) * 0.3989422804014327)
        dact = dot_nt(dbranch, w2[...])
        dpre = (dact * slope).astype(BF16)
        dpre_out[...] = dpre
        sums_ref[at : at + 1, :] = jnp.sum(dpre.astype(F32), axis=0, keepdims=True)
        this_branch = dot_nn(act, w2[...])
        this_dinner = dot_nt(dpre, w1[...])
        branch = this_branch if branch is None else branch + this_branch
        dinner = this_dinner if dinner is None else dinner + this_dinner
    if first:
        branch = branch + row_of(bias_ref)
        sums_ref[3:4, :] = jnp.sum(dbranch.astype(F32), axis=0, keepdims=True)
    else:
        sums_ref[3:4, :] = jnp.zeros_like(sums_ref[3:4, :])
    branch_ref[...] = branch.astype(branch_ref.dtype)
    dinner_ref[...] = dinner.astype(dinner_ref.dtype)
    sums_ref[2:3, :] = jnp.sum(cotangent * branch, axis=0, keepdims=True)
    sums_ref[4:8, :] = jnp.zeros_like(sums_ref[4:8, :])


def mlp(inner, weights, bias, given, first, deps=()):
    pad, width = inner.shape
    ff = weights[2].shape[1]
    kind = F32 if first else BF16
    outs = (
        (shape((pad, ff), BF16),) * 4
        + (shape_out((pad, width), kind), shape((pad, width), kind))
        + (shape((8, ff), F32),)
    )
    scratch = ()
    if first:
        outs = (shape((pad, width), BF16),) * 2 + (shape((pad, width), F32),) + outs
        scratch = (pltpu.VMEM((pad, width), F32), pltpu.VMEM((LANES, round_up(pad, LANES)), F32))
    return call(
        functools.partial(mlp_body, first), outs, "vhhvvvvh" + ("hvhvh" if first else "vv"),
        (inner, *weights, bias, *given), scratch, cost=COST["mlp"], deps=deps,
    )


def split_rows(out_send, out_keep, at, total, low, block):
    for step in range(total.shape[0] // (2 * block)):
        even = total[2 * step * block : (2 * step + 1) * block]
        odd = total[(2 * step + 1) * block : (2 * step + 2) * block]
        out_send[at, step] = jnp.where(low, even, odd).astype(BF16)
        out_keep[at, step] = jnp.where(low, odd, even).astype(BF16)


def pair_grad_body(left0, left1, right0, right1, out_ref):
    total = dot_tn(left0[...], right0[...]) + dot_tn(left1[...], right1[...])
    out_ref[...] = total.astype(BF16)


def pair_grad(left0, left1, right0, right1, deps=(), carry=()):
    return call(
        pair_grad_body, shape((left0.shape[1], right0.shape[1]), BF16), "vvvv",
        (left0, left1, right0, right1), cost=COST["pair"], deps=deps, carry=carry,
    )


def fc_keep_body(block, where_ref, *refs):
    send_ref, keep_ref = refs[10:]
    low = where_ref[2] > 0
    for at in range(2):
        left0, left1, right0, right1, other = refs[5 * at : 5 * at + 5]
        total = dot_tn(left0[...], right0[...]) + dot_tn(left1[...], right1[...])
        split_rows(send_ref, keep_ref, at, total + other[...].astype(F32), low, block)


def fc_keep(where, block, one, two, deps=(), carry=()):
    width, ff = one[0].shape[1], one[2].shape[1]
    outs = (shape((2, width // (2 * block), block, ff), BF16),) * 2
    return call(
        functools.partial(fc_keep_body, block), outs, "s" + "v" * 10, (where, *one, *two),
        cost=COST["keep"], deps=deps, carry=carry,
    )


def backward_body(
    heads,
    rows,
    where_ref,
    dinner0_ref,
    dinner1_ref,
    hidden_ref,
    attended_ref,
    outgrad_ref,
    mask_ref,
    gain2_ref,
    gamma1_ref,
    wproj_ref,
    q_ref,
    k_ref,
    v_ref,
    probs_ref,
    dhidden_ref,
    dattkeep_ref,
    dqkv_ref,
    send_ref,
    dscores_ref,
    sums_ref,
    pad_s,
    dmixed_s,
):
    pad, width = hidden_ref.shape
    head_size = width // heads
    cotangent = load_padded(outgrad_ref, pad_s) * mask_ref[:, 0:1]
    xhat, root = norm_stats(hidden_ref[...])
    dinner = dinner0_ref[...].astype(F32) + dinner1_ref[...].astype(F32)
    dhidden = cotangent + norm_back(dinner, xhat, root, row_of(gain2_ref))
    dhidden_ref[...] = dhidden
    datt = (row_of(gamma1_ref) * dhidden).astype(BF16)
    high = where_ref[0] > 0
    half = width // 2
    three = 3 * half
    send_ref[:, three:] = jnp.where(high, datt[:, :half], datt[:, half:])
    dattkeep_ref[...] = jnp.where(high, datt[:, half:], datt[:, :half])
    dmixed_s[...] = dot_nt(datt, wproj_ref[...]).astype(BF16)
    sums_ref[0:1, :] = jnp.sum(dinner * xhat, axis=0, keepdims=True)
    sums_ref[1:2, :] = jnp.sum(dinner, axis=0, keepdims=True)
    sums_ref[2:3, :] = jnp.sum(dhidden * attended_ref[...], axis=0, keepdims=True)
    sums_ref[3:4, :] = jnp.sum(datt.astype(F32), axis=0, keepdims=True)

    lane = lax.broadcasted_iota(jnp.int32, (1, LANES), 1)
    first = lane < head_size
    scale = head_size ** (-0.5)

    def pair_step(pair, carry):
        start = pl.multiple_of(pair * LANES, LANES)
        at = pl.ds(start, LANES)
        query = q_ref[:, at]
        key = k_ref[:, at]
        value = v_ref[:, at]
        dmixed = dmixed_s[:, at]
        dq, dk, dv = [], [], []
        for side in range(2):
            head = pair * 2 + side
            own = first if side == 0 else jnp.logical_not(first)
            probs_b = probs_ref[head]
            probs = probs_b.astype(F32)
            dprobs = dot_nt(jnp.where(own, dmixed, jnp.zeros_like(dmixed)), value)
            inside = jnp.sum(probs * dprobs, axis=-1, keepdims=True)
            dscores = (probs * (dprobs - inside)).astype(BF16)
            dscores_ref[head] = dscores
            dq.append(dot_nn(dscores, key))
            dk.append(dot_tn(dscores, query))
            dv.append(dot_tn(probs_b, dmixed))
        dqkv_ref[:, at] = (jnp.where(first, dq[0], dq[1]) * scale).astype(BF16)
        dqkv_ref[:, pl.ds(pl.multiple_of(start + width, LANES), LANES)] = (
            jnp.where(first, dk[0], dk[1])[:pad].astype(BF16)
        )
        dqkv_ref[:, pl.ds(pl.multiple_of(start + 2 * width, LANES), LANES)] = (
            jnp.where(first, dv[0], dv[1])[:pad].astype(BF16)
        )
        return carry

    lax.fori_loop(0, heads // 2, pair_step, 0, unroll=UNROLL_B)
    send_ref[:, :three] = jnp.where(high, dqkv_ref[:, :three], dqkv_ref[:, three:])
    sums_ref[4:5, :] = jnp.sum(dqkv_ref[:, :width].astype(F32), axis=0, keepdims=True)
    sums_ref[5:6, :] = jnp.sum(dqkv_ref[:, 2 * width :].astype(F32), axis=0, keepdims=True)
    sums_ref[6:8, :] = jnp.zeros((2, width), F32)


def backward(heads, where, dinner0, dinner1, hidden, attended, out_grad, mask_col, gain2, gamma1,
             wproj, q, k, v, probs, deps=()):
    pad, width = hidden.shape
    keys = k.shape[0]
    outs = (
        shape((pad, width), F32),
        shape_out((pad, width // 2), BF16),
        shape_out((pad, 3 * width), BF16),
        shape((pad, 2 * width), BF16),
        shape((heads, pad, keys), BF16),
        shape((8, width), F32),
    )
    return call(
        functools.partial(backward_body, heads, out_grad.shape[1]),
        outs,
        "svvhhhhhhhhhhh",
        (where, dinner0, dinner1, hidden, attended, out_grad, mask_col, gain2, gamma1, wproj, q, k,
         v, probs),
        (pltpu.VMEM((pad, width), F32), pltpu.VMEM((pad, width), BF16)),
        cost=COST["back"],
        deps=deps,
    )


def first_norm_body(
    patches_ref, mask_ref, token_ref, gain1_ref, dqkv_ref, wqkv_ref, dhidden_ref,
    patchgrad_ref, sums_ref, pad_s,
):
    rows, width = patches_ref.shape[1:]
    picked = mask_ref[:, 0:1] > 0
    start = jnp.where(picked, row_of(token_ref), load_padded(patches_ref, pad_s))
    xhat, root = norm_stats(start)
    dnormed = dot_nt(dqkv_ref[...], wqkv_ref[...])
    dstart = dhidden_ref[...] + norm_back(dnormed, xhat, root, row_of(gain1_ref))
    patchgrad_ref[0] = jnp.where(picked, 0.0, dstart)[0:rows]
    sums_ref[0:1, :] = jnp.sum(jnp.where(picked, dstart, 0.0), axis=0, keepdims=True)
    sums_ref[1:2, :] = jnp.sum(dnormed * xhat, axis=0, keepdims=True)
    sums_ref[2:3, :] = jnp.sum(dnormed, axis=0, keepdims=True)
    sums_ref[3:8, :] = jnp.zeros((5, width), F32)


def first_norm(patches, mask_col, token, gain1, dqkv, wqkv, dhidden, deps=()):
    rows, width = patches.shape[1:]
    pad = mask_col.shape[0]
    outs = (shape_out((1, rows, width), F32), shape((8, width), F32))
    return call(
        first_norm_body, outs, "hhhhhhv",
        (patches, mask_col, token, gain1, dqkv, wqkv, dhidden),
        (pltpu.VMEM((pad, width), F32),), cost=COST["norm"], deps=deps,
    )


def layer_end_body(hidden_ref, branch0_ref, branch1_ref, gamma2_ref, out_ref):
    branch = branch0_ref[...] + branch1_ref[...].astype(F32)
    layer = hidden_ref[...] + row_of(gamma2_ref) * branch
    out_ref[0] = layer[0 : out_ref.shape[1]].astype(BF16)


def layer_end(rows, hidden, branch0, branch1, gamma2):
    return call(
        layer_end_body, shape_out((1, rows, hidden.shape[1]), BF16), "hhvh",
        (hidden, branch0, branch1, gamma2), cost=COST["end"],
    )


def table_grad_body(
    where_ref, index_ref, ds_ref, sums_b_ref, sums_n_ref, sums0_ref, sums1_ref, out_ref, index_s,
    total_s,
):
    rows = index_ref.shape[0]
    pad, head_pad, keys = ds_ref.shape
    high_count = total_s.shape[0] // head_pad
    index_s[...] = jnp.zeros_like(index_s)
    index_s[0:rows, 0:rows] = index_ref[...]
    total_s[...] = jnp.zeros_like(total_s)
    below = lax.broadcasted_iota(jnp.int32, (LANES, keys), 0).astype(BF16)
    ones = jnp.ones((LANES, keys), BF16)
    group = 16

    def step(at, carry):
        base = pl.multiple_of(at * group, group)
        lines = index_s[pl.ds(base, group), :]
        low = (lines & (LANES - 1)).astype(F32).astype(BF16)
        high = (lines >> 7).astype(F32).astype(BF16)
        total = None
        for i in range(group):
            onehot = jnp.where(below == low[i : i + 1], ones, jnp.zeros_like(ones))
            ds = ds_ref[base + i]
            left = jnp.concatenate(
                [
                    jnp.where(high[i : i + 1] == jnp.asarray(part, BF16), ds, jnp.zeros_like(ds))
                    for part in range(high_count)
                ],
                axis=0,
            )
            one = dot_nt(left, onehot)
            total = one if total is None else total + one
        total_s[...] += total
        return carry

    lax.fori_loop(0, pad // group, step, 0, unroll=2)
    for part in range(high_count):
        out_ref[0:head_pad, part * LANES : (part + 1) * LANES] = total_s[
            part * head_pad : (part + 1) * head_pad
        ]
    sums = sums0_ref[...] + sums1_ref[...]
    out_ref[head_pad : head_pad + 6, :] = sums_b_ref[0:6, :]
    out_ref[head_pad + 6 : head_pad + 8, :] = sums[2:4]
    out_ref[head_pad + 8 : head_pad + 11, :] = sums_n_ref[0:3, :]
    for part in range(4):
        mine = jnp.where(where_ref[0] == part // 2, 1.0, 0.0)
        own = jnp.where(where_ref[1] == part % 2, sums[0:1], sums[1:2])
        out_ref[head_pad + 11 + part : head_pad + 12 + part, :] = mine * own
    out_ref[head_pad + 15 :, :] = jnp.zeros_like(out_ref[head_pad + 15 :, :])


def table_grad(where, rel_index, dscores, sums_b, sums_n, sums0, sums1, entries, deps=()):
    pad, head_pad, keys = dscores.shape
    high_count = round_up(entries, LANES) // LANES
    width = sums_b.shape[1]
    return call(
        table_grad_body, shape((head_pad + 16, width), F32), "shvvvvv",
        (where, rel_index, dscores, sums_b, sums_n, sums0, sums1),
        (pltpu.VMEM((pad, keys), jnp.int32), pltpu.VMEM((high_count * head_pad, LANES), F32)),
        cost=COST["table"], deps=deps,
    )


def gather_sum_body(count, *refs):
    for at, out_ref in enumerate(refs[count:]):
        total = refs[0][at].astype(F32)
        for ref in refs[1:count]:
            total = total + ref[at].astype(F32)
        out_ref[...] = total.astype(out_ref.dtype)


def gather_sum(parts, kind, deps=(), carry=()):
    count, block, width = parts[0].shape
    make = shape_out if kind == F32 else shape
    return call(
        functools.partial(gather_sum_body, len(parts)), (make((block, width), kind),) * count,
        "v" * len(parts), parts, cost=COST["total"], deps=deps, carry=carry,
    )


def late_grad_body(
    block, where_ref, normed0, normed1, mixed0, mixed1, dqkv_ref, met_ref, datt_ref, *rest
):
    width = normed0.shape[1]
    half, three = width // 2, 3 * width // 2
    high = where_ref[0] > 0
    core = where_ref[1] > 0
    low = where_ref[2] > 0
    second = jnp.logical_not(core) if block is None else core
    own = jnp.where(high, dqkv_ref[:, three:], dqkv_ref[:, :three])
    total0, total1 = None, None
    for normed_ref, mixed_ref, part, datt in (
        (normed0, mixed0, own, datt_ref[...]),
        (normed1, mixed1, met_ref[:, :three], met_ref[:, three:]),
    ):
        normed = normed_ref[...]
        right0 = jnp.where(second, part[:, width:], part[:, :half])
        left1 = jnp.where(second, mixed_ref[...], normed)
        right1 = jnp.where(second, datt, part[:, half:width])
        this0 = dot_tn(normed, right0)
        this1 = dot_tn(left1, right1)
        total0 = this0 if total0 is None else total0 + this0
        total1 = this1 if total1 is None else total1 + this1
    total = jnp.concatenate([total0, total1], axis=1)
    if block is None:
        rest[0][...] = total.astype(BF16)
    else:
        total = total + rest[0][...].astype(F32)
        split_rows(rest[1], rest[2], 0, total, low, block)


def late_grad(where, block, normed0, normed1, mixed0, mixed1, dqkv, met, datt, other=None,
              deps=(), carry=()):
    width = normed0.shape[1]
    values = (where, normed0, normed1, mixed0, mixed1, dqkv, met, datt)
    if other is None:
        block = None
        outs = shape((width, width), BF16)
    else:
        values += (other,)
        outs = (shape((1, width // (2 * block), block, width), BF16),) * 2
    return call(
        functools.partial(late_grad_body, block), outs, "shvhvhvhv"[: len(values)], values,
        cost=COST["late"], deps=deps, carry=carry,
    )


def spread_body(where_ref, keep_ref, met_ref, *outs):
    high = where_ref[3]
    for step, out in enumerate(outs):
        at = high ^ step
        for item in range(keep_ref.shape[0]):
            out[item] = (keep_ref[item, at].astype(F32) + met_ref[item, at].astype(F32)).astype(BF16)


def spread(where, keep, met, deps=(), carry=()):
    count, halves, block, width = keep.shape
    return call(
        spread_body, (shape((count, block, width), BF16),) * halves, "svv", (where, keep, met),
        cost=COST["spread"], deps=deps, carry=carry,
    )


def on_device(
    dp,
    patches,
    row_mask,
    out_grad,
    rel_index,
    mask_token,
    ln1_gain,
    ln1_bias,
    qkv_weight,
    query_bias,
    value_bias,
    rel_table,
    proj_weight,
    proj_bias,
    gamma1,
    ln2_gain,
    ln2_bias,
    fc1_weight,
    fc1_bias,
    fc2_weight,
    fc2_bias,
    gamma2,
):
    rows, width = patches.shape[1:]
    entries, heads = rel_table.shape
    pad = round_up(rows, 16)
    mp_at = lax.axis_index("mp")
    dp_at = lax.axis_index("dp")
    x_at, core_at = mp_at // 2, mp_at % 2
    where = jnp.stack([x_at, core_at, dp_at % 2, dp_at // 2]).astype(jnp.int32)

    def swap(axis, bit):
        count = 4 if axis == "mp" else dp
        pairs = [(at, at ^ bit) for at in range(count)]
        return lambda value: lax.ppermute(value, axis, pairs)

    over_core, over_x, over_low = swap("mp", 1), swap("mp", 2), swap("dp", 1)

    out_grad1, row_mask1 = over_x(out_grad), over_x(row_mask)
    b1b, w1b, w2b = over_core(fc1_bias), over_core(fc1_weight), over_core(fc2_weight)

    mask_col, normed, q, k, v, probs, mixed, attended, hidden, inner = forward(
        heads, pad, patches, row_mask, rel_index, mask_token, ln1_gain, ln1_bias, query_bias,
        value_bias, rel_table.T, proj_bias, gamma1, ln2_gain, ln2_bias, qkv_weight, proj_weight,
    )
    inner1 = over_x(inner)
    weights = (fc1_bias, b1b, fc1_weight, w1b, fc2_weight, w2b)
    dbranch, dbranch1, cot1, acta0, actb0, dprea0, dpreb0, branch0, dinner0, sums0 = mlp(
        inner, weights, fc2_bias, (out_grad, out_grad1, row_mask, row_mask1, gamma2), True
    )
    acta1, actb1, dprea1, dpreb1, branch1, dinner1, sums1 = mlp(
        inner1, weights, fc2_bias, (dbranch1, cot1), False
    )
    dinner_in = over_x(dinner1)

    block = width // dp
    halves = dp // 2
    fence = over_core(sums1)
    fc1_out = pair_grad(inner, inner1, dpreb0, dpreb1, deps=(fence,))
    fc2_out = pair_grad(dbranch, dbranch1, actb0, actb1, deps=(fc1_out,))
    fc1_other, fc2_other = over_core(fc1_out), over_core(fc2_out)
    fc_send, fc_kept, mixed, normed = fc_keep(
        where, block, (inner, inner1, dprea0, dprea1, fc1_other),
        (dbranch, dbranch1, acta0, acta1, fc2_other), carry=(mixed, normed),
    )
    fc_met = over_low(fc_send)
    mixed1 = over_x(mixed)
    normed1 = over_x(normed)

    dhidden, datt, dqkv, send, dscores, sums_b = backward(
        heads, where, dinner0, dinner_in, hidden, attended, out_grad, mask_col, ln2_gain, gamma1,
        proj_weight, q, k, v, probs, deps=(fc_kept,),
    )
    met = over_x(send)

    def cross_high(parts):
        own, *sends = parts
        return (own, *[swap("dp", 2 * (at + 1))(part) for at, part in enumerate(sends)])

    patch_grad, sums_n = first_norm(
        patches, mask_col, mask_token, ln1_gain, dqkv, qkv_weight, dhidden,
        deps=(normed1, mixed1),
    )
    fc_parts = spread(where, fc_kept, fc_met, deps=(sums_n,))
    fc_seen = cross_high(fc_parts)

    late_args = (where, block, normed, normed1, mixed, mixed1, dqkv, met, datt)
    late_out, branch1_late = late_grad(*late_args, deps=(fc_parts[0],), carry=(branch1,))
    late_other = over_core(late_out)
    branch_in = over_x(branch1_late)
    late_send, late_kept = late_grad(*late_args, late_other)
    late_met = over_low(late_send)

    head_pad = 16
    ds = jnp.pad(jnp.transpose(dscores, (1, 0, 2)), ((0, 0), (0, head_pad - heads), (0, 0)))
    small = table_grad(
        where, rel_index, ds, sums_b, sums_n, sums0, sums1, entries, deps=(late_kept,)
    )
    small = small + over_core(small)
    small = small + over_x(small)
    fc1_weight_grad, fc2_weight_grad = gather_sum(fc_seen, F32, deps=(small,))

    *late_parts, small = spread(
        where, late_kept, late_met, deps=(fc1_weight_grad,), carry=(small,)
    )
    late_seen = cross_high(late_parts)
    small = small + over_low(small)
    late_own, small = gather_sum(late_seen, BF16, carry=(small,))

    bit = 2
    while bit < dp:
        small = small + swap("dp", bit)(small)
        bit *= 2

    layer_out = layer_end(rows, hidden, branch0, branch_in, gamma2)

    late_x = over_x(late_own)
    mine = jnp.stack([late_own, late_x])
    pair_core = over_core(mine)
    on_core = core_at > 0
    on_x = x_at > 0
    core0 = jnp.where(on_core, pair_core, mine)
    core1 = jnp.where(on_core, mine, pair_core)
    low0 = jnp.where(on_x, core0[1], core0[0])
    high0 = jnp.where(on_x, core0[0], core0[1])
    low1 = jnp.where(on_x, core1[1], core1[0])
    high1 = jnp.where(on_x, core1[0], core1[1])
    half = width // 2
    qkv_weight_grad = jnp.concatenate(
        [low0, low1[:, :half], high0, high1[:, :half]], axis=1
    ).astype(F32)
    proj_weight_grad = jnp.concatenate([low1[:, half:], high1[:, half:]], axis=1).astype(F32)

    rel_grad = small[:heads, :entries].T
    (ln2_gain_grad, ln2_bias_grad, gamma1_grad, proj_bias_grad, query_bias_grad, value_bias_grad,
     gamma2_grad, fc2_bias_grad, mask_token_grad, ln1_gain_grad, ln1_bias_grad) = [
        small[head_pad + at] for at in range(11)
    ]
    fc1_bias_grad = lax.dynamic_index_in_dim(small, head_pad + 11 + mp_at, 0, False)
    return (
        layer_out,
        patch_grad,
        mask_token_grad,
        ln1_gain_grad,
        ln1_bias_grad,
        qkv_weight_grad,
        query_bias_grad,
        value_bias_grad,
        rel_grad,
        proj_weight_grad,
        proj_bias_grad,
        gamma1_grad,
        ln2_gain_grad,
        ln2_bias_grad,
        fc1_weight_grad,
        fc1_bias_grad,
        fc2_weight_grad.T,
        fc2_bias_grad,
        gamma2_grad,
    )


def solution(mesh):
    rows3 = P(("dp", "mp"), None, None)
    placed = (
        (rows3, P(("dp", "mp"), None), rows3)
        + (P(),) * 13
        + (P(None, "mp"), P("mp"), P("mp", None), P(), P())
    )
    return jax.shard_map(
        functools.partial(on_device, mesh.shape["dp"]),
        mesh=mesh,
        in_specs=placed,
        out_specs=(
            rows3,
            rows3,
            P(),
            P(),
            P(),
            P("dp", None),
            P(),
            P(),
            P(),
            P("dp", None),
            P(),
            P(),
            P(),
            P(),
            P("dp", "mp"),
            P("mp"),
            P("mp", "dp"),
            P(),
            P(),
        ),
        check_vma=False,
    )
```

time: 247 us -> 143 us (0.58)
  waiting for transfers between devices: 115 us -> 35.1 us
  Pallas kernels: 78.7 us -> 53 us
  starting transfers between devices: 28.7 us -> 38.7 us
  local copies, waits for them, and re-layouts: 19.2 us -> 12.5 us
    ppermute x28 -> x30, waiting for transfers between devices: 115 us -> 35.1 us  [swap(): return lambda value: lax.ppermute(value, axis, pairs)]
    pallas_call x11 -> x16, Pallas kernels: 78.7 us -> 53 us  [call(): pl.pallas_call(inner, name=getattr(body, 'func', body).__name__, out_shap...]
    ppermute x28 -> x30, starting transfers between devices: 28.7 us -> 38.7 us  [swap(): return lambda value: lax.ppermute(value, axis, pairs)]
    unnamed x53 -> x45, local copies, waits for them, and re-layouts: 9.26 us -> 10.4 us
  transfers between devices with their start and end apart: 28 -> 30, of which waited for: 15 -> 12; matrix products, arithmetic and copies ran while one was open for 7% -> 3% of each run, Pallas kernels for 25% -> 31%
where the time goes in v2:
time: 143 us; the launch traced here: 142 us
  Pallas kernels  53 us (37%)
  starting transfers between devices  38.7 us (27%)
  waiting for transfers between devices  35.1 us (25%)
  local copies, waits for them, and re-layouts  12.5 us (9%)
  other arithmetic  1.98 us (1%)
    pallas_call x16, Pallas kernels, call(): pl.pallas_call(inner, name=getattr(body, 'func', body).__name__, out_shap...  53 us
    ppermute x30, starting transfers between devices, swap(): return lambda value: lax.ppermute(value, axis, pairs)  38.7 us
    ppermute x30, waiting for transfers between devices, swap(): return lambda value: lax.ppermute(value, axis, pairs)  35.1 us
    unnamed x45, local copies, waits for them, and re-layouts  10.4 us
  transfers between devices with their start and end apart: 30, of which 12 were waited for; matrix products, arithmetic and copies ran while one was open for 3% of the time, Pallas kernels for 31%

profile of v2, /device:TPU:0, one launch (start us, length us, event | category | flops | bytes accessed | tf_op | source)
XLA Modules:
  0.0 142.2 jit_solution(1161807176462803304)
XLA Ops:
  1.3 2.9 %collective-permute-start.4 = (s32[1,197]{1,0:T(1,128)}, s32[1,197]{1,0:T(1,128)S(1)}, u32[]{:S(2)}, u32[]{:S(2)}) collective-permute-start(s32[1,197]{1,0:T(1,128)} %refs_10_.3), channel_id=1, source_target_pairs={{0,2},{1,3},{2,0},{3,1},{4,6},{5,7},{6,4},{7,5},{8,10},{9,11},{10,... | collective-permute-start | bytes 2372 | tf_op jit(solution)/shard_map/ppermute | solution.py:728
  4.3 9.7 %forward_body.1 = (f32[208,128]{1,0:T(8,128)}, bf16[208,768]{1,0:T(8,128)(2,1)}, bf16[208,768]{1,0:T(8,128)(2,1)}, bf16[256,768]{1,0:T(8,128)(2,1)}, bf16[256,76...) custom-call(bf16[1,197,768]{2,1,0:T(8,128)(2,1)} %refs_0_.3, ...), custom_call_target="tpu_custom_call" | custom-call | flops 12000000000 | bytes 1000 | tf_op jit(solution)/shard_map/forward_body/pallas_call | solution.py:77
  14.0 2.0 %collective-permute-start.5 = (bf16[208,768]{1,0:T(8,128)(2,1)S(1)}, bf16[208,768]{1,0:T(8,128)(2,1)S(1)}, u32[]{:S(2)}, u32[]{:S(2)}) collective-permute-start(bf16[208,768]{1,0:T(8,128)(2,1)S(1)} %get-tuple-element.76.refs_0_.refs_1_), channel_id=1, source_target_pairs={{0,2},{1,3},{2,0},{3,1},{4,6},{5,7},{6,4},{7,5},{8,10},{9,11},{10,... | collective-permute-start | bytes 958472 | tf_op jit(solution)/shard_map/ppermute | solution.py:728
  16.6 4.4 %mlp_body.2 = (bf16[208,768]{1,0:T(8,128)(2,1)S(1)}, bf16[208,768]{1,0:T(8,128)(2,1)S(1)}, f32[208,768]{1,0:T(8,128)S(1)}, bf16[208,768]{1,0:T(8,128)(2,1)S(1)},...) custom-call(bf16[208,768]{1,0:T(8,128)(2,1)S(1)} %get-tuple-element., ...), custom_call_target="tpu_custom_call" | custom-call | flops 4000000000 | bytes 1000 | tf_op jit(solution)/shard_map/mlp_body/pallas_call | solution.py:77
  23.9 4.2 %mlp_body.3 = (bf16[208,768]{1,0:T(8,128)(2,1)S(1)}, bf16[208,768]{1,0:T(8,128)(2,1)S(1)}, bf16[208,768]{1,0:T(8,128)(2,1)S(1)}, bf16[208,768]{1,0:T(8,128)(2,1)...) custom-call(bf16[208,768]{1,0:T(8,128)(2,1)S(1)} %collective-permute-done.5.refs_0_.refs_1_.refs_2_, ...), custom_call_target="tpu_custom_call" | custom-call | flops 4000000000 | bytes 1000 | tf_op jit(solution)/shard_map/mlp_body/pallas_call | solution.py:77
  31.7 1.7 %collective-permute-start.11 = (bf16[208,768]{1,0:T(8,128)(2,1)}, bf16[208,768]{1,0:T(8,128)(2,1)}, u32[]{:S(2)}, u32[]{:S(2)}) collective-permute-start(bf16[208,768]{1,0:T(8,128)(2,1)} %get-tuple-element.95), channel_id=1, source_target_pairs={{0,2},{1,3},{2,0},{3,1},{4,6},{5,7},{6,4},{7,5},{8,10},{9,11},{10,... | collective-permute-start | bytes 958472 | tf_op jit(solution)/shard_map/ppermute | solution.py:728
  34.2 1.7 %collective-permute-done.7.refs_5_ = bf16[768,768]{1,0:T(8,128)(2,1)} collective-permute-done((bf16[768,768]{1,0:T(8,128)(2,1)S(1)}, bf16[768,768]{1,0:T(8,128)(2,1)}, u32[]{:S(2)}, u32[]{:S(2)}) %collective-permute-start.7) | collective-permute-done | bytes 1179680 | tf_op jit(solution)/shard_map/ppermute | solution.py:728
  41.7 3.2 %fc_keep_body.1 = (bf16[2,4,96,768]{3,2,1,0:T(8,128)(2,1)S(1)}, bf16[2,4,96,768]{3,2,1,0:T(8,128)(2,1)S(1)}, bf16[208,768]{1,0:T(8,128)(2,1)}, bf16[208,768]{1,0:T(8,128)(2,1)S(1)}) custom-call(s32[4]{0:T(128)S(1)} %pad_add_fusion.refs_0_, bf16[208,768]{1,0:T(8,128)(2,1)S(1)} %copy-done.3, ...), custom_call_target="tpu_custom_call", output_to_operand_aliasing={{2}: (11, {}), {3}: (12, {})} | custom-call | flops 1500000000 | bytes 1000 | tf_op jit(solution)/shard_map/fc_keep_body/pallas_call | solution.py:77
  44.9 1.8 %collective-permute-start.9 = (bf16[208,768]{1,0:T(8,128)(2,1)S(1)}, bf16[208,768]{1,0:T(8,128)(2,1)S(1)}, u32[]{:S(2)}, u32[]{:S(2)}) collective-permute-start(bf16[208,768]{1,0:T(8,128)(2,1)S(1)} %get-tuple-element.92.refs_1_), channel_id=1, source_target_pairs={{0,2},{1,3},{2,0},{3,1},{4,6},{5,7},{6,4},{7,5},{8,10},{9,11},{10,... | collective-permute-start | bytes 958472 | tf_op jit(solution)/shard_map/ppermute | solution.py:728
  47.0 1.8 %collective-permute-start.13 = (bf16[2,4,96,768]{3,2,1,0:T(8,128)(2,1)S(1)}, bf16[2,4,96,768]{3,2,1,0:T(8,128)(2,1)S(1)}, u32[]{:S(2)}, u32[]{:S(2)}) collective-permute-start(bf16[2,4,96,768]{3,2,1,0:T(8,128)(2,1)S(1)} %get-tuple-element.106), channel_id=1, source_target_pairs={{0,4},{4,0},{8,12},{12,8},{16,20},{20,16},{24,28},{28,24},{1,5},{5... | collective-permute-start | bytes 3538952 | tf_op jit(solution)/shard_map/ppermute | solution.py:728
  48.7 9.2 %backward_body.1 = (f32[208,768]{1,0:T(8,128)S(1)}, bf16[208,384]{1,0:T(8,128)(2,1)}, bf16[208,2304]{1,0:T(8,128)(2,1)}, bf16[208,1536]{1,0:T(8,128)(2,1)S(1)}, ...) custom-call(s32[4]{0:T(128)S(1)} %pad_add_fusion.refs_0_, f32[208,768]{1,0:T(8,128)S(1)} %copy-done.19, ...), custom_call_target="tpu_custom_call" | custom-call | flops 8999999488 | bytes 1000 | tf_op jit(solution)/shard_map/backward_body/pallas_call | solution.py:77
  57.9 1.5 %collective-permute-start.12 = (bf16[208,1536]{1,0:T(8,128)(2,1)S(1)}, bf16[208,1536]{1,0:T(8,128)(2,1)S(1)}, u32[]{:S(2)}, u32[]{:S(2)}) collective-permute-start(bf16[208,1536]{1,0:T(8,128)(2,1)S(1)} %get-tuple-element.104), channel_id=1, source_target_pairs={{0,2},{1,3},{2,0},{3,1},{4,6},{5,7},{6,4},{7,5},{8,10},{9,11},{10,... | collective-permute-start | bytes 1916936 | tf_op jit(solution)/shard_map/ppermute | solution.py:728
  59.4 2.7 %collective-permute-done.10.refs_8_.refs_4_ = bf16[208,768]{1,0:T(8,128)(2,1)S(1)} collective-permute-done((bf16[208,768]{1,0:T(8,128)(2,1)}, bf16[208,768]{1,0:T(8,128)(2,1)S(1)}, u32[]{:S(2)}, u32[]{:S(2)}) %collective-permute-start.10) | collective-permute-done | bytes 319520 | tf_op jit(solution)/shard_map/ppermute | solution.py:728
  62.2 4.9 %first_norm_body.1 = (f32[1,197,768]{2,1,0:T(8,128)}, f32[8,768]{1,0:T(8,128)S(1)}) custom-call(bf16[1,197,768]{2,1,0:T(8,128)(2,1)} %refs_0_.3, f32[208,128]{1,0:T(8,128)} %get-tuple-element.97.refs_6_.refs_1_, f32[768]{0:T(1024)} %refs_2_.3, f32[768]{0:T(1024)} %refs_3_.8, bf16[208,2304]{1,0:T(8,128)(2,1)} %get-tuple-element.103.refs_4_.refs_5_, ...), custom_call_target="tpu_custom_call" | custom-call | flops 4000000000 | bytes 1000 | tf_op jit(solution)/shard_map/first_norm_body/pallas_call | solution.py:77
  67.0 7.5 %collective-permute-done.13.refs_2_ = bf16[2,4,96,768]{3,2,1,0:T(8,128)(2,1)S(1)} collective-permute-done((bf16[2,4,96,768]{3,2,1,0:T(8,128)(2,1)S(1)}, bf16[2,4,96,768]{3,2,1,0:T(8,128)(2,1)S(1)}, u32[]{:S(2)}, u32[]{:S(2)}) %collective-permute-start.13) | collective-permute-done | bytes 1179680 | tf_op jit(solution)/shard_map/ppermute | solution.py:728
  75.5 2.4 %late_grad_body.2 = (bf16[768,768]{1,0:T(8,128)(2,1)S(1)}, bf16[208,768]{1,0:T(8,128)(2,1)S(1)}) custom-call(s32[4]{0:T(128)S(1)} %pad_add_fusion.refs_0_, bf16[208,768]{1,0:T(8,128)(2,1)} %copy-done.1, bf16[208,768]{1,0:T(8,128)(2,1)S(1)} %collective-permute-done.9.refs_7_.refs_2_, ...), custom_call_target="tpu_custom_call", output_to_operand_aliasing={{1}: (9, {})} | custom-call | flops 2600000000 | bytes 1000 | tf_op jit(solution)/shard_map/late_grad_body/pallas_call | solution.py:77
  78.7 1.8 %collective-permute-start.17 = (bf16[2,96,768]{2,1,0:T(8,128)(2,1)S(1)}, bf16[2,96,768]{2,1,0:T(8,128)(2,1)S(1)}, u32[]{:S(2)}, u32[]{:S(2)}) collective-permute-start(bf16[2,96,768]{2,1,0:T(8,128)(2,1)S(1)} %get-tuple-element.116), channel_id=1, source_target_pairs={{0,8},{4,12},{8,0},{12,4},{16,24},{20,28},{24,16},{28,20},{1,9},{5... | collective-permute-start | bytes 884744 | tf_op jit(solution)/shard_map/ppermute | solution.py:728
  80.6 2.6 %collective-permute-start.18 = (bf16[2,96,768]{2,1,0:T(8,128)(2,1)S(1)}, bf16[2,96,768]{2,1,0:T(8,128)(2,1)S(1)}, u32[]{:S(2)}, u32[]{:S(2)}) collective-permute-start(bf16[2,96,768]{2,1,0:T(8,128)(2,1)S(1)} %get-tuple-element.117), channel_id=1, source_target_pairs={{0,16},{4,20},{8,24},{12,28},{16,0},{20,4},{24,8},{28,12},{1,17},{... | collective-permute-start | bytes 884744 | tf_op jit(solution)/shard_map/ppermute | solution.py:728
  83.2 2.5 %late_grad_body.3 = (bf16[1,4,96,768]{3,2,1,0:T(8,128)(2,1)S(1)}, bf16[1,4,96,768]{3,2,1,0:T(8,128)(2,1)S(1)}) custom-call(s32[4]{0:T(128)S(1)} %pad_add_fusion.refs_0_, bf16[208,768]{1,0:T(8,128)(2,1)} %copy-done.1, bf16[208,768]{1,0:T(8,128)(2,1)S(1)} %collective-permute-done.9.refs_7_.refs_2_, bf16[208,768]{1,0:T(8,128)(2,1)} %get-tuple-element.93.refs_3_, ...), custom_call_target="tpu_custom_call" | custom-call | flops 2600000000 | bytes 1000 | tf_op jit(solution)/shard_map/late_grad_body/pallas_call | solution.py:77
  85.7 1.8 %collective-permute-start.16 = (bf16[1,4,96,768]{3,2,1,0:T(8,128)(2,1)S(1)}, bf16[1,4,96,768]{3,2,1,0:T(8,128)(2,1)S(1)}, u32[]{:S(2)}, u32[]{:S(2)}) collective-permute-start(bf16[1,4,96,768]{3,2,1,0:T(8,128)(2,1)S(1)} %get-tuple-element.115), channel_id=1, source_target_pairs={{0,4},{4,0},{8,12},{12,8},{16,20},{20,16},{24,28},{28,24},{1,5},{5... | collective-permute-start | bytes 1769480 | tf_op jit(solution)/shard_map/ppermute | solution.py:728
  87.5 6.3 %table_grad_body.1 = f32[32,768]{1,0:T(8,128)S(1)} custom-call(s32[4]{0:T(128)S(1)} %pad_add_fusion.refs_0_, s32[197,197]{1,0:T(8,128)} %refs_1_.7, bf16[208,16,256]{2,1,0:T(8,128)(2,1)S(1)} %pad.4.refs_2_, f32[8,768]{1,0:T(8,128)S(1)} %get-tuple-element.120.refs_3_, f32[8,768]{1,0:T(8,128)S(1)} %get-tuple-element.108.refs_3_.refs_4_, ...), custom_call_target="tpu_custom_call" | custom-call | flops 6000000000 | bytes 1000 | tf_op jit(solution)/shard_map/table_grad_body/pallas_call | solution.py:77
  95.1 1.5 %collective-permute-start.21 = (f32[32,768]{1,0:T(8,128)S(1)}, f32[32,768]{1,0:T(8,128)S(1)}, u32[]{:S(2)}, u32[]{:S(2)}) collective-permute-start(f32[32,768]{1,0:T(8,128)S(1)} %add.34), channel_id=1, source_target_pairs={{0,2},{1,3},{2,0},{3,1},{4,6},{5,7},{6,4},{7,5},{8,10},{9,11},{10,... | collective-permute-start | bytes 294920 | tf_op jit(solution)/shard_map/ppermute | solution.py:728
  96.7 3.4 %collective-permute-done.21 = f32[32,768]{1,0:T(8,128)S(1)} collective-permute-done((f32[32,768]{1,0:T(8,128)S(1)}, f32[32,768]{1,0:T(8,128)S(1)}, u32[]{:S(2)}, u32[]{:S(2)}) %collective-permute-start.21) | collective-permute-done | bytes 98336 | tf_op jit(solution)/shard_map/ppermute | solution.py:728
  101.6 2.4 %collective-permute-done.18.refs_2_ = bf16[2,96,768]{2,1,0:T(8,128)(2,1)S(1)} collective-permute-done((bf16[2,96,768]{2,1,0:T(8,128)(2,1)S(1)}, bf16[2,96,768]{2,1,0:T(8,128)(2,1)S(1)}, u32[]{:S(2)}, u32[]{:S(2)}) %collective-permute-start.18) | collective-permute-done | bytes 294944 | tf_op jit(solution)/shard_map/ppermute | solution.py:728
  106.5 6.2 %collective-permute-start.22 = (bf16[1,96,768]{2,1,0:T(8,128)(2,1)S(1)}, bf16[1,96,768]{2,1,0:T(8,128)(2,1)S(1)}, u32[]{:S(2)}, u32[]{:S(2)}) collective-permute-start(bf16[1,96,768]{2,1,0:T(8,128)(2,1)S(1)} %get-tuple-element.124), channel_id=1, source_target_pairs={{0,8},{4,12},{8,0},{12,4},{16,24},{20,28},{24,16},{28,20},{1,9},{5... | collective-permute-start | bytes 442376 | tf_op jit(solution)/shard_map/ppermute | solution.py:728
  115.2 1.5 %collective-permute-start.25 = (f32[32,768]{1,0:T(8,128)S(1)}, f32[32,768]{1,0:T(8,128)S(1)}, u32[]{:S(2)}, u32[]{:S(2)}) collective-permute-start(f32[32,768]{1,0:T(8,128)S(1)} %get-tuple-element.127), channel_id=1, source_target_pairs={{0,4},{4,0},{8,12},{12,8},{16,20},{20,16},{24,28},{28,24},{1,5},{5... | collective-permute-start | bytes 294920 | tf_op jit(solution)/shard_map/ppermute | solution.py:728
  118.2 1.7 %collective-permute-done.25 = f32[32,768]{1,0:T(8,128)S(1)} collective-permute-done((f32[32,768]{1,0:T(8,128)S(1)}, f32[32,768]{1,0:T(8,128)S(1)}, u32[]{:S(2)}, u32[]{:S(2)}) %collective-permute-start.25) | collective-permute-done | bytes 98336 | tf_op jit(solution)/shard_map/ppermute | solution.py:728
  119.9 6.6 %collective-permute-done.23.refs_2_ = bf16[1,96,768]{2,1,0:T(8,128)(2,1)S(1)} collective-permute-done((bf16[1,96,768]{2,1,0:T(8,128)(2,1)S(1)}, bf16[1,96,768]{2,1,0:T(8,128)(2,1)S(1)}, u32[]{:S(2)}, u32[]{:S(2)}) %collective-permute-start.23) | collective-permute-done | bytes 147488 | tf_op jit(solution)/shard_map/ppermute | solution.py:728
  126.6 2.2 %collective-permute-start.26 = (f32[32,768]{1,0:T(8,128)S(1)}, f32[32,768]{1,0:T(8,128)S(1)}, u32[]{:S(2)}, u32[]{:S(2)}) collective-permute-start(f32[32,768]{1,0:T(8,128)S(1)} %get-tuple-element.128), channel_id=1, source_target_pairs={{0,8},{4,12},{8,0},{12,4},{16,24},{20,28},{24,16},{28,20},{1,9},{5... | collective-permute-start | bytes 294920 | tf_op jit(solution)/shard_map/ppermute | solution.py:728
  130.2 2.1 %layer_end_body.1 = bf16[1,197,768]{2,1,0:T(8,128)(2,1)} custom-call(f32[208,768]{1,0:T(8,128)} %get-tuple-element.75.refs_3_.refs_0_, f32[208,768]{1,0:T(8,128)} %get-tuple-element.77.refs_1_, bf16[208,768]{1,0:T(8,128)(2,1)S(1)} %collective-permute-done.14.refs_2_, f32[768]{0:T(1024)} %refs_3_.9), custom_call_target="tpu_custom_call" | custom-call | flops 2000000000 | bytes 1000 | tf_op jit(solution)/shard_map/layer_end_body/pallas_call | solution.py:77
  132.4 2.1 %collective-permute-start.27 = (f32[32,768]{1,0:T(8,128)S(1)}, f32[32,768]{1,0:T(8,128)S(1)}, u32[]{:S(2)}, u32[]{:S(2)}) collective-permute-start(f32[32,768]{1,0:T(8,128)S(1)} %add.37), channel_id=1, source_target_pairs={{0,16},{4,20},{8,24},{12,28},{16,0},{20,4},{24,8},{28,12},{1,17},{... | collective-permute-start | bytes 294920 | tf_op jit(solution)/shard_map/ppermute | solution.py:728
  134.5 4.5 %collective-permute-done.27 = f32[32,768]{1,0:T(8,128)S(1)} collective-permute-done((f32[32,768]{1,0:T(8,128)S(1)}, f32[32,768]{1,0:T(8,128)S(1)}, u32[]{:S(2)}, u32[]{:S(2)}) %collective-permute-start.27) | collective-permute-done | bytes 98336 | tf_op jit(solution)/shard_map/ppermute | solution.py:728
  (106 shorter events, 30.5 us)
Async XLA Ops:
  0.7 15.4 %collective-permute-start.1 = (bf16[768,768]{1,0:T(8,128)(2,1)}, bf16[768,768]{1,0:T(8,128)(2,1)S(1)}, u32[]{:S(2)}, u32[]{:S(2)}) collective-permute-start(bf16[768,768]{1,0:T(8,128)(2,1)} %refs_3_.7), channel_id=1, source_target_pairs={{0,1},{1,0},{2,3},{3,2},{4,5},{5,4},{6,7},{7,6},{8,9},{9,8},{10,11... | collective-permute-start | bytes 3538952 | tf_op jit(solution)/shard_map/ppermute | solution.py:728
  1.2 14.8 %collective-permute-start.2 = (bf16[768,768]{1,0:T(8,128)(2,1)}, bf16[768,768]{1,0:T(8,128)(2,1)S(1)}, u32[]{:S(2)}, u32[]{:S(2)}) collective-permute-start(bf16[768,768]{1,0:T(8,128)(2,1)} %refs_5_.7), channel_id=1, source_target_pairs={{0,1},{1,0},{2,3},{3,2},{4,5},{5,4},{6,7},{7,6},{8,9},{9,8},{10,11... | collective-permute-start | bytes 3538952 | tf_op jit(solution)/shard_map/ppermute | solution.py:728
  1.3 12.7 %collective-permute-start.4 = (s32[1,197]{1,0:T(1,128)}, s32[1,197]{1,0:T(1,128)S(1)}, u32[]{:S(2)}, u32[]{:S(2)}) collective-permute-start(s32[1,197]{1,0:T(1,128)} %refs_10_.3), channel_id=1, source_target_pairs={{0,2},{1,3},{2,0},{3,1},{4,6},{5,7},{6,4},{7,5},{8,10},{9,11},{10,... | collective-permute-start | bytes 2372 | tf_op jit(solution)/shard_map/ppermute | solution.py:728
  4.2 11.8 %collective-permute-start = (bf16[768]{0:T(1024)(128)(2,1)}, bf16[768]{0:T(1024)(128)(2,1)S(1)}, u32[]{:S(2)}, u32[]{:S(2)}) collective-permute-start(bf16[768]{0:T(1024)(128)(2,1)} %refs_1_.6), channel_id=1, source_target_pairs={{0,1},{1,0},{2,3},{3,2},{4,5},{5,4},{6,7},{7,6},{8,9},{9,8},{10,11... | collective-permute-start | bytes 4616 | tf_op jit(solution)/shard_map/ppermute | solution.py:728
  4.2 11.8 %collective-permute-start.3 = (bf16[1,197,768]{2,1,0:T(8,128)(2,1)}, bf16[1,197,768]{2,1,0:T(8,128)(2,1)S(1)}, u32[]{:S(2)}, u32[]{:S(2)}) collective-permute-start(bf16[1,197,768]{2,1,0:T(8,128)(2,1)} %refs_5_.8), channel_id=1, source_target_pairs={{0,2},{1,3},{2,0},{3,1},{4,6},{5,7},{6,4},{7,5},{8,10},{9,11},{10,... | collective-permute-start | bytes 907784 | tf_op jit(solution)/shard_map/ppermute | solution.py:728
  14.0 15.5 %copy-start.2 = (bf16[208,768]{1,0:T(8,128)(2,1)}, bf16[208,768]{1,0:T(8,128)(2,1)S(1)}, u32[]{:S(2)}) copy-start(bf16[208,768]{1,0:T(8,128)(2,1)S(1)} %get-tuple-element.76.refs_0_.refs_1_) | copy-start | bytes 958468
  14.0 10.0 %collective-permute-start.5 = (bf16[208,768]{1,0:T(8,128)(2,1)S(1)}, bf16[208,768]{1,0:T(8,128)(2,1)S(1)}, u32[]{:S(2)}, u32[]{:S(2)}) collective-permute-start(bf16[208,768]{1,0:T(8,128)(2,1)S(1)} %get-tuple-element.76.refs_0_.refs_1_), channel_id=1, source_target_pairs={{0,2},{1,3},{2,0},{3,1},{4,6},{5,7},{6,4},{7,5},{8,10},{9,11},{10,... | collective-permute-start | bytes 958472 | tf_op jit(solution)/shard_map/ppermute | solution.py:728
  28.2 1.3 collective-permute-start.6
  31.1 3.0 %collective-permute-start.8 = (bf16[768,768]{1,0:T(8,128)(2,1)S(1)}, bf16[768,768]{1,0:T(8,128)(2,1)}, u32[]{:S(2)}, u32[]{:S(2)}) collective-permute-start(bf16[768,768]{1,0:T(8,128)(2,1)S(1)} %pair_grad_body.3), channel_id=1, source_target_pairs={{0,1},{1,0},{2,3},{3,2},{4,5},{5,4},{6,7},{7,6},{8,9},{9,8},{10,11... | collective-permute-start | bytes 3538952 | tf_op jit(solution)/shard_map/ppermute | solution.py:728
  31.4 4.5 %collective-permute-start.7 = (bf16[768,768]{1,0:T(8,128)(2,1)S(1)}, bf16[768,768]{1,0:T(8,128)(2,1)}, u32[]{:S(2)}, u32[]{:S(2)}) collective-permute-start(bf16[768,768]{1,0:T(8,128)(2,1)S(1)} %pair_grad_body.2.refs_4_), channel_id=1, source_target_pairs={{0,1},{1,0},{2,3},{3,2},{4,5},{5,4},{6,7},{7,6},{8,9},{9,8},{10,11... | collective-permute-start | bytes 3538952 | tf_op jit(solution)/shard_map/ppermute | solution.py:728
  31.7 17.0 %collective-permute-start.11 = (bf16[208,768]{1,0:T(8,128)(2,1)}, bf16[208,768]{1,0:T(8,128)(2,1)}, u32[]{:S(2)}, u32[]{:S(2)}) collective-permute-start(bf16[208,768]{1,0:T(8,128)(2,1)} %get-tuple-element.95), channel_id=1, source_target_pairs={{0,2},{1,3},{2,0},{3,1},{4,6},{5,7},{6,4},{7,5},{8,10},{9,11},{10,... | collective-permute-start | bytes 958472 | tf_op jit(solution)/shard_map/ppermute | solution.py:728
  44.9 13.1 %copy-start.1 = (bf16[208,768]{1,0:T(8,128)(2,1)}, bf16[208,768]{1,0:T(8,128)(2,1)S(1)}, u32[]{:S(2)}) copy-start(bf16[208,768]{1,0:T(8,128)(2,1)S(1)} %get-tuple-element.92.refs_1_) | copy-start | bytes 958468
  44.9 14.5 %collective-permute-start.9 = (bf16[208,768]{1,0:T(8,128)(2,1)S(1)}, bf16[208,768]{1,0:T(8,128)(2,1)S(1)}, u32[]{:S(2)}, u32[]{:S(2)}) collective-permute-start(bf16[208,768]{1,0:T(8,128)(2,1)S(1)} %get-tuple-element.92.refs_1_), channel_id=1, source_target_pairs={{0,2},{1,3},{2,0},{3,1},{4,6},{5,7},{6,4},{7,5},{8,10},{9,11},{10,... | collective-permute-start | bytes 958472 | tf_op jit(solution)/shard_map/ppermute | solution.py:728
  46.7 15.5 %collective-permute-start.10 = (bf16[208,768]{1,0:T(8,128)(2,1)}, bf16[208,768]{1,0:T(8,128)(2,1)S(1)}, u32[]{:S(2)}, u32[]{:S(2)}) collective-permute-start(bf16[208,768]{1,0:T(8,128)(2,1)} %get-tuple-element.93.refs_3_), channel_id=1, source_target_pairs={{0,2},{1,3},{2,0},{3,1},{4,6},{5,7},{6,4},{7,5},{8,10},{9,11},{10,... | collective-permute-start | bytes 958472 | tf_op jit(solution)/shard_map/ppermute | solution.py:728
  47.0 27.5 %collective-permute-start.13 = (bf16[2,4,96,768]{3,2,1,0:T(8,128)(2,1)S(1)}, bf16[2,4,96,768]{3,2,1,0:T(8,128)(2,1)S(1)}, u32[]{:S(2)}, u32[]{:S(2)}) collective-permute-start(bf16[2,4,96,768]{3,2,1,0:T(8,128)(2,1)S(1)} %get-tuple-element.106), channel_id=1, source_target_pairs={{0,4},{4,0},{8,12},{12,8},{16,20},{20,16},{24,28},{28,24},{1,5},{5... | collective-permute-start | bytes 3538952 | tf_op jit(solution)/shard_map/ppermute | solution.py:728
  57.9 17.4 %collective-permute-start.12 = (bf16[208,1536]{1,0:T(8,128)(2,1)S(1)}, bf16[208,1536]{1,0:T(8,128)(2,1)S(1)}, u32[]{:S(2)}, u32[]{:S(2)}) collective-permute-start(bf16[208,1536]{1,0:T(8,128)(2,1)S(1)} %get-tuple-element.104), channel_id=1, source_target_pairs={{0,2},{1,3},{2,0},{3,1},{4,6},{5,7},{6,4},{7,5},{8,10},{9,11},{10,... | collective-permute-start | bytes 1916936 | tf_op jit(solution)/shard_map/ppermute | solution.py:728
  77.9 5.2 %collective-permute-start.15 = (bf16[768,768]{1,0:T(8,128)(2,1)S(1)}, bf16[768,768]{1,0:T(8,128)(2,1)S(1)}, u32[]{:S(2)}, u32[]{:S(2)}) collective-permute-start(bf16[768,768]{1,0:T(8,128)(2,1)S(1)} %get-tuple-element.113), channel_id=1, source_target_pairs={{0,1},{1,0},{2,3},{3,2},{4,5},{5,4},{6,7},{7,6},{8,9},{9,8},{10,11... | collective-permute-start | bytes 3538952 | tf_op jit(solution)/shard_map/ppermute | solution.py:728
  78.7 22.8 %collective-permute-start.17 = (bf16[2,96,768]{2,1,0:T(8,128)(2,1)S(1)}, bf16[2,96,768]{2,1,0:T(8,128)(2,1)S(1)}, u32[]{:S(2)}, u32[]{:S(2)}) collective-permute-start(bf16[2,96,768]{2,1,0:T(8,128)(2,1)S(1)} %get-tuple-element.116), channel_id=1, source_target_pairs={{0,8},{4,12},{8,0},{12,4},{16,24},{20,28},{24,16},{28,20},{1,9},{5... | collective-permute-start | bytes 884744 | tf_op jit(solution)/shard_map/ppermute | solution.py:728
  80.6 23.4 %collective-permute-start.18 = (bf16[2,96,768]{2,1,0:T(8,128)(2,1)S(1)}, bf16[2,96,768]{2,1,0:T(8,128)(2,1)S(1)}, u32[]{:S(2)}, u32[]{:S(2)}) collective-permute-start(bf16[2,96,768]{2,1,0:T(8,128)(2,1)S(1)} %get-tuple-element.117), channel_id=1, source_target_pairs={{0,16},{4,20},{8,24},{12,28},{16,0},{20,4},{24,8},{28,12},{1,17},{... | collective-permute-start | bytes 884744 | tf_op jit(solution)/shard_map/ppermute | solution.py:728
  83.1 20.8 %collective-permute-start.19 = (bf16[2,96,768]{2,1,0:T(8,128)(2,1)S(1)}, bf16[2,96,768]{2,1,0:T(8,128)(2,1)S(1)}, u32[]{:S(2)}, u32[]{:S(2)}) collective-permute-start(bf16[2,96,768]{2,1,0:T(8,128)(2,1)S(1)} %get-tuple-element.118), channel_id=1, source_target_pairs={{0,24},{4,28},{8,16},{12,20},{16,8},{20,12},{24,0},{28,4},{1,25},{... | collective-permute-start | bytes 884744 | tf_op jit(solution)/shard_map/ppermute | solution.py:728
  85.7 19.2 %collective-permute-start.16 = (bf16[1,4,96,768]{3,2,1,0:T(8,128)(2,1)S(1)}, bf16[1,4,96,768]{3,2,1,0:T(8,128)(2,1)S(1)}, u32[]{:S(2)}, u32[]{:S(2)}) collective-permute-start(bf16[1,4,96,768]{3,2,1,0:T(8,128)(2,1)S(1)} %get-tuple-element.115), channel_id=1, source_target_pairs={{0,4},{4,0},{8,12},{12,8},{16,20},{20,16},{24,28},{28,24},{1,5},{5... | collective-permute-start | bytes 1769480 | tf_op jit(solution)/shard_map/ppermute | solution.py:728
  93.8 1.4 collective-permute-start.20
  95.1 4.9 %collective-permute-start.21 = (f32[32,768]{1,0:T(8,128)S(1)}, f32[32,768]{1,0:T(8,128)S(1)}, u32[]{:S(2)}, u32[]{:S(2)}) collective-permute-start(f32[32,768]{1,0:T(8,128)S(1)} %add.34), channel_id=1, source_target_pairs={{0,2},{1,3},{2,0},{3,1},{4,6},{5,7},{6,4},{7,5},{8,10},{9,11},{10,... | collective-permute-start | bytes 294920 | tf_op jit(solution)/shard_map/ppermute | solution.py:728
  100.1 30.2 %collective-permute-start.14 = (bf16[208,768]{1,0:T(8,128)(2,1)S(1)}, bf16[208,768]{1,0:T(8,128)(2,1)S(1)}, u32[]{:S(2)}, u32[]{:S(2)}) collective-permute-start(bf16[208,768]{1,0:T(8,128)(2,1)S(1)} %get-tuple-element.111), channel_id=1, source_target_pairs={{0,2},{1,3},{2,0},{3,1},{4,6},{5,7},{6,4},{7,5},{8,10},{9,11},{10,... | collective-permute-start | bytes 958472 | tf_op jit(solution)/shard_map/ppermute | solution.py:728
  106.5 13.3 %collective-permute-start.22 = (bf16[1,96,768]{2,1,0:T(8,128)(2,1)S(1)}, bf16[1,96,768]{2,1,0:T(8,128)(2,1)S(1)}, u32[]{:S(2)}, u32[]{:S(2)}) collective-permute-start(bf16[1,96,768]{2,1,0:T(8,128)(2,1)S(1)} %get-tuple-element.124), channel_id=1, source_target_pairs={{0,8},{4,12},{8,0},{12,4},{16,24},{20,28},{24,16},{28,20},{1,9},{5... | collective-permute-start | bytes 442376 | tf_op jit(solution)/shard_map/ppermute | solution.py:728
  112.8 13.7 %collective-permute-start.23 = (bf16[1,96,768]{2,1,0:T(8,128)(2,1)S(1)}, bf16[1,96,768]{2,1,0:T(8,128)(2,1)S(1)}, u32[]{:S(2)}, u32[]{:S(2)}) collective-permute-start(bf16[1,96,768]{2,1,0:T(8,128)(2,1)S(1)} %get-tuple-element.125), channel_id=1, source_target_pairs={{0,16},{4,20},{8,24},{12,28},{16,0},{20,4},{24,8},{28,12},{1,17},{... | collective-permute-start | bytes 442376 | tf_op jit(solution)/shard_map/ppermute | solution.py:728
  113.8 12.6 %collective-permute-start.24 = (bf16[1,96,768]{2,1,0:T(8,128)(2,1)S(1)}, bf16[1,96,768]{2,1,0:T(8,128)(2,1)S(1)}, u32[]{:S(2)}, u32[]{:S(2)}) collective-permute-start(bf16[1,96,768]{2,1,0:T(8,128)(2,1)S(1)} %get-tuple-element.126), channel_id=1, source_target_pairs={{0,24},{4,28},{8,16},{12,20},{16,8},{20,12},{24,0},{28,4},{1,25},{... | collective-permute-start | bytes 442376 | tf_op jit(solution)/shard_map/ppermute | solution.py:728
  115.2 4.6 %collective-permute-start.25 = (f32[32,768]{1,0:T(8,128)S(1)}, f32[32,768]{1,0:T(8,128)S(1)}, u32[]{:S(2)}, u32[]{:S(2)}) collective-permute-start(f32[32,768]{1,0:T(8,128)S(1)} %get-tuple-element.127), channel_id=1, source_target_pairs={{0,4},{4,0},{8,12},{12,8},{16,20},{20,16},{24,28},{28,24},{1,5},{5... | collective-permute-start | bytes 294920 | tf_op jit(solution)/shard_map/ppermute | solution.py:728
  126.6 5.8 %collective-permute-start.26 = (f32[32,768]{1,0:T(8,128)S(1)}, f32[32,768]{1,0:T(8,128)S(1)}, u32[]{:S(2)}, u32[]{:S(2)}) collective-permute-start(f32[32,768]{1,0:T(8,128)S(1)} %get-tuple-element.128), channel_id=1, source_target_pairs={{0,8},{4,12},{8,0},{12,4},{16,24},{20,28},{24,16},{28,20},{1,9},{5... | collective-permute-start | bytes 294920 | tf_op jit(solution)/shard_map/ppermute | solution.py:728
  128.8 5.7 %collective-permute-start.28 = (bf16[96,768]{1,0:T(8,128)(2,1)S(1)}, bf16[96,768]{1,0:T(8,128)(2,1)S(1)}, u32[]{:S(2)}, u32[]{:S(2)}) collective-permute-start(bf16[96,768]{1,0:T(8,128)(2,1)S(1)} %get-tuple-element.129), channel_id=1, source_target_pairs={{0,2},{1,3},{2,0},{3,1},{4,6},{5,7},{6,4},{7,5},{8,10},{9,11},{10,... | collective-permute-start | bytes 442376 | tf_op jit(solution)/shard_map/ppermute | solution.py:728
  132.4 6.6 %collective-permute-start.27 = (f32[32,768]{1,0:T(8,128)S(1)}, f32[32,768]{1,0:T(8,128)S(1)}, u32[]{:S(2)}, u32[]{:S(2)}) collective-permute-start(f32[32,768]{1,0:T(8,128)S(1)} %add.37), channel_id=1, source_target_pairs={{0,16},{4,20},{8,24},{12,28},{16,0},{20,4},{24,8},{28,12},{1,17},{... | collective-permute-start | bytes 294920 | tf_op jit(solution)/shard_map/ppermute | solution.py:728
  134.5 5.9 %collective-permute-start.29 = (bf16[2,96,768]{2,1,0:T(8,128)(2,1)S(1)}, bf16[2,96,768]{2,1,0:T(8,128)(2,1)S(1)}, u32[]{:S(2)}, u32[]{:S(2)}) collective-permute-start(bf16[2,96,768]{2,1,0:T(8,128)(2,1)S(1)} %pad_maximum_fusion), channel_id=1, source_target_pairs={{0,1},{1,0},{2,3},{3,2},{4,5},{5,4},{6,7},{7,6},{8,9},{9,8},{10,11... | collective-permute-start | bytes 884744 | tf_op jit(solution)/shard_map/ppermute | solution.py:728
  (20 other events, 73.4 us)

commit v3 on v2

v3 whole, which is shorter than its diff:
```python
import functools

import jax
import jax.numpy as jnp
from jax import lax
from jax.experimental import pallas as pl
from jax.experimental.pallas import tpu as pltpu
from jax.sharding import PartitionSpec as P

F32 = jnp.float32
BF16 = jnp.bfloat16
EPS = 1e-06
LANES = 128
SCALE = 1
UNROLL_F = 6
UNROLL_B = 6
VMEM_LIMIT = 16 * 1024 * 1024


def round_up(value, step):
    return -(-value // step) * step


def dot_nn(left, right):
    return lax.dot_general(left, right, (((1,), (0,)), ((), ())), preferred_element_type=F32)


def dot_nt(left, right):
    return lax.dot_general(left, right, (((1,), (1,)), ((), ())), preferred_element_type=F32)


def dot_tn(left, right):
    return lax.dot_general(left, right, (((0,), (0,)), ((), ())), preferred_element_type=F32)


def row_of(ref):
    return ref[...].reshape(1, ref.shape[0])


def norm_stats(values):
    middle = jnp.mean(values, axis=-1, keepdims=True)
    centred = values - middle
    spread = jnp.mean(centred * centred, axis=-1, keepdims=True)
    root = lax.rsqrt(spread + EPS)
    return centred * root, root


def norm_back(d_out, xhat, root, gain):
    t = d_out * gain
    mean_t = jnp.mean(t, axis=-1, keepdims=True)
    mean_tx = jnp.mean(t * xhat, axis=-1, keepdims=True)
    return root * (t - mean_t - xhat * mean_tx)


SPACES = {
    "h": (pltpu.HBM, pltpu.VMEM),
    "v": (None, pltpu.VMEM),
    "s": (None, pltpu.SMEM),
    "a": (pltpu.HBM, pl.ANY),
}


def call(body, outs, kinds, values, scratch=(), cost=1, deps=(), carry=()):
    specs, given = [], []
    for kind, value in zip(kinds, values, strict=True):
        keep, space = SPACES[kind]
        specs.append(pl.BlockSpec(memory_space=space))
        given.append(value if keep is None else pltpu.with_memory_space_constraint(value, keep))
    outs = outs if isinstance(outs, tuple) else (outs,)
    n_in, n_more, n_out = len(given), len(deps) + len(carry), len(outs)

    def inner(*refs):
        rest = refs[n_in + n_more :]
        rest[n_out][...] = jnp.zeros_like(rest[n_out])
        body(*refs[:n_in], *rest[:n_out], *rest[n_out + 1 + len(carry) :])

    anywhere = pl.BlockSpec(memory_space=pl.ANY)
    whole = pl.BlockSpec(memory_space=pltpu.VMEM)
    in_hbm = [value.dtype == BF16 and len(value.shape) == 2 for value in carry]
    out = pl.pallas_call(
        inner,
        name=getattr(body, "func", body).__name__,
        out_shape=outs
        + (pltpu.VMEM((8, LANES), F32),)
        + tuple(
            (pltpu.HBM if pinned else jax.ShapeDtypeStruct)(c.shape, c.dtype)
            for pinned, c in zip(in_hbm, carry)
        ),
        in_specs=specs + [anywhere] * n_more,
        out_specs=(whole,) * (n_out + 1) + (anywhere,) * len(carry),
        input_output_aliases={n_in + len(deps) + at: n_out + 1 + at for at in range(len(carry))},
        scratch_shapes=list(scratch),
        compiler_params=pltpu.CompilerParams(vmem_limit_bytes=VMEM_LIMIT),
        cost_estimate=pl.CostEstimate(
            flops=int(cost * SCALE * 10**9), bytes_accessed=1000, transcendentals=0
        ),
    )(
        *given,
        *deps,
        *(
            pltpu.with_memory_space_constraint(c, pltpu.HBM) if pinned else c
            for pinned, c in zip(in_hbm, carry)
        ),
    )
    results = out[:n_out] + out[n_out + 1 :]
    return (results if len(results) > 1 else results[0]), out[n_out]


def shape(dims, kind):
    return pltpu.VMEM(dims, kind)


def shape_out(dims, kind):
    return pltpu.HBM(dims, kind)


def load_padded(source_ref, pad_ref):
    rows = source_ref.shape[1]
    tail = (rows // 8) * 8
    pad_ref[tail:, :] = jnp.zeros_like(pad_ref[tail:, :])
    pad_ref[0:rows, :] = source_ref[0].astype(F32)
    return pad_ref[...]


def mask_column(mask_ref, wide_ref, pad):
    rows = mask_ref.shape[1]
    wide_ref[...] = jnp.zeros_like(wide_ref)
    line = jnp.where(mask_ref[...] > 0, 1.0, 0.0)
    wide_ref[:, 0:rows] = jnp.broadcast_to(line, (LANES, rows))
    return wide_ref[...].T[:pad]


def place_is(where_ref, step, place):
    high = where_ref[0] == (place >> 1) ^ (step >> 1)
    low = where_ref[1] == (place & 1) ^ (step & 1)
    return jnp.logical_and(high, low)


def forward_body(
    heads,
    where_ref,
    patches_ref,
    mask_ref,
    index_ref,
    token_ref,
    gain1_ref,
    bias1_ref,
    qbias_ref,
    vbias_ref,
    table_ref,
    pbias_ref,
    gamma1_ref,
    gain2_ref,
    bias2_ref,
    wqkv_hbm,
    wproj_hbm,
    mask_out,
    left0_ref,
    left1_ref,
    left2_ref,
    left3_ref,
    q_ref,
    k_ref,
    v_ref,
    probs_ref,
    attended_ref,
    hidden_ref,
    inner_ref,
    pad_s,
    wide_s,
    index_s,
    table_s,
    bias_s,
    wqkv_ref,
    wproj_ref,
    lefts_ref,
    sems,
):
    rows, width = patches_ref.shape[1:]
    pad = q_ref.shape[0]
    keys = k_ref.shape[0]
    head_size = width // heads
    copy_qkv = pltpu.make_async_copy(wqkv_hbm, wqkv_ref, sems.at[0])
    copy_qkv.start()
    copy_proj = pltpu.make_async_copy(wproj_hbm, wproj_ref, sems.at[1])
    copy_proj.start()

    index_s[...] = jnp.zeros_like(index_s)
    index_s[0:rows, 0:rows] = index_ref[...]
    entries = table_ref.shape[1]
    chunks = table_s.shape[2] // LANES
    top = jnp.max(jnp.abs(table_ref[...]))
    grow = 32767.0 / jnp.maximum(top, 1e-30)
    shrink = jnp.maximum(top, 1e-30) / 32767.0
    whole = jnp.round(table_ref[...] * grow).astype(jnp.int32)
    table_s[...] = jnp.zeros_like(table_s)
    for pair in range(heads // 2):
        both = whole[2 * pair : 2 * pair + 1] * 65536 + (whole[2 * pair + 1 : 2 * pair + 2] & 65535)
        table_s[pair, :, 0:entries] = jnp.broadcast_to(both, (8, entries))
    key_lane = lax.broadcasted_iota(jnp.int32, (1, LANES), 1)

    def gather_step(tile, carry):
        at_rows = pl.ds(pl.multiple_of(tile * 8, 8), 8)
        for half in range(keys // LANES):
            lanes = slice(half * LANES, (half + 1) * LANES)
            at = index_s[at_rows, lanes]
            low = at & (LANES - 1)
            high = at >> 7
            marks = [high == chunk for chunk in range(chunks)]
            real = key_lane + half * LANES < rows
            for pair in range(heads // 2):
                value = None
                for chunk in range(chunks):
                    line = table_s[pair, :, chunk * LANES : (chunk + 1) * LANES]
                    found = jnp.take_along_axis(line, low, axis=1, mode="promise_in_bounds")
                    value = found if value is None else jnp.where(marks[chunk], found, value)
                one = (value >> 16).astype(F32) * shrink
                two = ((value << 16) >> 16).astype(F32) * shrink
                if (half + 1) * LANES > rows:
                    one = jnp.where(real, one, -1e30)
                    two = jnp.where(real, two, -1e30)
                bias_s[2 * pair, at_rows, lanes] = one
                bias_s[2 * pair + 1, at_rows, lanes] = two
        return carry

    lax.fori_loop(0, pad // 8, gather_step, 0, unroll=2)

    column = mask_column(mask_ref, wide_s, pad)
    mask_out[...] = column
    picked = column[:, 0:1] > 0
    start = jnp.where(picked, row_of(token_ref), load_padded(patches_ref, pad_s))
    pad_s[...] = start
    xhat, _ = norm_stats(start)
    normed = (xhat * row_of(gain1_ref) + row_of(bias1_ref)).astype(BF16)
    lefts_ref[0] = normed
    copy_qkv.wait()
    scale = head_size ** (-0.5)
    q_ref[...] = ((dot_nn(normed, wqkv_ref[:, :width]) + row_of(qbias_ref)) * scale).astype(BF16)
    k_ref[0:pad, :] = dot_nn(normed, wqkv_ref[:, width : 2 * width]).astype(BF16)
    k_ref[pad:, :] = jnp.zeros_like(k_ref[pad:, :])
    v_ref[0:pad, :] = (dot_nn(normed, wqkv_ref[:, 2 * width :]) + row_of(vbias_ref)).astype(BF16)
    v_ref[pad:, :] = jnp.zeros_like(v_ref[pad:, :])

    lane = lax.broadcasted_iota(jnp.int32, (1, LANES), 1)
    first = lane < head_size

    def pair_step(pair, carry):
        at = pl.ds(pl.multiple_of(pair * LANES, LANES), LANES)
        query = q_ref[:, at]
        key = k_ref[:, at]
        value = v_ref[:, at]
        outs = []
        for side in range(2):
            head = pair * 2 + side
            own = first if side == 0 else jnp.logical_not(first)
            scores = dot_nt(jnp.where(own, query, jnp.zeros_like(query)), key) + bias_s[head]
            top = jnp.max(scores, axis=-1, keepdims=True)
            grown = jnp.exp(scores - top)
            probs = (grown * (1.0 / jnp.sum(grown, axis=-1, keepdims=True))).astype(BF16)
            probs_ref[head] = probs
            outs.append(dot_nn(probs, value))
        lefts_ref[1, :, at] = jnp.where(first, outs[0], outs[1]).astype(BF16)
        return carry

    lax.fori_loop(0, heads // 2, pair_step, 0, unroll=UNROLL_F)
    for at, out_ref in enumerate((left0_ref, left1_ref, left2_ref, left3_ref)):
        out_ref[...] = jnp.where(place_is(where_ref, at, 3), lefts_ref[1], lefts_ref[0])
    copy_proj.wait()
    attended = dot_nn(lefts_ref[1], wproj_ref[...]) + row_of(pbias_ref)
    attended_ref[...] = attended
    hidden = pad_s[...] + row_of(gamma1_ref) * attended
    hidden_ref[...] = hidden
    xhat2, _ = norm_stats(hidden)
    inner_ref[...] = (xhat2 * row_of(gain2_ref) + row_of(bias2_ref)).astype(BF16)


def forward(heads, pad, where, patches, row_mask, rel_index, token, gain1, bias1, qbias, vbias, table_t,
            pbias, gamma1, gain2, bias2, wqkv, wproj, deps=()):
    rows, width = patches.shape[1:]
    keys = round_up(pad, LANES)
    entries = round_up(table_t.shape[1], LANES)
    outs = (
        shape_out((pad, LANES), F32),
        shape_out((pad, width), BF16),
        shape_out((pad, width), BF16),
        shape_out((pad, width), BF16),
        shape_out((pad, width), BF16),
        shape_out((pad, width), BF16),
        shape_out((keys, width), BF16),
        shape_out((keys, width), BF16),
        shape_out((heads, pad, keys), BF16),
        shape_out((pad, width), F32),
        shape_out((pad, width), F32),
        shape((pad, width), BF16),
    )
    return call(
        functools.partial(forward_body, heads),
        outs,
        "shhhhhhhhhhhhhaa",
        (where, patches, row_mask, rel_index, token, gain1, bias1, qbias, vbias, table_t, pbias, gamma1,
         gain2, bias2, wqkv, wproj),
        (
            pltpu.VMEM((pad, width), F32),
            pltpu.VMEM((LANES, keys), F32),
            pltpu.VMEM((pad, keys), jnp.int32),
            pltpu.VMEM((heads // 2, 8, entries), jnp.int32),
            pltpu.VMEM((heads, pad, keys), F32),
            pltpu.VMEM(wqkv.shape, BF16),
            pltpu.VMEM(wproj.shape, BF16),
            pltpu.VMEM((2, pad, width), BF16),
            pltpu.SemaphoreType.DMA((2,)),
        ),
            )


def mlp_body(
    first, inner_ref, b1a_ref, b1b_ref, w1a_ref, w1b_ref, w2a_ref, w2b_ref, bias_ref, *rest
):
    if first:
        grads, masks, gamma2_ref = rest[0:2], rest[2:4], rest[4]
        rest = rest[5:]
        dbranches, rest = rest[0:2], rest[2:]
        cot_out, rest = rest[0], rest[1:]
        pad_s, wide_s = rest[-2:]
        rest = rest[:-2]
        pad = inner_ref.shape[0]
        for grad_ref, mask_ref, out_ref in zip(grads, masks, dbranches):
            column = mask_column(mask_ref, wide_s, pad)[:, 0:1]
            cotangent = load_padded(grad_ref, pad_s) * column
            out_ref[...] = (row_of(gamma2_ref) * cotangent).astype(BF16)
            if out_ref is dbranches[0]:
                own_cotangent = cotangent
            else:
                cot_out[...] = cotangent
        dbranch = dbranches[0][...]
        cotangent = own_cotangent
    else:
        dbranch, rest = rest[0][...], rest[1:]
    acta_ref, actb_ref, dprea_ref, dpreb_ref, dinner_ref, sums_ref, *more = rest
    if first:
        branch_ref = more[0]
    inner = inner_ref[...]
    branch = None
    dinner = None
    for at, (w1, w2, b1, act_out, dpre_out) in enumerate((
        (w1a_ref, w2a_ref, b1a_ref, acta_ref, dprea_ref),
        (w1b_ref, w2b_ref, b1b_ref, actb_ref, dpreb_ref),
    )):
        pre = dot_nn(inner, w1[...]) + row_of(b1).astype(F32)
        phi = 0.5 + 0.5 * lax.erf(pre * (0.5**0.5))
        act = (pre * phi).astype(BF16)
        act_out[...] = act
        slope = phi + pre * (jnp.exp(-0.5 * pre * pre) * 0.3989422804014327)
        dact = dot_nt(dbranch, w2[...])
        dpre = (dact * slope).astype(BF16)
        dpre_out[...] = dpre
        sums_ref[at : at + 1, :] = jnp.sum(dpre.astype(F32), axis=0, keepdims=True)
        this_dinner = dot_nt(dpre, w1[...])
        dinner = this_dinner if dinner is None else dinner + this_dinner
        if first:
            this_branch = dot_nn(act, w2[...])
            branch = this_branch if branch is None else branch + this_branch
    dinner_ref[...] = dinner.astype(dinner_ref.dtype)
    if first:
        branch = branch + row_of(bias_ref)
        branch_ref[...] = branch
        sums_ref[2:3, :] = jnp.sum(cotangent * branch, axis=0, keepdims=True)
        sums_ref[3:4, :] = jnp.sum(dbranch.astype(F32), axis=0, keepdims=True)
    else:
        sums_ref[2:4, :] = jnp.zeros_like(sums_ref[2:4, :])
    sums_ref[4:8, :] = jnp.zeros_like(sums_ref[4:8, :])


def mlp(inner, weights, bias, given, first, deps=(), carry=()):
    pad, width = inner.shape
    ff = weights[2].shape[1]
    kind = F32 if first else BF16
    outs = (
        (shape((pad, ff), BF16),) * 4
        + (shape((pad, width), kind), shape((8, ff), F32))
    )
    scratch = ()
    if first:
        outs = (shape((pad, width), BF16),) * 2 + (shape((pad, width), F32),) + outs
        outs += (shape_out((pad, width), F32),)
        scratch = (pltpu.VMEM((pad, width), F32), pltpu.VMEM((LANES, round_up(pad, LANES)), F32))
    return call(
        functools.partial(mlp_body, first), outs, "vhhvvvvh" + ("hvhvh" if first else "v"),
        (inner, *weights, bias, *given), scratch, cost=5, deps=deps, carry=carry,
    )


def far_branch_body(acta_ref, actb_ref, w2a_ref, w2b_ref, cot_ref, branch_ref, sums_ref):
    branch = dot_nn(acta_ref[...], w2a_ref[...]) + dot_nn(actb_ref[...], w2b_ref[...])
    branch_ref[...] = branch.astype(BF16)
    sums_ref[...] = jnp.zeros_like(sums_ref)
    sums_ref[2:3, :] = jnp.sum(cot_ref[...] * branch, axis=0, keepdims=True)


def far_branch(acta, actb, w2a, w2b, cotangent, deps=()):
    pad, width = cotangent.shape
    return call(
        far_branch_body, (shape_out((pad, width), BF16), shape((8, width), F32)), "vvvvv",
        (acta, actb, w2a, w2b, cotangent), cost=30, deps=deps,
    )


def split_rows(out_send, out_keep, total, low, block):
    for step in range(total.shape[0] // (2 * block)):
        even = total[2 * step * block : (2 * step + 1) * block]
        odd = total[(2 * step + 1) * block : (2 * step + 2) * block]
        out_send[step] = jnp.where(low, even, odd).astype(BF16)
        out_keep[step] = jnp.where(low, odd, even).astype(BF16)


def pair_grad_body(*refs):
    out_ref = refs[-1]
    for at in range(2):
        left0, left1, right0, right1 = refs[4 * at : 4 * at + 4]
        total = dot_tn(left0[...], right0[...]) + dot_tn(left1[...], right1[...])
        out_ref[at] = total.astype(BF16)


def pair_grad(one, two, deps=(), carry=()):
    width, ff = one[0].shape[1], one[2].shape[1]
    return call(
        pair_grad_body, shape((2, width, ff), BF16), "v" * 8, (*one, *two), cost=0.7, deps=deps,
        carry=carry,
    )


def fc_keep_body(block, where_ref, *refs):
    other, send_ref, keep_ref = refs[8:]
    for at in range(2):
        left0, left1, right0, right1 = refs[4 * at : 4 * at + 4]
        total = dot_tn(left0[...], right0[...]) + dot_tn(left1[...], right1[...])
        split_rows(
            send_ref.at[at], keep_ref.at[at], total + other[at].astype(F32), where_ref[2] > 0,
            block,
        )


def fc_keep(where, block, one, two, other, deps=(), carry=()):
    width, ff = one[0].shape[1], one[2].shape[1]
    outs = (shape((2, width // (2 * block), block, ff), BF16),) * 2
    return call(
        functools.partial(fc_keep_body, block), outs, "s" + "v" * 9, (where, *one, *two, other),
        cost=1.2, deps=deps, carry=carry,
    )


def deal_out(where_ref, outs, dqkv_ref, datt):
    third = dqkv_ref.shape[1] // 3
    for step, out_ref in enumerate(outs):
        part = datt
        for place in range(3):
            columns = dqkv_ref[:, place * third : (place + 1) * third]
            part = jnp.where(place_is(where_ref, step, place), columns, part)
        out_ref[...] = part


def heads_back(pairs, first_pair, head_size, q_ref, k_ref, v_ref, probs_ref, dmixed_ref, dqkv_ref,
               dscores_ref):
    pad = q_ref.shape[0]
    third = dqkv_ref.shape[1] // 3
    lane = lax.broadcasted_iota(jnp.int32, (1, LANES), 1)
    first = lane < head_size
    scale = head_size ** (-0.5)

    def pair_step(step, carry):
        at = pl.ds(pl.multiple_of((first_pair + step) * LANES, LANES), LANES)
        query = q_ref[:, at]
        key = k_ref[:, at]
        value = v_ref[:, at]
        dmixed = dmixed_ref[:, at]
        dq, dk, dv = [], [], []
        for side in range(2):
            own = first if side == 0 else jnp.logical_not(first)
            probs_b = probs_ref[2 * (first_pair + step) + side]
            probs = probs_b.astype(F32)
            dprobs = dot_nt(jnp.where(own, dmixed, jnp.zeros_like(dmixed)), value)
            inside = jnp.sum(probs * dprobs, axis=-1, keepdims=True)
            dscores = (probs * (dprobs - inside)).astype(BF16)
            dscores_ref[2 * step + side] = dscores
            dq.append(dot_nn(dscores, key))
            dk.append(dot_tn(dscores, query))
            dv.append(dot_tn(probs_b, dmixed))
        out = pl.multiple_of(step * LANES, LANES)
        dqkv_ref[:, pl.ds(out, LANES)] = (jnp.where(first, dq[0], dq[1]) * scale).astype(BF16)
        dqkv_ref[:, pl.ds(pl.multiple_of(out + third, LANES), LANES)] = (
            jnp.where(first, dk[0], dk[1])[:pad].astype(BF16)
        )
        dqkv_ref[:, pl.ds(pl.multiple_of(out + 2 * third, LANES), LANES)] = (
            jnp.where(first, dv[0], dv[1])[:pad].astype(BF16)
        )
        return carry

    lax.fori_loop(0, pairs, pair_step, 0, unroll=pairs)


def column_sums(out_ref, at, dqkv_ref):
    third = dqkv_ref.shape[1] // 3
    for row, part in ((4, 0), (5, 2)):
        lanes = slice(part * third, (part + 1) * third)
        out_ref[row : row + 1, at * third : (at + 1) * third] = jnp.sum(
            dqkv_ref[:, lanes].astype(F32), axis=0, keepdims=True
        )


def backward_body(
    heads,
    where_ref,
    dinner0_ref,
    dinner1_ref,
    hidden_ref,
    attended_ref,
    outgrad_ref,
    mask_ref,
    gain2_ref,
    gamma1_ref,
    wproj_ref,
    q_ref,
    k_ref,
    v_ref,
    probs_ref,
    dhidden_ref,
    dqkv_ref,
    out0_ref,
    out1_ref,
    out2_ref,
    out3_ref,
    dscores_ref,
    sums_ref,
    pad_s,
    dmixed_ref,
):
    width = hidden_ref.shape[1]
    cotangent = load_padded(outgrad_ref, pad_s) * mask_ref[:, 0:1]
    xhat, root = norm_stats(hidden_ref[...])
    dinner = dinner0_ref[...].astype(F32) + dinner1_ref[...].astype(F32)
    dhidden = cotangent + norm_back(dinner, xhat, root, row_of(gain2_ref))
    dhidden_ref[...] = dhidden
    datt = (row_of(gamma1_ref) * dhidden).astype(BF16)
    dmixed_ref[...] = dot_nt(datt, wproj_ref[...]).astype(BF16)
    sums_ref[0:1, :] = jnp.sum(dinner * xhat, axis=0, keepdims=True)
    sums_ref[1:2, :] = jnp.sum(dinner, axis=0, keepdims=True)
    sums_ref[2:3, :] = jnp.sum(dhidden * attended_ref[...], axis=0, keepdims=True)
    sums_ref[3:4, :] = jnp.sum(datt.astype(F32), axis=0, keepdims=True)
    sums_ref[4:8, :] = jnp.zeros((4, width), F32)
    heads_back(heads // 2, 0, width // heads, q_ref, k_ref, v_ref, probs_ref, dmixed_ref, dqkv_ref,
               dscores_ref)
    deal_out(
        where_ref, (out0_ref, out1_ref, out2_ref, out3_ref), dqkv_ref, datt
    )
    column_sums(sums_ref, 0, dqkv_ref)


def backward(heads, where, dinner0, dinner1, hidden, attended, out_grad, mask_col, gain2, gamma1,
             wproj, q, k, v, probs, deps=()):
    pad, width = hidden.shape
    keys = k.shape[0]
    outs = (
        shape((pad, width), F32),
        shape((pad, 3 * width), BF16),
        shape((pad, width), BF16),
        shape((pad, width), BF16),
        shape((pad, width), BF16),
        shape((pad, width), BF16),
        shape((heads, pad, keys), BF16),
        shape((8, width), F32),
    )
    return call(
        functools.partial(backward_body, heads),
        outs,
        "svvhhhhhhhhhhh",
        (where, dinner0, dinner1, hidden, attended, out_grad, mask_col, gain2, gamma1, wproj, q, k,
         v, probs),
        (pltpu.VMEM((pad, width), F32), pltpu.VMEM((pad, width), BF16)),
        cost=5,
        deps=deps,
    )


def first_norm_body(
    patches_ref, mask_ref, token_ref, gain1_ref, dqkv_ref, wqkv_ref, dhidden_ref,
    patchgrad_ref, sums_ref, pad_s,
):
    rows, width = patches_ref.shape[1:]
    picked = mask_ref[:, 0:1] > 0
    start = jnp.where(picked, row_of(token_ref), load_padded(patches_ref, pad_s))
    xhat, root = norm_stats(start)
    dnormed = dot_nt(dqkv_ref[...], wqkv_ref[...])
    dstart = dhidden_ref[...] + norm_back(dnormed, xhat, root, row_of(gain1_ref))
    patchgrad_ref[0] = jnp.where(picked, 0.0, dstart)[0:rows]
    sums_ref[0:1, :] = jnp.sum(jnp.where(picked, dstart, 0.0), axis=0, keepdims=True)
    sums_ref[1:2, :] = jnp.sum(dnormed * xhat, axis=0, keepdims=True)
    sums_ref[2:3, :] = jnp.sum(dnormed, axis=0, keepdims=True)
    sums_ref[3:8, :] = jnp.zeros((5, width), F32)


def first_norm(patches, mask_col, token, gain1, dqkv, wqkv, dhidden, deps=()):
    rows, width = patches.shape[1:]
    pad = mask_col.shape[0]
    outs = (shape_out((1, rows, width), F32), shape((8, width), F32))
    return call(
        first_norm_body, outs, "hhhhvhv",
        (patches, mask_col, token, gain1, dqkv, wqkv, dhidden),
        (pltpu.VMEM((pad, width), F32),), cost=5, deps=deps,
    )


def layer_end_body(hidden_ref, branch0_ref, branch1_ref, gamma2_ref, out_ref):
    branch = branch0_ref[...] + branch1_ref[...].astype(F32)
    layer = hidden_ref[...] + row_of(gamma2_ref) * branch
    out_ref[0] = layer[0 : out_ref.shape[1]].astype(BF16)


def layer_end(rows, hidden, branch0, branch1, gamma2, deps=(), carry=()):
    return call(
        layer_end_body, shape_out((1, rows, hidden.shape[1]), BF16), "hhvh",
        (hidden, branch0, branch1, gamma2), deps=deps, carry=carry,
    )


def table_grad_body(
    where_ref, index_ref, ds_ref, sums_b_ref, sums_n_ref, sums0_ref, sums1_ref, sums_f_ref, out_ref,
    index_s,
    total_s,
):
    rows = index_ref.shape[0]
    pad, head_pad, keys = ds_ref.shape
    high_count = total_s.shape[0] // head_pad
    index_s[...] = jnp.zeros_like(index_s)
    index_s[0:rows, 0:rows] = index_ref[...]
    total_s[...] = jnp.zeros_like(total_s)
    below = lax.broadcasted_iota(jnp.int32, (LANES, keys), 0).astype(BF16)
    ones = jnp.ones((LANES, keys), BF16)
    group = 16

    def step(at, carry):
        base = pl.multiple_of(at * group, group)
        lines = index_s[pl.ds(base, group), :]
        low = (lines & (LANES - 1)).astype(F32).astype(BF16)
        high = (lines >> 7).astype(F32).astype(BF16)
        total = None
        for i in range(group):
            onehot = jnp.where(below == low[i : i + 1], ones, jnp.zeros_like(ones))
            ds = ds_ref[base + i]
            left = jnp.concatenate(
                [
                    jnp.where(high[i : i + 1] == jnp.asarray(part, BF16), ds, jnp.zeros_like(ds))
                    for part in range(high_count)
                ],
                axis=0,
            )
            one = dot_nt(left, onehot)
            total = one if total is None else total + one
        total_s[...] += total
        return carry

    lax.fori_loop(0, pad // group, step, 0, unroll=2)
    for part in range(high_count):
        out_ref[0:head_pad, part * LANES : (part + 1) * LANES] = total_s[
            part * head_pad : (part + 1) * head_pad
        ]
    sums = sums0_ref[...] + sums1_ref[...] + sums_f_ref[...]
    out_ref[head_pad : head_pad + 6, :] = sums_b_ref[0:6, :]
    out_ref[head_pad + 6 : head_pad + 8, :] = sums[2:4]
    out_ref[head_pad + 8 : head_pad + 11, :] = sums_n_ref[0:3, :]
    for part in range(4):
        mine = jnp.where(where_ref[0] == part // 2, 1.0, 0.0)
        own = jnp.where(where_ref[1] == part % 2, sums[0:1], sums[1:2])
        out_ref[head_pad + 11 + part : head_pad + 12 + part, :] = mine * own
    out_ref[head_pad + 15 :, :] = jnp.zeros_like(out_ref[head_pad + 15 :, :])


def table_grad(where, rel_index, dscores, sums_b, sums_n, sums0, sums1, sums_f, entries, deps=()):
    pad, head_pad, keys = dscores.shape
    high_count = round_up(entries, LANES) // LANES
    width = sums_b.shape[1]
    return call(
        table_grad_body, shape((head_pad + 16, width), F32), "shvvvvvv",
        (where, rel_index, dscores, sums_b, sums_n, sums0, sums1, sums_f),
        (pltpu.VMEM((pad, keys), jnp.int32), pltpu.VMEM((high_count * head_pad, LANES), F32)),
        cost=3.2, deps=deps,
    )


def late_grad_body(block, piece, where_ref, *refs):
    lefts, rights, send_ref, keep_ref = refs[:4], refs[4:8], refs[8], refs[9]
    total = None
    for step in range(4):
        half = rights[step].shape[1] // 2
        one = dot_tn(lefts[step][...], rights[step][:, piece * half : (piece + 1) * half])
        total = one if total is None else total + one
    split_rows(send_ref.at[0], keep_ref.at[0], total, where_ref[2] > 0, block)


def late_grad(where, block, piece, lefts, rights, deps=(), carry=()):
    width = lefts[0].shape[1]
    half = rights[0].shape[1] // 2
    outs = (shape((1, width // (2 * block), block, half), BF16),) * 2
    return call(
        functools.partial(late_grad_body, block, piece), outs, "shvvvvvvv",
        (where, *lefts, *rights), cost=1.2, deps=deps, carry=carry,
    )


def fold_body(bit, where_ref, keep_ref, met_ref, send_out, keep_out):
    low = where_ref[2 + bit] > 0
    for at in range(send_out.shape[0]):
        for step in range(send_out.shape[1]):
            even, odd = (
                keep_ref[at, 2 * step + side].astype(F32) + met_ref[at, 2 * step + side].astype(F32)
                for side in range(2)
            )
            send_out[at, step] = jnp.where(low, even, odd).astype(BF16)
            keep_out[at, step] = jnp.where(low, odd, even).astype(BF16)


def fold(where, bit, keep, met, deps=(), carry=()):
    items, count, block, width = keep.shape
    return call(
        functools.partial(fold_body, bit), (shape((items, count // 2, block, width), BF16),) * 2,
        "svv", (where, keep, met), cost=0.4, deps=deps, carry=carry,
    )


def last_sum_body(keep_ref, met_ref, *outs):
    for at, out_ref in enumerate(outs):
        total = keep_ref[at, 0].astype(F32) + met_ref[at, 0].astype(F32)
        out_ref[...] = total.astype(out_ref.dtype)


def last_sum(keep, met, kind, deps=(), carry=()):
    make = shape_out if kind == F32 else shape
    return call(
        last_sum_body, (make(keep.shape[2:], kind),) * keep.shape[0], "vv", (keep, met), cost=0.4,
        deps=deps, carry=carry,
    )


def join_body(before_ref, keep_ref, met_ref, out_ref):
    half = before_ref.shape[1]
    out_ref[:, :half] = before_ref[...]
    out_ref[:, half:] = (keep_ref[0, 0].astype(F32) + met_ref[0, 0].astype(F32)).astype(BF16)


def join(before, keep, met, deps=(), carry=()):
    block, half = before.shape
    return call(
        join_body, shape((block, 2 * half), BF16), "vvv", (before, keep, met), deps=deps,
        carry=carry,
    )


def assemble_body(where_ref, own_ref, over_x_ref, over_core_ref, qkv_ref, proj_ref):
    width = own_ref.shape[1]
    high = where_ref[0] > 0
    core = where_ref[1] > 0
    own, far = own_ref[...], over_x_ref[...]
    side, corner = over_core_ref[0], over_core_ref[1]
    here = (jnp.where(core, side, own), jnp.where(core, own, side))
    there = (jnp.where(core, corner, far), jnp.where(core, far, corner))
    for at in range(2):
        qkv_ref[:, at * width : (at + 1) * width] = jnp.where(high, there[at], here[at]).astype(F32)
    qkv_ref[:, 2 * width :] = jnp.where(high, here[0], there[0]).astype(F32)
    proj_ref[...] = jnp.where(high, here[1], there[1]).astype(F32)


def assemble(where, own, far, pair, deps=()):
    block, width = own.shape
    return call(
        assemble_body, (shape_out((block, 3 * width), F32), shape_out((block, width), F32)),
        "svvv", (where, own, far, pair), deps=deps,
    )


def on_device(
    dp,
    patches,
    row_mask,
    out_grad,
    rel_index,
    mask_token,
    ln1_gain,
    ln1_bias,
    qkv_weight,
    query_bias,
    value_bias,
    rel_table,
    proj_weight,
    proj_bias,
    gamma1,
    ln2_gain,
    ln2_bias,
    fc1_weight,
    fc1_bias,
    fc2_weight,
    fc2_bias,
    gamma2,
):
    rows, width = patches.shape[1:]
    entries, heads = rel_table.shape
    pad = round_up(rows, 16)
    mp_at = lax.axis_index("mp")
    dp_at = lax.axis_index("dp")
    x_at, core_at = mp_at // 2, mp_at % 2
    bits = dp.bit_length() - 1
    where = jnp.stack(
        [x_at, core_at] + [(dp_at >> bit) & 1 for bit in range(bits)]
    ).astype(jnp.int32)

    def swap(axis, bit):
        count = 4 if axis == "mp" else dp
        pairs = [(at, at ^ bit) for at in range(count)]
        return lambda value: lax.ppermute(value, axis, pairs)

    over_core, over_x = swap("mp", 1), swap("mp", 2)
    over_bit = [swap("dp", 1 << bit) for bit in range(bits)]

    out_grad1, row_mask1 = over_x(out_grad), over_x(row_mask)
    b1b, w1b, w2b = over_core(fc1_bias), over_core(fc1_weight), over_core(fc2_weight)

    before = []

    def step(kernel, *args, deps=(), **more):
        out, token = kernel(*args, deps=tuple(before) + tuple(deps), **more)
        before[:] = [token]
        return out

    mask_col, left0, left1, left2, left3, q, k, v, probs, attended, hidden, inner = step(
        forward, heads, pad, where, patches, row_mask, rel_index, mask_token, ln1_gain, ln1_bias,
        query_bias, value_bias, rel_table.T, proj_bias, gamma1, ln2_gain, ln2_bias, qkv_weight,
        proj_weight,
    )
    inner1 = over_x(inner)
    weights = (fc1_bias, b1b, fc1_weight, w1b, fc2_weight, w2b)
    dbranch, dbranch1, cot1, acta0, actb0, dprea0, dpreb0, dinner0, sums0, branch0, left1 = step(
        mlp, inner, weights, fc2_bias, (out_grad, out_grad1, row_mask, row_mask1, gamma2), True,
        carry=(left1,),
    )
    met_left1 = over_core(left1)
    acta1, actb1, dprea1, dpreb1, dinner1, sums1 = step(
        mlp, inner1, weights, fc2_bias, (dbranch1,), False
    )
    dinner_in = over_x(dinner1)

    block = width // dp

    def middle(keep, met, first, last):
        for bit in range(first, last):
            send, keep = step(fold, where, bit, keep, met)
            met = over_bit[bit](send)
        return keep, met

    fc_other = over_core(
        step(pair_grad, (inner, inner1, dpreb0, dpreb1), (dbranch, dbranch1, actb0, actb1))
    )
    branch1, sums_f = step(far_branch, acta1, actb1, fc2_weight, w2b, cot1)
    fc_send, fc_kept, left2, left3 = step(
        fc_keep, where, block, (inner, inner1, dprea0, dprea1), (dbranch, dbranch1, acta0, acta1),
        fc_other, deps=(met_left1,), carry=(left2, left3),
    )
    fc_met = over_bit[0](fc_send)
    met_left2, met_left3 = over_x(left2), swap("mp", 3)(left3)

    dhidden, dqkv, own, core, far, corner, dscores, sums_b = step(
        backward, heads, where, dinner0, dinner_in, hidden, attended, out_grad, mask_col, ln2_gain,
        gamma1, proj_weight, q, k, v, probs,
    )
    met_far, met_corner, met_core = over_x(far), swap("mp", 3)(corner), over_core(core)
    patch_grad, sums_n = step(
        first_norm, patches, mask_col, mask_token, ln1_gain, dqkv, qkv_weight, dhidden,
        deps=(met_left2, met_left3),
    )
    head_pad = 16
    ds = jnp.pad(jnp.transpose(dscores, (1, 0, 2)), ((0, 0), (0, head_pad - heads), (0, 0)))
    small = step(table_grad, where, rel_index, ds, sums_b, sums_n, sums0, sums1, sums_f,
                 entries)
    small = small + over_core(small)
    fc_kept, fc_met = middle(fc_kept, fc_met, 1, 2)

    late = ((left0, met_left1, met_left2, met_left3), (own, met_core, met_far, met_corner))
    late0_send, late0_keep = step(late_grad, where, block, 0, *late)
    late0_met = over_bit[0](late0_send)
    late1_send, late1_keep = step(late_grad, where, block, 1, *late)
    late1_met = over_bit[0](late1_send)
    small = small + over_x(small)

    late0_send, late0_keep = step(fold, where, 1, late0_keep, late0_met)
    late0_met = over_bit[1](late0_send)
    fc_send, fc_kept, small, branch1 = step(
        fold, where, 2, fc_kept, fc_met, carry=(small, branch1)
    )
    fc_met = over_bit[2](fc_send)
    fc_kept, fc_met = middle(fc_kept, fc_met, 3, bits)
    branch_in = over_x(branch1)
    small = small + over_bit[0](small)
    late1_send, late1_keep = step(fold, where, 1, late1_keep, late1_met)
    late1_met = over_bit[1](late1_send)
    late0_send, late0_keep, small = step(
        fold, where, 2, late0_keep, late0_met, carry=(small,)
    )
    late0_met = over_bit[2](late0_send)
    late0_keep, late0_met = middle(late0_keep, late0_met, 3, bits)
    small = small + over_bit[1](small)
    layer_out, small = step(layer_end, rows, hidden, branch0, branch_in, gamma2, carry=(small,))
    late1_keep, late1_met = middle(late1_keep, late1_met, 2, bits)
    for bit in range(2, bits):
        small = small + over_bit[bit](small)
    fc1_weight_grad, fc2_weight_grad = step(last_sum, fc_kept, fc_met, F32)
    late0_own = step(last_sum, late0_keep, late0_met, BF16)
    late_own = step(join, late0_own, late1_keep, late1_met)
    late_x = over_x(late_own)

    late_pair = over_core(jnp.stack([late_own, late_x]))
    qkv_weight_grad, proj_weight_grad = step(assemble, where, late_own, late_x, late_pair)

    rel_grad = small[:heads, :entries].T
    (ln2_gain_grad, ln2_bias_grad, gamma1_grad, proj_bias_grad, query_bias_grad, value_bias_grad,
     gamma2_grad, fc2_bias_grad, mask_token_grad, ln1_gain_grad, ln1_bias_grad) = [
        small[head_pad + at] for at in range(11)
    ]
    fc1_bias_grad = lax.dynamic_index_in_dim(small, head_pad + 11 + mp_at, 0, False)
    return (
        layer_out,
        patch_grad,
        mask_token_grad,
        ln1_gain_grad,
        ln1_bias_grad,
        qkv_weight_grad,
        query_bias_grad,
        value_bias_grad,
        rel_grad,
        proj_weight_grad,
        proj_bias_grad,
        gamma1_grad,
        ln2_gain_grad,
        ln2_bias_grad,
        fc1_weight_grad,
        fc1_bias_grad,
        fc2_weight_grad.T,
        fc2_bias_grad,
        gamma2_grad,
    )


def solution(mesh):
    rows3 = P(("dp", "mp"), None, None)
    placed = (
        (rows3, P(("dp", "mp"), None), rows3)
        + (P(),) * 13
        + (P(None, "mp"), P("mp"), P("mp", None), P(), P())
    )
    return jax.shard_map(
        functools.partial(on_device, mesh.shape["dp"]),
        mesh=mesh,
        in_specs=placed,
        out_specs=(
            rows3,
            rows3,
            P(),
            P(),
            P(),
            P("dp", None),
            P(),
            P(),
            P(),
            P("dp", None),
            P(),
            P(),
            P(),
            P(),
            P("dp", "mp"),
            P("mp"),
            P("mp", "dp"),
            P(),
            P(),
        ),
        check_vma=False,
    )
```

time: 143 us -> 121 us (0.85); the launches traced: 142 us -> 119 us
  waiting for transfers between devices: 35.1 us -> 23.3 us
  local copies, waits for them, and re-layouts: 12.5 us -> 4.1 us
  starting transfers between devices: 38.7 us -> 35.7 us
  other arithmetic: 1.98 us -> 0.11 us
    ppermute x30 -> x31, waiting for transfers between devices: 35.1 us -> 23.3 us  [swap(): return lambda value: lax.ppermute(value, axis, pairs)]
    unnamed x45 -> x9, local copies, waits for them, and re-layouts: 10.4 us -> 2 us
    ppermute x30 -> x31, starting transfers between devices: 38.7 us -> 35.7 us  [swap(): return lambda value: lax.ppermute(value, axis, pairs)]
    convert_element_type x2 -> x0, other arithmetic: 1.71 us -> none  [the longest x1 0.97 us: on_device(): qkv_weight_grad = jnp.concatenate([low0, low1[:, :half], high0, high1[:,...]
    pallas_call x16 -> x22, Pallas kernels: 53 us -> 54.4 us  [call(): pl.pallas_call(inner, name=getattr(body, 'func', body).__name__, out_shap...]
  transfers between devices with their start and end apart: 30 -> 31, of which waited for: 12 -> 14; matrix products, arithmetic and copies ran while one was open for 3% -> 3% of each run, Pallas kernels for 31% -> 44%
where the time goes in v3:
time: 121 us; the launch traced here: 119 us
  Pallas kernels  54.4 us (45%)
  starting transfers between devices  35.7 us (30%)
  waiting for transfers between devices  23.3 us (19%)
  local copies, waits for them, and re-layouts  4.1 us (3%)
    pallas_call x22, Pallas kernels, call(): pl.pallas_call(inner, name=getattr(body, 'func', body).__name__, out_shap...  54.4 us
    ppermute x31, starting transfers between devices, swap(): return lambda value: lax.ppermute(value, axis, pairs)  35.7 us
    ppermute x31, waiting for transfers between devices, swap(): return lambda value: lax.ppermute(value, axis, pairs)  23.3 us
  transfers between devices with their start and end apart: 31, of which 14 were waited for; matrix products, arithmetic and copies ran while one was open for 3% of the time, Pallas kernels for 44%

profile of v3, /device:TPU:0, one launch (start us, length us, event | category | flops | bytes accessed | tf_op | source)
XLA Modules:
  0.0 118.6 jit_solution(12965592315472056124)
XLA Ops:
  1.3 2.9 %collective-permute-start.3 = (bf16[1,197,768]{2,1,0:T(8,128)(2,1)}, bf16[1,197,768]{2,1,0:T(8,128)(2,1)S(1)}, u32[]{:S(2)}, u32[]{:S(2)}) collective-permute-start(bf16[1,197,768]{2,1,0:T(8,128)(2,1)} %refs_5_.8), channel_id=1, source_target_pairs={{0,2},{1,3},{2,0},{3,1},{4,6},{5,7},{6,4},{7,5},{8,10},{9,11},{10,... | collective-permute-start | bytes 907784 | tf_op jit(solution)/shard_map/ppermute | solution.py:817
  4.3 10.0 %forward_body.1 = (f32[208,128]{1,0:T(8,128)}, bf16[208,768]{1,0:T(8,128)(2,1)}, bf16[208,768]{1,0:T(8,128)(2,1)}, bf16[208,768]{1,0:T(8,128)(2,1)}, bf16[208,76...) custom-call(s32[5]{0:T(128)S(1)} %stack.32.refs_0_, ...), custom_call_target="tpu_custom_call" | custom-call | flops 1000000000 | bytes 1000 | tf_op jit(solution)/shard_map/forward_body/pallas_call | solution.py:80
  14.3 2.1 %collective-permute-start.5 = (bf16[208,768]{1,0:T(8,128)(2,1)S(1)}, bf16[208,768]{1,0:T(8,128)(2,1)S(1)}, u32[]{:S(2)}, u32[]{:S(2)}) collective-permute-start(bf16[208,768]{1,0:T(8,128)(2,1)S(1)} %get-tuple-element.115.refs_0_.refs_1_), channel_id=1, source_target_pairs={{0,2},{1,3},{2,0},{3,1},{4,6},{5,7},{6,4},{7,5},{8,10},{9,11},{10,... | collective-permute-start | bytes 958472 | tf_op jit(solution)/shard_map/ppermute | solution.py:817
  16.9 4.7 %mlp_body.2 = (bf16[208,768]{1,0:T(8,128)(2,1)S(1)}, bf16[208,768]{1,0:T(8,128)(2,1)S(1)}, f32[208,768]{1,0:T(8,128)S(1)}, bf16[208,768]{1,0:T(8,128)(2,1)S(1)},...) custom-call(bf16[208,768]{1,0:T(8,128)(2,1)S(1)} %get-tuple-element., ...), custom_call_target="tpu_custom_call", output_to_operand_aliasing={{11}: (14, {})} | custom-call | flops 5000000000 | bytes 1000 | tf_op jit(solution)/shard_map/mlp_body/pallas_call | solution.py:80
  21.8 2.7 %collective-permute-done.5.refs_0_.refs_1_.refs_2_ = bf16[208,768]{1,0:T(8,128)(2,1)S(1)} collective-permute-done((bf16[208,768]{1,0:T(8,128)(2,1)S(1)}, bf16[208,768]{1,0:T(8,128)(2,1)S(1)}, u32[]{:S(2)}, u32[]{:S(2)}) %collective-permute-start.5) | collective-permute-done | bytes 319520 | tf_op jit(solution)/shard_map/ppermute | solution.py:817
  24.6 3.0 %mlp_body.3 = (bf16[208,768]{1,0:T(8,128)(2,1)S(1)}, bf16[208,768]{1,0:T(8,128)(2,1)S(1)}, bf16[208,768]{1,0:T(8,128)(2,1)S(1)}, bf16[208,768]{1,0:T(8,128)(2,1)...) custom-call(bf16[208,768]{1,0:T(8,128)(2,1)S(1)} %collective-permute-done.5.refs_0_.refs_1_.refs_2_, ...), custom_call_target="tpu_custom_call" | custom-call | flops 5000000000 | bytes 1000 | tf_op jit(solution)/shard_map/mlp_body/pallas_call | solution.py:80
  27.6 1.8 %collective-permute-start.9 = (bf16[208,768]{1,0:T(8,128)(2,1)S(1)}, bf16[208,768]{1,0:T(8,128)(2,1)S(1)}, u32[]{:S(2)}, u32[]{:S(2)}) collective-permute-start(bf16[208,768]{1,0:T(8,128)(2,1)S(1)} %get-tuple-element.141), channel_id=1, source_target_pairs={{0,2},{1,3},{2,0},{3,1},{4,6},{5,7},{6,4},{7,5},{8,10},{9,11},{10,... | collective-permute-start | bytes 958472 | tf_op jit(solution)/shard_map/ppermute | solution.py:817
  32.4 3.1 %collective-permute-done.6.refs_9_ = bf16[2,768,768]{2,1,0:T(8,128)(2,1)S(1)} collective-permute-done((bf16[2,768,768]{2,1,0:T(8,128)(2,1)S(1)}, bf16[2,768,768]{2,1,0:T(8,128)(2,1)S(1)}, u32[]{:S(2)}, u32[]{:S(2)}) %collective-permute-start.6) | collective-permute-done | bytes 2359328 | tf_op jit(solution)/shard_map/ppermute | solution.py:817
  35.4 2.1 %fc_keep_body.1 = (bf16[2,4,96,768]{3,2,1,0:T(8,128)(2,1)S(1)}, bf16[2,4,96,768]{3,2,1,0:T(8,128)(2,1)S(1)}, f32[8,128]{1,0:T(8,128)S(1)}, bf16[208,768]{1,0:T(8,128)(2,1)}, bf16[208,768]{1,0:T(8,128)(2,1)}) custom-call(s32[5]{0:T(128)S(1)} %stack.32.refs_0_, ...), custom_call_target="tpu_custom_call", output_to_operand_aliasing={{3}: (12, {}), {4}: (13, {})} | custom-call | flops 1200000000 | bytes 1000 | tf_op jit(solution)/shard_map/fc_keep_body/pallas_call | solution.py:80
  39.1 1.5 %collective-permute-start.8 = (bf16[2,4,96,768]{3,2,1,0:T(8,128)(2,1)S(1)}, bf16[2,4,96,768]{3,2,1,0:T(8,128)(2,1)S(1)}, u32[]{:S(2)}, u32[]{:S(2)}) collective-permute-start(bf16[2,4,96,768]{3,2,1,0:T(8,128)(2,1)S(1)} %get-tuple-element.139), channel_id=1, source_target_pairs={{0,4},{4,0},{8,12},{12,8},{16,20},{20,16},{24,28},{28,24},{1,5},{5... | collective-permute-start | bytes 3538952 | tf_op jit(solution)/shard_map/ppermute | solution.py:817
  40.6 8.2 %backward_body.1 = (f32[208,768]{1,0:T(8,128)S(1)}, bf16[208,2304]{1,0:T(8,128)(2,1)S(1)}, bf16[208,768]{1,0:T(8,128)(2,1)S(1)}, bf16[208,768]{1,0:T(8,128)(2,1)...) custom-call(s32[5]{0:T(128)S(1)} %stack.32.refs_0_, ...), custom_call_target="tpu_custom_call" | custom-call | flops 5000000000 | bytes 1000 | tf_op jit(solution)/shard_map/backward_body/pallas_call | solution.py:80
  51.5 1.9 %collective-permute-done.11.refs_9_.refs_4_ = bf16[208,768]{1,0:T(8,128)(2,1)S(1)} collective-permute-done((bf16[208,768]{1,0:T(8,128)(2,1)}, bf16[208,768]{1,0:T(8,128)(2,1)S(1)}, u32[]{:S(2)}, u32[]{:S(2)}) %collective-permute-start.11) | collective-permute-done | bytes 319520 | tf_op jit(solution)/shard_map/ppermute | solution.py:817
  53.4 4.6 %first_norm_body.1 = (f32[1,197,768]{2,1,0:T(8,128)}, f32[8,768]{1,0:T(8,128)S(1)}, f32[8,128]{1,0:T(8,128)S(1)}) custom-call(bf16[1,197,768]{2,1,0:T(8,128)(2,1)} %refs_0_.1, f32[208,128]{1,0:T(8,128)} %get-tuple-element.143.refs_6_.refs_1_, f32[768]{0:T(1024)} %refs_2_.5, f32[768]{0:T(1024)} %refs_3_.8, bf16[208,2304]{1,0:T(8,128)(2,1)S(1)} %get-tuple-element.151.refs_4_, ...), custom_call_target="tpu_custom_call" | custom-call | flops 5000000000 | bytes 1000 | tf_op jit(solution)/shard_map/first_norm_body/pallas_call | solution.py:80
  58.0 6.3 %table_grad_body.1 = (f32[32,768]{1,0:T(8,128)S(1)}, f32[8,128]{1,0:T(8,128)S(1)}) custom-call(s32[5]{0:T(128)S(1)} %stack.32.refs_0_, s32[197,197]{1,0:T(8,128)} %refs_1_.7, bf16[208,16,256]{2,1,0:T(8,128)(2,1)S(1)} %pad.4.refs_2_, f32[8,768]{1,0:T(8,128)S(1)} %get-tuple-element.150.refs_3_, f32[8,768]{1,0:T(8,128)S(1)} %get-tuple-element.156.refs_4_, ...), custom_call_target="tpu_custom_call" | custom-call | flops 3200000000 | bytes 1000 | tf_op jit(solution)/shard_map/table_grad_body/pallas_call | solution.py:80
  64.3 3.3 %collective-permute-done.8.refs_2_ = bf16[2,4,96,768]{3,2,1,0:T(8,128)(2,1)S(1)} collective-permute-done((bf16[2,4,96,768]{3,2,1,0:T(8,128)(2,1)S(1)}, bf16[2,4,96,768]{3,2,1,0:T(8,128)(2,1)S(1)}, u32[]{:S(2)}, u32[]{:S(2)}) %collective-permute-start.8) | collective-permute-done | bytes 1179680 | tf_op jit(solution)/shard_map/ppermute | solution.py:817
  68.5 1.7 %collective-permute-start.12 = (bf16[2,2,96,768]{3,2,1,0:T(8,128)(2,1)S(1)}, bf16[2,2,96,768]{3,2,1,0:T(8,128)(2,1)S(1)}, u32[]{:S(2)}, u32[]{:S(2)}) collective-permute-start(bf16[2,2,96,768]{3,2,1,0:T(8,128)(2,1)S(1)} %get-tuple-element.163), channel_id=1, source_target_pairs={{0,8},{4,12},{8,0},{12,4},{16,24},{20,28},{24,16},{28,20},{1,9},{5... | collective-permute-start | bytes 1769480 | tf_op jit(solution)/shard_map/ppermute | solution.py:817
  70.2 2.0 %late_grad_body.2 = (bf16[1,4,96,384]{3,2,1,0:T(8,128)(2,1)S(1)}, bf16[1,4,96,384]{3,2,1,0:T(8,128)(2,1)S(1)}, f32[8,128]{1,0:T(8,128)S(1)}) custom-call(s32[5]{0:T(128)S(1)} %stack.32.refs_0_, bf16[208,768]{1,0:T(8,128)(2,1)} %get-tuple-element.164.refs_1_, bf16[208,768]{1,0:T(8,128)(2,1)S(1)} %collective-permute-done.7.refs_11_.refs_2_, ...), custom_call_target="tpu_custom_call" | custom-call | flops 1200000000 | bytes 1000 | tf_op jit(solution)/shard_map/late_grad_body/pallas_call | solution.py:80
  72.2 1.6 %collective-permute-start.16 = (bf16[1,4,96,384]{3,2,1,0:T(8,128)(2,1)S(1)}, bf16[1,4,96,384]{3,2,1,0:T(8,128)(2,1)S(1)}, u32[]{:S(2)}, u32[]{:S(2)}) collective-permute-start(bf16[1,4,96,384]{3,2,1,0:T(8,128)(2,1)S(1)} %get-tuple-element.171), channel_id=1, source_target_pairs={{0,4},{4,0},{8,12},{12,8},{16,20},{20,16},{24,28},{28,24},{1,5},{5... | collective-permute-start | bytes 884744 | tf_op jit(solution)/shard_map/ppermute | solution.py:817
  75.7 2.0 %late_grad_body.3 = (bf16[1,4,96,384]{3,2,1,0:T(8,128)(2,1)S(1)}, bf16[1,4,96,384]{3,2,1,0:T(8,128)(2,1)S(1)}, f32[8,128]{1,0:T(8,128)S(1)}) custom-call(s32[5]{0:T(128)S(1)} %stack.32.refs_0_, bf16[208,768]{1,0:T(8,128)(2,1)} %get-tuple-element.164.refs_1_, bf16[208,768]{1,0:T(8,128)(2,1)S(1)} %collective-permute-done.7.refs_11_.refs_2_, ...), custom_call_target="tpu_custom_call" | custom-call | flops 1200000000 | bytes 1000 | tf_op jit(solution)/shard_map/late_grad_body/pallas_call | solution.py:80
  78.3 1.8 %collective-permute-done.18 = f32[32,768]{1,0:T(8,128)S(1)} collective-permute-done((f32[32,768]{1,0:T(8,128)S(1)}, f32[32,768]{1,0:T(8,128)S(1)}, u32[]{:S(2)}, u32[]{:S(2)}) %collective-permute-start.18) | collective-permute-done | bytes 98336 | tf_op jit(solution)/shard_map/ppermute | solution.py:817
  81.9 1.7 %collective-permute-done.12.refs_2_ = bf16[2,2,96,768]{3,2,1,0:T(8,128)(2,1)S(1)} collective-permute-done((bf16[2,2,96,768]{3,2,1,0:T(8,128)(2,1)S(1)}, bf16[2,2,96,768]{3,2,1,0:T(8,128)(2,1)S(1)}, u32[]{:S(2)}, u32[]{:S(2)}) %collective-permute-start.12) | collective-permute-done | bytes 589856 | tf_op jit(solution)/shard_map/ppermute | solution.py:817
  84.8 1.7 %collective-permute-start.20 = (bf16[1,2,96,384]{3,2,1,0:T(8,128)(2,1)S(1)}, bf16[1,2,96,384]{3,2,1,0:T(8,128)(2,1)S(1)}, u32[]{:S(2)}, u32[]{:S(2)}) collective-permute-start(bf16[1,2,96,384]{3,2,1,0:T(8,128)(2,1)S(1)} %get-tuple-element.179), channel_id=1, source_target_pairs={{0,8},{4,12},{8,0},{12,4},{16,24},{20,28},{24,16},{28,20},{1,9},{5... | collective-permute-start | bytes 442376 | tf_op jit(solution)/shard_map/ppermute | solution.py:817
  86.6 1.5 %collective-permute-start.22 = (f32[32,768]{1,0:T(8,128)S(1)}, f32[32,768]{1,0:T(8,128)S(1)}, u32[]{:S(2)}, u32[]{:S(2)}) collective-permute-start(f32[32,768]{1,0:T(8,128)S(1)} %get-tuple-element.184), channel_id=1, source_target_pairs={{0,4},{4,0},{8,12},{12,8},{16,20},{20,16},{24,28},{28,24},{1,5},{5... | collective-permute-start | bytes 294920 | tf_op jit(solution)/shard_map/ppermute | solution.py:817
  88.1 2.6 %collective-permute-start.26 = (bf16[2,1,96,768]{3,2,1,0:T(8,128)(2,1)S(1)}, bf16[2,1,96,768]{3,2,1,0:T(8,128)(2,1)S(1)}, u32[]{:S(2)}, u32[]{:S(2)}) collective-permute-start(bf16[2,1,96,768]{3,2,1,0:T(8,128)(2,1)S(1)} %get-tuple-element.193), channel_id=1, source_target_pairs={{0,16},{4,20},{8,24},{12,28},{16,0},{20,4},{24,8},{28,12},{1,17},{... | collective-permute-start | bytes 884744 | tf_op jit(solution)/shard_map/ppermute | solution.py:817
  92.6 1.4 %collective-permute-start.27 = (bf16[1,2,96,384]{3,2,1,0:T(8,128)(2,1)S(1)}, bf16[1,2,96,384]{3,2,1,0:T(8,128)(2,1)S(1)}, u32[]{:S(2)}, u32[]{:S(2)}) collective-permute-start(bf16[1,2,96,384]{3,2,1,0:T(8,128)(2,1)S(1)} %get-tuple-element.195), channel_id=1, source_target_pairs={{0,8},{4,12},{8,0},{12,4},{16,24},{20,28},{24,16},{28,20},{1,9},{5... | collective-permute-start | bytes 442376 | tf_op jit(solution)/shard_map/ppermute | solution.py:817
  94.1 3.0 %collective-permute-start.25 = (bf16[1,1,96,384]{3,2,1,0:T(8,128)(2,1)S(1)}, bf16[1,1,96,384]{3,2,1,0:T(8,128)(2,1)S(1)}, u32[]{:S(2)}, u32[]{:S(2)}) collective-permute-start(bf16[1,1,96,384]{3,2,1,0:T(8,128)(2,1)S(1)} %get-tuple-element.191), channel_id=1, source_target_pairs={{0,16},{4,20},{8,24},{12,28},{16,0},{20,4},{24,8},{28,12},{1,17},{... | collective-permute-start | bytes 221192 | tf_op jit(solution)/shard_map/ppermute | solution.py:817
  97.1 3.0 %collective-permute-done.23 = f32[32,768]{1,0:T(8,128)S(1)} collective-permute-done((f32[32,768]{1,0:T(8,128)S(1)}, f32[32,768]{1,0:T(8,128)S(1)}, u32[]{:S(2)}, u32[]{:S(2)}) %collective-permute-start.23) | collective-permute-done | bytes 98336 | tf_op jit(solution)/shard_map/ppermute | solution.py:817
  100.1 2.1 %layer_end_body.1 = (bf16[1,197,768]{2,1,0:T(8,128)(2,1)}, f32[8,128]{1,0:T(8,128)S(1)}, f32[32,768]{1,0:T(8,128)S(1)}) custom-call(f32[208,768]{1,0:T(8,128)} %get-tuple-element.114.refs_3_.refs_0_, f32[208,768]{1,0:T(8,128)} %get-tuple-element.118.refs_1_, bf16[208,768]{1,0:T(8,128)(2,1)S(1)} %collective-permute-done.19.refs_2_, ...), custom_call_target="tpu_custom_call", output_to_operand_aliasing={{2}: (5, {})} | custom-call | flops 1000000000 | bytes 1000 | tf_op jit(solution)/shard_map/layer_end_body/pallas_call | solution.py:80
  102.8 2.8 %collective-permute-start.28 = (bf16[1,1,96,384]{3,2,1,0:T(8,128)(2,1)S(1)}, bf16[1,1,96,384]{3,2,1,0:T(8,128)(2,1)S(1)}, u32[]{:S(2)}, u32[]{:S(2)}) collective-permute-start(bf16[1,1,96,384]{3,2,1,0:T(8,128)(2,1)S(1)} %get-tuple-element.201), channel_id=1, source_target_pairs={{0,16},{4,20},{8,24},{12,28},{16,0},{20,4},{24,8},{28,12},{1,17},{... | collective-permute-start | bytes 221192 | tf_op jit(solution)/shard_map/ppermute | solution.py:817
  108.2 1.6 %collective-permute-start.29 = (bf16[96,768]{1,0:T(8,128)(2,1)S(1)}, bf16[96,768]{1,0:T(8,128)(2,1)S(1)}, u32[]{:S(2)}, u32[]{:S(2)}) collective-permute-start(bf16[96,768]{1,0:T(8,128)(2,1)S(1)} %get-tuple-element.203.refs_1_), channel_id=1, source_target_pairs={{0,2},{1,3},{2,0},{3,1},{4,6},{5,7},{6,4},{7,5},{8,10},{9,11},{10,... | collective-permute-start | bytes 442376 | tf_op jit(solution)/shard_map/ppermute | solution.py:817
  109.7 2.7 %collective-permute-start.24 = (f32[32,768]{1,0:T(8,128)S(1)}, f32[32,768]{1,0:T(8,128)S(1)}, u32[]{:S(2)}, u32[]{:S(2)}) collective-permute-start(f32[32,768]{1,0:T(8,128)S(1)} %get-tuple-element.189), channel_id=1, source_target_pairs={{0,16},{4,20},{8,24},{12,28},{16,0},{20,4},{24,8},{28,12},{1,17},{... | collective-permute-start | bytes 294920 | tf_op jit(solution)/shard_map/ppermute | solution.py:817
  116.9 1.6 %assemble_body.1 = (f32[96,2304]{1,0:T(8,128)}, f32[96,768]{1,0:T(8,128)}, f32[8,128]{1,0:T(8,128)}) custom-call(s32[5]{0:T(128)S(1)} %stack.32.refs_0_, bf16[96,768]{1,0:T(8,128)(2,1)S(1)} %get-tuple-element.203.refs_1_, bf16[96,768]{1,0:T(8,128)(2,1)S(1)} %collective-permute-done.29.refs_2_, bf16[2,96,768]{2,1,0:T(8,128)(2,1)S(1)} %collective-permute-done.30.refs_3_, ...), custom_call_target="tpu_custom_call" | custom-call | flops 1000000000 | bytes 1000 | tf_op jit(solution)/shard_map/assemble_body/pallas_call | solution.py:80
  (72 shorter events, 24.6 us)
Async XLA Ops:
  0.7 15.7 %collective-permute-start.1 = (bf16[768,768]{1,0:T(8,128)(2,1)}, bf16[768,768]{1,0:T(8,128)(2,1)S(1)}, u32[]{:S(2)}, u32[]{:S(2)}) collective-permute-start(bf16[768,768]{1,0:T(8,128)(2,1)} %refs_3_.7), channel_id=1, source_target_pairs={{0,1},{1,0},{2,3},{3,2},{4,5},{5,4},{6,7},{7,6},{8,9},{9,8},{10,11... | collective-permute-start | bytes 3538952 | tf_op jit(solution)/shard_map/ppermute | solution.py:817
  1.2 15.2 %collective-permute-start.2 = (bf16[768,768]{1,0:T(8,128)(2,1)}, bf16[768,768]{1,0:T(8,128)(2,1)S(1)}, u32[]{:S(2)}, u32[]{:S(2)}) collective-permute-start(bf16[768,768]{1,0:T(8,128)(2,1)} %refs_2_.4), channel_id=1, source_target_pairs={{0,1},{1,0},{2,3},{3,2},{4,5},{5,4},{6,7},{7,6},{8,9},{9,8},{10,11... | collective-permute-start | bytes 3538952 | tf_op jit(solution)/shard_map/ppermute | solution.py:817
  1.3 15.1 %collective-permute-start.3 = (bf16[1,197,768]{2,1,0:T(8,128)(2,1)}, bf16[1,197,768]{2,1,0:T(8,128)(2,1)S(1)}, u32[]{:S(2)}, u32[]{:S(2)}) collective-permute-start(bf16[1,197,768]{2,1,0:T(8,128)(2,1)} %refs_5_.8), channel_id=1, source_target_pairs={{0,2},{1,3},{2,0},{3,1},{4,6},{5,7},{6,4},{7,5},{8,10},{9,11},{10,... | collective-permute-start | bytes 907784 | tf_op jit(solution)/shard_map/ppermute | solution.py:817
  4.2 10.1 %collective-permute-start.4 = (s32[1,197]{1,0:T(1,128)}, s32[1,197]{1,0:T(1,128)S(1)}, u32[]{:S(2)}, u32[]{:S(2)}) collective-permute-start(s32[1,197]{1,0:T(1,128)} %refs_10_.3), channel_id=1, source_target_pairs={{0,2},{1,3},{2,0},{3,1},{4,6},{5,7},{6,4},{7,5},{8,10},{9,11},{10,... | collective-permute-start | bytes 2372 | tf_op jit(solution)/shard_map/ppermute | solution.py:817
  4.2 12.1 %collective-permute-start = (bf16[768]{0:T(1024)(128)(2,1)}, bf16[768]{0:T(1024)(128)(2,1)S(1)}, u32[]{:S(2)}, u32[]{:S(2)}) collective-permute-start(bf16[768]{0:T(1024)(128)(2,1)} %refs_1_.6), channel_id=1, source_target_pairs={{0,1},{1,0},{2,3},{3,2},{4,5},{5,4},{6,7},{7,6},{8,9},{9,8},{10,11... | collective-permute-start | bytes 4616 | tf_op jit(solution)/shard_map/ppermute | solution.py:817
  4.3 12.6 %copy-start.1 = (bf16[768,768]{1,0:T(8,128)(2,1)S(1)}, bf16[768,768]{1,0:T(8,128)(2,1)}, u32[]{:S(2)}) copy-start(bf16[768,768]{1,0:T(8,128)(2,1)} %refs_2_.4) | copy-start | bytes 3538948
  14.3 10.3 %collective-permute-start.5 = (bf16[208,768]{1,0:T(8,128)(2,1)S(1)}, bf16[208,768]{1,0:T(8,128)(2,1)S(1)}, u32[]{:S(2)}, u32[]{:S(2)}) collective-permute-start(bf16[208,768]{1,0:T(8,128)(2,1)S(1)} %get-tuple-element.115.refs_0_.refs_1_), channel_id=1, source_target_pairs={{0,2},{1,3},{2,0},{3,1},{4,6},{5,7},{6,4},{7,5},{8,10},{9,11},{10,... | collective-permute-start | bytes 958472 | tf_op jit(solution)/shard_map/ppermute | solution.py:817
  21.6 10.7 %collective-permute-start.7 = (bf16[208,768]{1,0:T(8,128)(2,1)}, bf16[208,768]{1,0:T(8,128)(2,1)S(1)}, u32[]{:S(2)}, u32[]{:S(2)}) collective-permute-start(bf16[208,768]{1,0:T(8,128)(2,1)} %get-tuple-element.135), channel_id=1, source_target_pairs={{0,1},{1,0},{2,3},{3,2},{4,5},{5,4},{6,7},{7,6},{8,9},{9,8},{10,11... | collective-permute-start | bytes 958472 | tf_op jit(solution)/shard_map/ppermute | solution.py:817
  27.6 13.0 %collective-permute-start.9 = (bf16[208,768]{1,0:T(8,128)(2,1)S(1)}, bf16[208,768]{1,0:T(8,128)(2,1)S(1)}, u32[]{:S(2)}, u32[]{:S(2)}) collective-permute-start(bf16[208,768]{1,0:T(8,128)(2,1)S(1)} %get-tuple-element.141), channel_id=1, source_target_pairs={{0,2},{1,3},{2,0},{3,1},{4,6},{5,7},{6,4},{7,5},{8,10},{9,11},{10,... | collective-permute-start | bytes 958472 | tf_op jit(solution)/shard_map/ppermute | solution.py:817
  30.8 4.6 %collective-permute-start.6 = (bf16[2,768,768]{2,1,0:T(8,128)(2,1)S(1)}, bf16[2,768,768]{2,1,0:T(8,128)(2,1)S(1)}, u32[]{:S(2)}, u32[]{:S(2)}) collective-permute-start(bf16[2,768,768]{2,1,0:T(8,128)(2,1)S(1)} %get-tuple-element.131), channel_id=1, source_target_pairs={{0,1},{1,0},{2,3},{3,2},{4,5},{5,4},{6,7},{7,6},{8,9},{9,8},{10,11... | collective-permute-start | bytes 7077896 | tf_op jit(solution)/shard_map/ppermute | solution.py:817
  37.5 12.9 %collective-permute-start.10 = (bf16[208,768]{1,0:T(8,128)(2,1)}, bf16[208,768]{1,0:T(8,128)(2,1)S(1)}, u32[]{:S(2)}, u32[]{:S(2)}) collective-permute-start(bf16[208,768]{1,0:T(8,128)(2,1)} %get-tuple-element.154), channel_id=1, source_target_pairs={{0,2},{1,3},{2,0},{3,1},{4,6},{5,7},{6,4},{7,5},{8,10},{9,11},{10,... | collective-permute-start | bytes 958472 | tf_op jit(solution)/shard_map/ppermute | solution.py:817
  37.9 15.5 %collective-permute-start.11 = (bf16[208,768]{1,0:T(8,128)(2,1)}, bf16[208,768]{1,0:T(8,128)(2,1)S(1)}, u32[]{:S(2)}, u32[]{:S(2)}) collective-permute-start(bf16[208,768]{1,0:T(8,128)(2,1)} %get-tuple-element.155), channel_id=1, source_target_pairs={{0,3},{1,2},{2,1},{3,0},{4,7},{5,6},{6,5},{7,4},{8,11},{9,10},{10,... | collective-permute-start | bytes 958472 | tf_op jit(solution)/shard_map/ppermute | solution.py:817
  39.1 28.5 %collective-permute-start.8 = (bf16[2,4,96,768]{3,2,1,0:T(8,128)(2,1)S(1)}, bf16[2,4,96,768]{3,2,1,0:T(8,128)(2,1)S(1)}, u32[]{:S(2)}, u32[]{:S(2)}) collective-permute-start(bf16[2,4,96,768]{3,2,1,0:T(8,128)(2,1)S(1)} %get-tuple-element.139), channel_id=1, source_target_pairs={{0,4},{4,0},{8,12},{12,8},{16,20},{20,16},{24,28},{28,24},{1,5},{5... | collective-permute-start | bytes 3538952 | tf_op jit(solution)/shard_map/ppermute | solution.py:817
  48.8 21.4 %collective-permute-start.13 = (bf16[208,768]{1,0:T(8,128)(2,1)S(1)}, bf16[208,768]{1,0:T(8,128)(2,1)S(1)}, u32[]{:S(2)}, u32[]{:S(2)}) collective-permute-start(bf16[208,768]{1,0:T(8,128)(2,1)S(1)} %get-tuple-element.166), channel_id=1, source_target_pairs={{0,1},{1,0},{2,3},{3,2},{4,5},{5,4},{6,7},{7,6},{8,9},{9,8},{10,11... | collective-permute-start | bytes 958472 | tf_op jit(solution)/shard_map/ppermute | solution.py:817
  49.2 20.9 %collective-permute-start.14 = (bf16[208,768]{1,0:T(8,128)(2,1)S(1)}, bf16[208,768]{1,0:T(8,128)(2,1)S(1)}, u32[]{:S(2)}, u32[]{:S(2)}) collective-permute-start(bf16[208,768]{1,0:T(8,128)(2,1)S(1)} %get-tuple-element.167), channel_id=1, source_target_pairs={{0,2},{1,3},{2,0},{3,1},{4,6},{5,7},{6,4},{7,5},{8,10},{9,11},{10,... | collective-permute-start | bytes 958472 | tf_op jit(solution)/shard_map/ppermute | solution.py:817
  50.5 19.7 %collective-permute-start.15 = (bf16[208,768]{1,0:T(8,128)(2,1)S(1)}, bf16[208,768]{1,0:T(8,128)(2,1)S(1)}, u32[]{:S(2)}, u32[]{:S(2)}) collective-permute-start(bf16[208,768]{1,0:T(8,128)(2,1)S(1)} %get-tuple-element.168), channel_id=1, source_target_pairs={{0,3},{1,2},{2,1},{3,0},{4,7},{5,6},{6,5},{7,4},{8,11},{9,10},{10,... | collective-permute-start | bytes 958472 | tf_op jit(solution)/shard_map/ppermute | solution.py:817
  68.5 15.1 %collective-permute-start.12 = (bf16[2,2,96,768]{3,2,1,0:T(8,128)(2,1)S(1)}, bf16[2,2,96,768]{3,2,1,0:T(8,128)(2,1)S(1)}, u32[]{:S(2)}, u32[]{:S(2)}) collective-permute-start(bf16[2,2,96,768]{3,2,1,0:T(8,128)(2,1)S(1)} %get-tuple-element.163), channel_id=1, source_target_pairs={{0,8},{4,12},{8,0},{12,4},{16,24},{20,28},{24,16},{28,20},{1,9},{5... | collective-permute-start | bytes 1769480 | tf_op jit(solution)/shard_map/ppermute | solution.py:817
  72.2 9.0 %collective-permute-start.16 = (bf16[1,4,96,384]{3,2,1,0:T(8,128)(2,1)S(1)}, bf16[1,4,96,384]{3,2,1,0:T(8,128)(2,1)S(1)}, u32[]{:S(2)}, u32[]{:S(2)}) collective-permute-start(bf16[1,4,96,384]{3,2,1,0:T(8,128)(2,1)S(1)} %get-tuple-element.171), channel_id=1, source_target_pairs={{0,4},{4,0},{8,12},{12,8},{16,20},{20,16},{24,28},{28,24},{1,5},{5... | collective-permute-start | bytes 884744 | tf_op jit(solution)/shard_map/ppermute | solution.py:817
  73.8 1.3 %collective-permute-start.17 = (f32[32,768]{1,0:T(8,128)S(1)}, f32[32,768]{1,0:T(8,128)S(1)}, u32[]{:S(2)}, u32[]{:S(2)}) collective-permute-start(f32[32,768]{1,0:T(8,128)S(1)} %get-tuple-element.175), channel_id=1, source_target_pairs={{0,1},{1,0},{2,3},{3,2},{4,5},{5,4},{6,7},{7,6},{8,9},{9,8},{10,11... | collective-permute-start | bytes 294920 | tf_op jit(solution)/shard_map/ppermute | solution.py:817
  75.1 4.9 %collective-permute-start.18 = (f32[32,768]{1,0:T(8,128)S(1)}, f32[32,768]{1,0:T(8,128)S(1)}, u32[]{:S(2)}, u32[]{:S(2)}) collective-permute-start(f32[32,768]{1,0:T(8,128)S(1)} %add.29), channel_id=1, source_target_pairs={{0,2},{1,3},{2,0},{3,1},{4,6},{5,7},{6,4},{7,5},{8,10},{9,11},{10,... | collective-permute-start | bytes 294920 | tf_op jit(solution)/shard_map/ppermute | solution.py:817
  77.7 13.0 %collective-permute-start.21 = (bf16[1,4,96,384]{3,2,1,0:T(8,128)(2,1)S(1)}, bf16[1,4,96,384]{3,2,1,0:T(8,128)(2,1)S(1)}, u32[]{:S(2)}, u32[]{:S(2)}) collective-permute-start(bf16[1,4,96,384]{3,2,1,0:T(8,128)(2,1)S(1)} %get-tuple-element.181), channel_id=1, source_target_pairs={{0,4},{4,0},{8,12},{12,8},{16,20},{20,16},{24,28},{28,24},{1,5},{5... | collective-permute-start | bytes 884744 | tf_op jit(solution)/shard_map/ppermute | solution.py:817
  84.3 15.7 %collective-permute-start.19 = (bf16[208,768]{1,0:T(8,128)(2,1)}, bf16[208,768]{1,0:T(8,128)(2,1)S(1)}, u32[]{:S(2)}, u32[]{:S(2)}) collective-permute-start(bf16[208,768]{1,0:T(8,128)(2,1)} %get-tuple-element.177), channel_id=1, source_target_pairs={{0,2},{1,3},{2,0},{3,1},{4,6},{5,7},{6,4},{7,5},{8,10},{9,11},{10,... | collective-permute-start | bytes 958472 | tf_op jit(solution)/shard_map/ppermute | solution.py:817
  84.8 6.5 %collective-permute-start.20 = (bf16[1,2,96,384]{3,2,1,0:T(8,128)(2,1)S(1)}, bf16[1,2,96,384]{3,2,1,0:T(8,128)(2,1)S(1)}, u32[]{:S(2)}, u32[]{:S(2)}) collective-permute-start(bf16[1,2,96,384]{3,2,1,0:T(8,128)(2,1)S(1)} %get-tuple-element.179), channel_id=1, source_target_pairs={{0,8},{4,12},{8,0},{12,4},{16,24},{20,28},{24,16},{28,20},{1,9},{5... | collective-permute-start | bytes 442376 | tf_op jit(solution)/shard_map/ppermute | solution.py:817
  86.6 4.8 %collective-permute-start.22 = (f32[32,768]{1,0:T(8,128)S(1)}, f32[32,768]{1,0:T(8,128)S(1)}, u32[]{:S(2)}, u32[]{:S(2)}) collective-permute-start(f32[32,768]{1,0:T(8,128)S(1)} %get-tuple-element.184), channel_id=1, source_target_pairs={{0,4},{4,0},{8,12},{12,8},{16,20},{20,16},{24,28},{28,24},{1,5},{5... | collective-permute-start | bytes 294920 | tf_op jit(solution)/shard_map/ppermute | solution.py:817
  88.1 17.8 %collective-permute-start.26 = (bf16[2,1,96,768]{3,2,1,0:T(8,128)(2,1)S(1)}, bf16[2,1,96,768]{3,2,1,0:T(8,128)(2,1)S(1)}, u32[]{:S(2)}, u32[]{:S(2)}) collective-permute-start(bf16[2,1,96,768]{3,2,1,0:T(8,128)(2,1)S(1)} %get-tuple-element.193), channel_id=1, source_target_pairs={{0,16},{4,20},{8,24},{12,28},{16,0},{20,4},{24,8},{28,12},{1,17},{... | collective-permute-start | bytes 884744 | tf_op jit(solution)/shard_map/ppermute | solution.py:817
  92.0 8.1 %collective-permute-start.23 = (f32[32,768]{1,0:T(8,128)S(1)}, f32[32,768]{1,0:T(8,128)S(1)}, u32[]{:S(2)}, u32[]{:S(2)}) collective-permute-start(f32[32,768]{1,0:T(8,128)S(1)} %get-tuple-element.186), channel_id=1, source_target_pairs={{0,8},{4,12},{8,0},{12,4},{16,24},{20,28},{24,16},{28,20},{1,9},{5... | collective-permute-start | bytes 294920 | tf_op jit(solution)/shard_map/ppermute | solution.py:817
  92.6 9.6 %collective-permute-start.27 = (bf16[1,2,96,384]{3,2,1,0:T(8,128)(2,1)S(1)}, bf16[1,2,96,384]{3,2,1,0:T(8,128)(2,1)S(1)}, u32[]{:S(2)}, u32[]{:S(2)}) collective-permute-start(bf16[1,2,96,384]{3,2,1,0:T(8,128)(2,1)S(1)} %get-tuple-element.195), channel_id=1, source_target_pairs={{0,8},{4,12},{8,0},{12,4},{16,24},{20,28},{24,16},{28,20},{1,9},{5... | collective-permute-start | bytes 442376 | tf_op jit(solution)/shard_map/ppermute | solution.py:817
  94.1 13.1 %collective-permute-start.25 = (bf16[1,1,96,384]{3,2,1,0:T(8,128)(2,1)S(1)}, bf16[1,1,96,384]{3,2,1,0:T(8,128)(2,1)S(1)}, u32[]{:S(2)}, u32[]{:S(2)}) collective-permute-start(bf16[1,1,96,384]{3,2,1,0:T(8,128)(2,1)S(1)} %get-tuple-element.191), channel_id=1, source_target_pairs={{0,16},{4,20},{8,24},{12,28},{16,0},{20,4},{24,8},{28,12},{1,17},{... | collective-permute-start | bytes 221192 | tf_op jit(solution)/shard_map/ppermute | solution.py:817
  102.8 5.3 %collective-permute-start.28 = (bf16[1,1,96,384]{3,2,1,0:T(8,128)(2,1)S(1)}, bf16[1,1,96,384]{3,2,1,0:T(8,128)(2,1)S(1)}, u32[]{:S(2)}, u32[]{:S(2)}) collective-permute-start(bf16[1,1,96,384]{3,2,1,0:T(8,128)(2,1)S(1)} %get-tuple-element.201), channel_id=1, source_target_pairs={{0,16},{4,20},{8,24},{12,28},{16,0},{20,4},{24,8},{28,12},{1,17},{... | collective-permute-start | bytes 221192 | tf_op jit(solution)/shard_map/ppermute | solution.py:817
  108.2 7.1 %collective-permute-start.29 = (bf16[96,768]{1,0:T(8,128)(2,1)S(1)}, bf16[96,768]{1,0:T(8,128)(2,1)S(1)}, u32[]{:S(2)}, u32[]{:S(2)}) collective-permute-start(bf16[96,768]{1,0:T(8,128)(2,1)S(1)} %get-tuple-element.203.refs_1_), channel_id=1, source_target_pairs={{0,2},{1,3},{2,0},{3,1},{4,6},{5,7},{6,4},{7,5},{8,10},{9,11},{10,... | collective-permute-start | bytes 442376 | tf_op jit(solution)/shard_map/ppermute | solution.py:817
  109.7 5.5 %collective-permute-start.24 = (f32[32,768]{1,0:T(8,128)S(1)}, f32[32,768]{1,0:T(8,128)S(1)}, u32[]{:S(2)}, u32[]{:S(2)}) collective-permute-start(f32[32,768]{1,0:T(8,128)S(1)} %get-tuple-element.189), channel_id=1, source_target_pairs={{0,16},{4,20},{8,24},{12,28},{16,0},{20,4},{24,8},{28,12},{1,17},{... | collective-permute-start | bytes 294920 | tf_op jit(solution)/shard_map/ppermute | solution.py:817
  115.3 1.6 %collective-permute-start.30 = (bf16[2,96,768]{2,1,0:T(8,128)(2,1)S(1)}, bf16[2,96,768]{2,1,0:T(8,128)(2,1)S(1)}, u32[]{:S(2)}, u32[]{:S(2)}) collective-permute-start(bf16[2,96,768]{2,1,0:T(8,128)(2,1)S(1)} %pad_maximum_fusion), channel_id=1, source_target_pairs={{0,1},{1,0},{2,3},{3,2},{4,5},{5,4},{6,7},{7,6},{8,9},{9,8},{10,11... | collective-permute-start | bytes 884744 | tf_op jit(solution)/shard_map/ppermute | solution.py:817
  (3 other events, 17.5 us)

commit v4 on v3

--- a/solution.py
+++ b/solution.py
@@ -12,6 +12,10 @@
 EPS = 1e-06
 LANES = 128
 SCALE = 1
+COST = dict(fwd=1, mlp=5, far=30, pair=0.42, keep=0.6, back=5, norm=5, table=3.2, late=1.2, fold=0.4, last=0.4, end=0.2, join=1)
+ORDER = (
+    "N", "T", "f1", "A", "B", "x", "a1", "f2@%", "h", "y", "b1", "a2@", "z", "b2", "E@", "w", "F", "S", "J",
+)
 UNROLL_F = 6
 UNROLL_B = 6
 VMEM_LIMIT = 16 * 1024 * 1024
@@ -60,23 +64,25 @@
 }
 
 
-def call(body, outs, kinds, values, scratch=(), cost=1, deps=(), carry=()):
+def call(body, outs, kinds, values, scratch=(), cost=1, deps=(), carry=(), hold=()):
     specs, given = [], []
     for kind, value in zip(kinds, values, strict=True):
         keep, space = SPACES[kind]
         specs.append(pl.BlockSpec(memory_space=space))
         given.append(value if keep is None else pltpu.with_memory_space_constraint(value, keep))
     outs = outs if isinstance(outs, tuple) else (outs,)
-    n_in, n_more, n_out = len(given), len(deps) + len(carry), len(outs)
+    passed = tuple(carry) + tuple(hold)
+    n_in, n_more, n_out = len(given), len(deps) + len(passed), len(outs)
 
     def inner(*refs):
         rest = refs[n_in + n_more :]
         rest[n_out][...] = jnp.zeros_like(rest[n_out])
-        body(*refs[:n_in], *rest[:n_out], *rest[n_out + 1 + len(carry) :])
+        body(*refs[:n_in], *rest[:n_out], *rest[n_out + 1 + len(passed) :])
 
     anywhere = pl.BlockSpec(memory_space=pl.ANY)
     whole = pl.BlockSpec(memory_space=pltpu.VMEM)
     in_hbm = [value.dtype == BF16 and len(value.shape) == 2 for value in carry]
+    held = tuple(pltpu.with_memory_space_constraint(value, pltpu.VMEM) for value in hold)
     out = pl.pallas_call(
         inner,
         name=getattr(body, "func", body).__name__,
@@ -85,10 +91,11 @@
         + tuple(
             (pltpu.HBM if pinned else jax.ShapeDtypeStruct)(c.shape, c.dtype)
             for pinned, c in zip(in_hbm, carry)
-        ),
+        )
+        + tuple(pltpu.VMEM(value.shape, value.dtype) for value in hold),
         in_specs=specs + [anywhere] * n_more,
-        out_specs=(whole,) * (n_out + 1) + (anywhere,) * len(carry),
-        input_output_aliases={n_in + len(deps) + at: n_out + 1 + at for at in range(len(carry))},
+        out_specs=(whole,) * (n_out + 1) + (anywhere,) * len(passed),
+        input_output_aliases={n_in + len(deps) + at: n_out + 1 + at for at in range(len(passed))},
         scratch_shapes=list(scratch),
         compiler_params=pltpu.CompilerParams(vmem_limit_bytes=VMEM_LIMIT),
         cost_estimate=pl.CostEstimate(
@@ -101,6 +108,7 @@
             pltpu.with_memory_space_constraint(c, pltpu.HBM) if pinned else c
             for pinned, c in zip(in_hbm, carry)
         ),
+        *held,
     )
     results = out[:n_out] + out[n_out + 1 :]
     return (results if len(results) > 1 else results[0]), out[n_out]
@@ -286,10 +294,10 @@
         shape_out((pad, width), BF16),
         shape_out((pad, width), BF16),
         shape_out((pad, width), BF16),
-        shape_out((keys, width), BF16),
-        shape_out((keys, width), BF16),
-        shape_out((heads, pad, keys), BF16),
-        shape_out((pad, width), F32),
+        shape((keys, width), BF16),
+        shape((keys, width), BF16),
+        shape((heads, pad, keys), BF16),
+        shape((pad, width), F32),
         shape_out((pad, width), F32),
         shape((pad, width), BF16),
     )
@@ -371,7 +379,7 @@
     sums_ref[4:8, :] = jnp.zeros_like(sums_ref[4:8, :])
 
 
-def mlp(inner, weights, bias, given, first, deps=(), carry=()):
+def mlp(inner, weights, bias, given, first, deps=(), carry=(), hold=()):
     pad, width = inner.shape
     ff = weights[2].shape[1]
     kind = F32 if first else BF16
@@ -386,7 +394,7 @@
         scratch = (pltpu.VMEM((pad, width), F32), pltpu.VMEM((LANES, round_up(pad, LANES)), F32))
     return call(
         functools.partial(mlp_body, first), outs, "vhhvvvvh" + ("hvhvh" if first else "v"),
-        (inner, *weights, bias, *given), scratch, cost=5, deps=deps, carry=carry,
+        (inner, *weights, bias, *given), scratch, cost=COST["mlp"], deps=deps, carry=carry, hold=hold,
     )
 
 
@@ -397,11 +405,11 @@
     sums_ref[2:3, :] = jnp.sum(cot_ref[...] * branch, axis=0, keepdims=True)
 
 
-def far_branch(acta, actb, w2a, w2b, cotangent, deps=()):
+def far_branch(acta, actb, w2a, w2b, cotangent, deps=(), hold=()):
     pad, width = cotangent.shape
     return call(
         far_branch_body, (shape_out((pad, width), BF16), shape((8, width), F32)), "vvvvv",
-        (acta, actb, w2a, w2b, cotangent), cost=30, deps=deps,
+        (acta, actb, w2a, w2b, cotangent), cost=COST["far"], deps=deps, hold=hold,
     )
 
 
@@ -421,11 +429,11 @@
         out_ref[at] = total.astype(BF16)
 
 
-def pair_grad(one, two, deps=(), carry=()):
+def pair_grad(one, two, deps=(), carry=(), hold=()):
     width, ff = one[0].shape[1], one[2].shape[1]
     return call(
-        pair_grad_body, shape((2, width, ff), BF16), "v" * 8, (*one, *two), cost=0.7, deps=deps,
-        carry=carry,
+        pair_grad_body, shape((2, width, ff), BF16), "v" * 8, (*one, *two), cost=COST["pair"], deps=deps,
+        carry=carry, hold=hold,
     )
 
 
@@ -440,12 +448,12 @@
         )
 
 
-def fc_keep(where, block, one, two, other, deps=(), carry=()):
+def fc_keep(where, block, one, two, other, deps=(), carry=(), hold=()):
     width, ff = one[0].shape[1], one[2].shape[1]
     outs = (shape((2, width // (2 * block), block, ff), BF16),) * 2
     return call(
         functools.partial(fc_keep_body, block), outs, "s" + "v" * 9, (where, *one, *two, other),
-        cost=1.2, deps=deps, carry=carry,
+        cost=COST["keep"], deps=deps, carry=carry, hold=hold,
     )
 
 
@@ -572,11 +580,11 @@
     return call(
         functools.partial(backward_body, heads),
         outs,
-        "svvhhhhhhhhhhh",
+        "svvhvhhhhhhvvv",
         (where, dinner0, dinner1, hidden, attended, out_grad, mask_col, gain2, gamma1, wproj, q, k,
          v, probs),
         (pltpu.VMEM((pad, width), F32), pltpu.VMEM((pad, width), BF16)),
-        cost=5,
+        cost=COST["back"],
         deps=deps,
     )
 
@@ -598,14 +606,14 @@
     sums_ref[3:8, :] = jnp.zeros((5, width), F32)
 
 
-def first_norm(patches, mask_col, token, gain1, dqkv, wqkv, dhidden, deps=()):
+def first_norm(patches, mask_col, token, gain1, dqkv, wqkv, dhidden, deps=(), carry=()):
     rows, width = patches.shape[1:]
     pad = mask_col.shape[0]
     outs = (shape_out((1, rows, width), F32), shape((8, width), F32))
     return call(
         first_norm_body, outs, "hhhhvhv",
         (patches, mask_col, token, gain1, dqkv, wqkv, dhidden),
-        (pltpu.VMEM((pad, width), F32),), cost=5, deps=deps,
+        (pltpu.VMEM((pad, width), F32),), cost=COST["norm"], deps=deps, carry=carry,
     )
 
 
@@ -618,7 +626,7 @@
 def layer_end(rows, hidden, branch0, branch1, gamma2, deps=(), carry=()):
     return call(
         layer_end_body, shape_out((1, rows, hidden.shape[1]), BF16), "hhvh",
-        (hidden, branch0, branch1, gamma2), deps=deps, carry=carry,
+        (hidden, branch0, branch1, gamma2), cost=COST["end"], deps=deps, carry=carry,
     )
 
 
@@ -682,7 +690,7 @@
         table_grad_body, shape((head_pad + 16, width), F32), "shvvvvvv",
         (where, rel_index, dscores, sums_b, sums_n, sums0, sums1, sums_f),
         (pltpu.VMEM((pad, keys), jnp.int32), pltpu.VMEM((high_count * head_pad, LANES), F32)),
-        cost=3.2, deps=deps,
+        cost=COST["table"], deps=deps,
     )
 
 
@@ -702,7 +710,7 @@
     outs = (shape((1, width // (2 * block), block, half), BF16),) * 2
     return call(
         functools.partial(late_grad_body, block, piece), outs, "shvvvvvvv",
-        (where, *lefts, *rights), cost=1.2, deps=deps, carry=carry,
+        (where, *lefts, *rights), cost=COST["late"], deps=deps, carry=carry,
     )
 
 
@@ -722,7 +730,7 @@
     items, count, block, width = keep.shape
     return call(
         functools.partial(fold_body, bit), (shape((items, count // 2, block, width), BF16),) * 2,
-        "svv", (where, keep, met), cost=0.4, deps=deps, carry=carry,
+        "svv", (where, keep, met), cost=COST["fold"], deps=deps, carry=carry,
     )
 
 
@@ -735,7 +743,7 @@
 def last_sum(keep, met, kind, deps=(), carry=()):
     make = shape_out if kind == F32 else shape
     return call(
-        last_sum_body, (make(keep.shape[2:], kind),) * keep.shape[0], "vv", (keep, met), cost=0.4,
+        last_sum_body, (make(keep.shape[2:], kind),) * keep.shape[0], "vv", (keep, met), cost=COST["last"],
         deps=deps, carry=carry,
     )
 
@@ -749,7 +757,7 @@
 def join(before, keep, met, deps=(), carry=()):
     block, half = before.shape
     return call(
-        join_body, shape((block, 2 * half), BF16), "vvv", (before, keep, met), deps=deps,
+        join_body, shape((block, 2 * half), BF16), "vvv", (before, keep, met), cost=COST["join"], deps=deps,
         carry=carry,
     )
 
@@ -834,14 +842,23 @@
         query_bias, value_bias, rel_table.T, proj_bias, gamma1, ln2_gain, ln2_bias, qkv_weight,
         proj_weight,
     )
+    held = [k, v, probs, attended]
+
+    def holding(kernel, *args, **more):
+        out = step(kernel, *args, hold=tuple(held), **more)
+        count = len(held)
+        held[:] = out[-count:]
+        out = tuple(out[:-count])
+        return out if len(out) > 1 else out[0]
+
     inner1 = over_x(inner)
     weights = (fc1_bias, b1b, fc1_weight, w1b, fc2_weight, w2b)
-    dbranch, dbranch1, cot1, acta0, actb0, dprea0, dpreb0, dinner0, sums0, branch0, left1 = step(
+    dbranch, dbranch1, cot1, acta0, actb0, dprea0, dpreb0, dinner0, sums0, branch0, left1 = holding(
         mlp, inner, weights, fc2_bias, (out_grad, out_grad1, row_mask, row_mask1, gamma2), True,
         carry=(left1,),
     )
     met_left1 = over_core(left1)
-    acta1, actb1, dprea1, dpreb1, dinner1, sums1 = step(
+    acta1, actb1, dprea1, dpreb1, dinner1, sums1 = holding(
         mlp, inner1, weights, fc2_bias, (dbranch1,), False
     )
     dinner_in = over_x(dinner1)
@@ -855,65 +872,90 @@
         return keep, met
 
     fc_other = over_core(
-        step(pair_grad, (inner, inner1, dpreb0, dpreb1), (dbranch, dbranch1, actb0, actb1))
-    )
-    branch1, sums_f = step(far_branch, acta1, actb1, fc2_weight, w2b, cot1)
-    fc_send, fc_kept, left2, left3 = step(
+        holding(pair_grad, (inner, inner1, dpreb0, dpreb1), (dbranch, dbranch1, actb0, actb1))
+    )
+    branch1, sums_f = holding(far_branch, acta1, actb1, fc2_weight, w2b, cot1)
+    fc_send, fc_kept, left2, left3 = holding(
         fc_keep, where, block, (inner, inner1, dprea0, dprea1), (dbranch, dbranch1, acta0, acta1),
         fc_other, deps=(met_left1,), carry=(left2, left3),
     )
     fc_met = over_bit[0](fc_send)
     met_left2, met_left3 = over_x(left2), swap("mp", 3)(left3)
+    k, v, probs, attended = held
 
     dhidden, dqkv, own, core, far, corner, dscores, sums_b = step(
         backward, heads, where, dinner0, dinner_in, hidden, attended, out_grad, mask_col, ln2_gain,
         gamma1, proj_weight, q, k, v, probs,
     )
     met_far, met_corner, met_core = over_x(far), swap("mp", 3)(corner), over_core(core)
-    patch_grad, sums_n = step(
-        first_norm, patches, mask_col, mask_token, ln1_gain, dqkv, qkv_weight, dhidden,
-        deps=(met_left2, met_left3),
-    )
     head_pad = 16
-    ds = jnp.pad(jnp.transpose(dscores, (1, 0, 2)), ((0, 0), (0, head_pad - heads), (0, 0)))
-    small = step(table_grad, where, rel_index, ds, sums_b, sums_n, sums0, sums1, sums_f,
-                 entries)
-    small = small + over_core(small)
-    fc_kept, fc_met = middle(fc_kept, fc_met, 1, 2)
-
     late = ((left0, met_left1, met_left2, met_left3), (own, met_core, met_far, met_corner))
-    late0_send, late0_keep = step(late_grad, where, block, 0, *late)
-    late0_met = over_bit[0](late0_send)
-    late1_send, late1_keep = step(late_grad, where, block, 1, *late)
-    late1_met = over_bit[0](late1_send)
-    small = small + over_x(small)
-
-    late0_send, late0_keep = step(fold, where, 1, late0_keep, late0_met)
-    late0_met = over_bit[1](late0_send)
-    fc_send, fc_kept, small, branch1 = step(
-        fold, where, 2, fc_kept, fc_met, carry=(small, branch1)
-    )
-    fc_met = over_bit[2](fc_send)
-    fc_kept, fc_met = middle(fc_kept, fc_met, 3, bits)
-    branch_in = over_x(branch1)
-    small = small + over_bit[0](small)
-    late1_send, late1_keep = step(fold, where, 1, late1_keep, late1_met)
-    late1_met = over_bit[1](late1_send)
-    late0_send, late0_keep, small = step(
-        fold, where, 2, late0_keep, late0_met, carry=(small,)
-    )
-    late0_met = over_bit[2](late0_send)
-    late0_keep, late0_met = middle(late0_keep, late0_met, 3, bits)
-    small = small + over_bit[1](small)
-    layer_out, small = step(layer_end, rows, hidden, branch0, branch_in, gamma2, carry=(small,))
-    late1_keep, late1_met = middle(late1_keep, late1_met, 2, bits)
-    for bit in range(2, bits):
-        small = small + over_bit[bit](small)
-    fc1_weight_grad, fc2_weight_grad = step(last_sum, fc_kept, fc_met, F32)
-    late0_own = step(last_sum, late0_keep, late0_met, BF16)
-    late_own = step(join, late0_own, late1_keep, late1_met)
-    late_x = over_x(late_own)
-
+    keep, met, made = {"f": fc_kept}, {"f": fc_met}, {}
+    state = {"small": None, "branch": branch1, "own": None}
+
+    def tailed(mark, kernel, *args, **more):
+        names = [name for sign, name in (("@", "small"), ("%", "branch"), ("!", "own")) if sign in mark]
+        carried = tuple(state[name] for name in names)
+        out = step(kernel, *args, carry=carried, **more)
+        if not names:
+            return out
+        state.update(zip(names, out[-len(names) :]))
+        out = tuple(out[: -len(names)])
+        return out if len(out) > 1 else out[0]
+
+    def spread_on(name, mark, first, last):
+        for bit in range(first, last):
+            send, keep[name] = tailed(mark if bit == first else "", fold, where, bit, keep[name], met[name])
+            met[name] = over_bit[bit](send)
+
+    def hop(swaps):
+        for swapped in swaps:
+            state["small"] = state["small"] + swapped(state["small"])
+
+    for item in ORDER:
+        name, mark = item.rstrip("@%!"), item[len(item.rstrip("@%!")) :]
+        if name == "N":
+            made["patch"], made["sums"] = tailed(
+                mark, first_norm, patches, mask_col, mask_token, ln1_gain, dqkv, qkv_weight, dhidden,
+                deps=(met_left2, met_left3),
+            )
+        elif name == "T":
+            ds = jnp.pad(
+                jnp.transpose(dscores, (1, 0, 2)), ((0, 0), (0, head_pad - heads), (0, 0))
+            )
+            state["small"] = step(
+                table_grad, where, rel_index, ds, sums_b, made["sums"], sums0, sums1, sums_f, entries
+            )
+            hop([over_core])
+        elif name in ("A", "B"):
+            send, keep[name] = tailed(mark, late_grad, where, block, "AB".index(name), *late)
+            met[name] = over_bit[0](send)
+        elif name in ("f1", "a1", "b1"):
+            spread_on(name[0].upper() if name[0] != "f" else "f", mark, 1, 2)
+        elif name in ("f2", "a2", "b2"):
+            spread_on(name[0].upper() if name[0] != "f" else "f", mark, 2, bits)
+        elif name == "x":
+            hop([over_x])
+        elif name == "y":
+            hop([over_bit[0]])
+        elif name == "z":
+            hop([over_bit[1]])
+        elif name == "w":
+            hop(over_bit[2:])
+        elif name == "h":
+            made["branch"] = over_x(state["branch"])
+        elif name == "E":
+            made["layer"] = tailed(mark, layer_end, rows, hidden, branch0, made["branch"], gamma2)
+        elif name == "F":
+            made["fc"] = tailed(mark, last_sum, keep["f"], met["f"], F32)
+        elif name == "S":
+            made["A"] = tailed(mark, last_sum, keep["A"], met["A"], BF16)
+        elif name == "J":
+            state["own"] = tailed(mark, join, made["A"], keep["B"], met["B"])
+            late_x = over_x(state["own"])
+    small, late_own = state["small"], state["own"]
+    patch_grad, layer_out = made["patch"], made["layer"]
+    fc1_weight_grad, fc2_weight_grad = made["fc"]
     late_pair = over_core(jnp.stack([late_own, late_x]))
     qkv_weight_grad, proj_weight_grad = step(assemble, where, late_own, late_x, late_pair)
 

time: 121 us -> 117 us (0.967); the launches traced: 119 us -> 117 us
  Pallas kernels: 54.4 us -> 52.7 us
    pallas_call x22, Pallas kernels: 54.4 us -> 52.7 us  [call(): pl.pallas_call(inner, name=getattr(body, 'func', body).__name__, out_shap...]
  transfers between devices with their start and end apart: 31 -> 31, of which waited for: 14 -> 11; matrix products, arithmetic and copies ran while one was open for 3% -> 3% of each run, Pallas kernels for 44% -> 44%
where the time goes in v4:
time: 117 us
  Pallas kernels  52.7 us (45%)
  starting transfers between devices  34.6 us (30%)
  waiting for transfers between devices  24.1 us (21%)
  local copies, waits for them, and re-layouts  4.07 us (3%)
    pallas_call x22, Pallas kernels, call(): pl.pallas_call(inner, name=getattr(body, 'func', body).__name__, out_shap...  52.7 us
    ppermute x31, starting transfers between devices, swap(): return lambda value: lax.ppermute(value, axis, pairs)  34.6 us
    ppermute x31, waiting for transfers between devices, swap(): return lambda value: lax.ppermute(value, axis, pairs)  24.1 us
  transfers between devices with their start and end apart: 31, of which 11 were waited for; matrix products, arithmetic and copies ran while one was open for 3% of the time, Pallas kernels for 44%

profile of v4, /device:TPU:0, one launch (start us, length us, event | category | flops | bytes accessed | tf_op | source)
XLA Modules:
  0.0 116.5 jit_solution(9223510186736844141)
XLA Ops:
  1.3 2.9 %collective-permute-start.3 = (bf16[1,197,768]{2,1,0:T(8,128)(2,1)}, bf16[1,197,768]{2,1,0:T(8,128)(2,1)S(1)}, u32[]{:S(2)}, u32[]{:S(2)}) collective-permute-start(bf16[1,197,768]{2,1,0:T(8,128)(2,1)} %refs_5_.8), channel_id=1, source_target_pairs={{0,2},{1,3},{2,0},{3,1},{4,6},{5,7},{6,4},{7,5},{8,10},{9,11},{10,... | collective-permute-start | bytes 907784 | tf_op jit(solution)/shard_map/ppermute | solution.py:825
  4.3 9.1 %forward_body.1 = (f32[208,128]{1,0:T(8,128)}, bf16[208,768]{1,0:T(8,128)(2,1)}, bf16[208,768]{1,0:T(8,128)(2,1)}, bf16[208,768]{1,0:T(8,128)(2,1)}, bf16[208,76...) custom-call(s32[5]{0:T(128)S(1)} %stack.32.refs_0_, ...), custom_call_target="tpu_custom_call" | custom-call | flops 1000000000 | bytes 1000 | tf_op jit(solution)/shard_map/forward_body/pallas_call | solution.py:86
  13.4 2.1 %collective-permute-start.5 = (bf16[208,768]{1,0:T(8,128)(2,1)S(1)}, bf16[208,768]{1,0:T(8,128)(2,1)S(1)}, u32[]{:S(2)}, u32[]{:S(2)}) collective-permute-start(bf16[208,768]{1,0:T(8,128)(2,1)S(1)} %get-tuple-element.135.refs_0_.refs_1_), channel_id=1, source_target_pairs={{0,2},{1,3},{2,0},{3,1},{4,6},{5,7},{6,4},{7,5},{8,10},{9,11},{10,... | collective-permute-start | bytes 958472 | tf_op jit(solution)/shard_map/ppermute | solution.py:825
  16.1 4.7 %mlp_body.2 = (bf16[208,768]{1,0:T(8,128)(2,1)S(1)}, bf16[208,768]{1,0:T(8,128)(2,1)S(1)}, f32[208,768]{1,0:T(8,128)S(1)}, bf16[208,768]{1,0:T(8,128)(2,1)S(1)},...) custom-call(bf16[208,768]{1,0:T(8,128)(2,1)S(1)} %get-tuple-element., ...), custom_call_target="tpu_custom_call", output_to_operand_aliasing={{11}: (14, {}), {12}: (15, {}), {13}: (16, {}), {14}: (17, ... | custom-call | flops 5000000000 | bytes 1000 | tf_op jit(solution)/shard_map/mlp_body/pallas_call | solution.py:86
  21.0 2.7 %collective-permute-done.5.refs_0_.refs_1_.refs_2_ = bf16[208,768]{1,0:T(8,128)(2,1)S(1)} collective-permute-done((bf16[208,768]{1,0:T(8,128)(2,1)S(1)}, bf16[208,768]{1,0:T(8,128)(2,1)S(1)}, u32[]{:S(2)}, u32[]{:S(2)}) %collective-permute-start.5) | collective-permute-done | bytes 319520 | tf_op jit(solution)/shard_map/ppermute | solution.py:825
  23.7 3.0 %mlp_body.3 = (bf16[208,768]{1,0:T(8,128)(2,1)S(1)}, bf16[208,768]{1,0:T(8,128)(2,1)S(1)}, bf16[208,768]{1,0:T(8,128)(2,1)S(1)}, bf16[208,768]{1,0:T(8,128)(2,1)...) custom-call(bf16[208,768]{1,0:T(8,128)(2,1)S(1)} %collective-permute, ...), custom_call_target="tpu_custom_call", output_to_operand_aliasing={{7}: (10, {}), {8}: (11, {}), {9}: (12, {}), {10}: (13, {})} | custom-call | flops 5000000000 | bytes 1000 | tf_op jit(solution)/shard_map/mlp_body/pallas_call | solution.py:86
  26.7 1.8 %collective-permute-start.9 = (bf16[208,768]{1,0:T(8,128)(2,1)S(1)}, bf16[208,768]{1,0:T(8,128)(2,1)S(1)}, u32[]{:S(2)}, u32[]{:S(2)}) collective-permute-start(bf16[208,768]{1,0:T(8,128)(2,1)S(1)} %get-tuple-element.181), channel_id=1, source_target_pairs={{0,2},{1,3},{2,0},{3,1},{4,6},{5,7},{6,4},{7,5},{8,10},{9,11},{10,... | collective-permute-start | bytes 958472 | tf_op jit(solution)/shard_map/ppermute | solution.py:825
  28.5 1.4 %pair_grad_body.1 = (bf16[2,768,768]{2,1,0:T(8,128)(2,1)S(1)}, f32[8,128]{1,0:T(8,128)S(1)}, bf16[256,768]{1,0:T(8,128)(2,1)S(1)}, bf16[256,768]{1,0:T(8,128)(2,...) custom-call(bf16[208,768]{1,0:T(8,128)(2,1)S(1)} %get-tuple-element., ...), custom_call_target="tpu_custom_call", output_to_operand_aliasing={{2}: (9, {}), {3}: (10, {}), {4}: (11, {}), {5}: (12, {})} | custom-call | flops 420000000 | bytes 1000 | tf_op jit(solution)/shard_map/pair_grad_body/pallas_call | solution.py:86
  31.5 3.1 %collective-permute-done.6.refs_9_ = bf16[2,768,768]{2,1,0:T(8,128)(2,1)S(1)} collective-permute-done((bf16[2,768,768]{2,1,0:T(8,128)(2,1)S(1)}, bf16[2,768,768]{2,1,0:T(8,128)(2,1)S(1)}, u32[]{:S(2)}, u32[]{:S(2)}) %collective-permute-start.6) | collective-permute-done | bytes 2359328 | tf_op jit(solution)/shard_map/ppermute | solution.py:825
  34.6 2.0 %fc_keep_body.1 = (bf16[2,4,96,768]{3,2,1,0:T(8,128)(2,1)S(1)}, bf16[2,4,96,768]{3,2,1,0:T(8,128)(2,1)S(1)}, f32[8,128]{1,0:T(8,128)S(1)}, bf16[208,768]{1,0:T(8...) custom-call(s32[5]{0:T(128)S(1)} %stack.32.refs_0_, ...), custom_call_target="tpu_custom_call", output_to_operand_aliasing={{3}: (12, {}), {4}: (13, {}), {5}: (14, {}), {6}: (15, {}),... | custom-call | flops 600000000 | bytes 1000 | tf_op jit(solution)/shard_map/fc_keep_body/pallas_call | solution.py:86
  38.2 1.5 %collective-permute-start.8 = (bf16[2,4,96,768]{3,2,1,0:T(8,128)(2,1)S(1)}, bf16[2,4,96,768]{3,2,1,0:T(8,128)(2,1)S(1)}, u32[]{:S(2)}, u32[]{:S(2)}) collective-permute-start(bf16[2,4,96,768]{3,2,1,0:T(8,128)(2,1)S(1)} %get-tuple-element.179), channel_id=1, source_target_pairs={{0,4},{4,0},{8,12},{12,8},{16,20},{20,16},{24,28},{28,24},{1,5},{5... | collective-permute-start | bytes 3538952 | tf_op jit(solution)/shard_map/ppermute | solution.py:825
  39.7 7.4 %backward_body.1 = (f32[208,768]{1,0:T(8,128)S(1)}, bf16[208,2304]{1,0:T(8,128)(2,1)S(1)}, bf16[208,768]{1,0:T(8,128)(2,1)S(1)}, bf16[208,768]{1,0:T(8,128)(2,1)...) custom-call(s32[5]{0:T(128)S(1)} %stack.32.refs_0_, ...), custom_call_target="tpu_custom_call" | custom-call | flops 5000000000 | bytes 1000 | tf_op jit(solution)/shard_map/backward_body/pallas_call | solution.py:86
  49.8 2.8 %collective-permute-done.11.refs_9_.refs_4_ = bf16[208,768]{1,0:T(8,128)(2,1)S(1)} collective-permute-done((bf16[208,768]{1,0:T(8,128)(2,1)}, bf16[208,768]{1,0:T(8,128)(2,1)S(1)}, u32[]{:S(2)}, u32[]{:S(2)}) %collective-permute-start.11) | collective-permute-done | bytes 319520 | tf_op jit(solution)/shard_map/ppermute | solution.py:825
  52.5 4.6 %first_norm_body.1 = (f32[1,197,768]{2,1,0:T(8,128)}, f32[8,768]{1,0:T(8,128)S(1)}, f32[8,128]{1,0:T(8,128)S(1)}) custom-call(bf16[1,197,768]{2,1,0:T(8,128)(2,1)} %refs_0_.1, f32[208,128]{1,0:T(8,128)} %get-tuple-element.183.refs_6_.refs_1_, f32[768]{0:T(1024)} %refs_2_.5, f32[768]{0:T(1024)} %refs_3_.8, bf16[208,2304]{1,0:T(8,128)(2,1)S(1)} %get-tuple-element.191.refs_4_, ...), custom_call_target="tpu_custom_call" | custom-call | flops 5000000000 | bytes 1000 | tf_op jit(solution)/shard_map/first_norm_body/pallas_call | solution.py:86
  57.1 6.3 %table_grad_body.1 = (f32[32,768]{1,0:T(8,128)S(1)}, f32[8,128]{1,0:T(8,128)S(1)}) custom-call(s32[5]{0:T(128)S(1)} %stack.32.refs_0_, s32[197,197]{1,0:T(8,128)} %refs_1_.7, bf16[208,16,256]{2,1,0:T(8,128)(2,1)S(1)} %pad.4.refs_2_, f32[8,768]{1,0:T(8,128)S(1)} %get-tuple-element.190.refs_3_, f32[8,768]{1,0:T(8,128)S(1)} %get-tuple-element.196.refs_4_, ...), custom_call_target="tpu_custom_call" | custom-call | flops 3200000000 | bytes 1000 | tf_op jit(solution)/shard_map/table_grad_body/pallas_call | solution.py:86
  63.4 3.3 %collective-permute-done.8.refs_2_ = bf16[2,4,96,768]{3,2,1,0:T(8,128)(2,1)S(1)} collective-permute-done((bf16[2,4,96,768]{3,2,1,0:T(8,128)(2,1)S(1)}, bf16[2,4,96,768]{3,2,1,0:T(8,128)(2,1)S(1)}, u32[]{:S(2)}, u32[]{:S(2)}) %collective-permute-start.8) | collective-permute-done | bytes 1179680 | tf_op jit(solution)/shard_map/ppermute | solution.py:825
  67.6 1.7 %collective-permute-start.12 = (bf16[2,2,96,768]{3,2,1,0:T(8,128)(2,1)S(1)}, bf16[2,2,96,768]{3,2,1,0:T(8,128)(2,1)S(1)}, u32[]{:S(2)}, u32[]{:S(2)}) collective-permute-start(bf16[2,2,96,768]{3,2,1,0:T(8,128)(2,1)S(1)} %get-tuple-element.203), channel_id=1, source_target_pairs={{0,8},{4,12},{8,0},{12,4},{16,24},{20,28},{24,16},{28,20},{1,9},{5... | collective-permute-start | bytes 1769480 | tf_op jit(solution)/shard_map/ppermute | solution.py:825
  69.3 2.0 %late_grad_body.2 = (bf16[1,4,96,384]{3,2,1,0:T(8,128)(2,1)S(1)}, bf16[1,4,96,384]{3,2,1,0:T(8,128)(2,1)S(1)}, f32[8,128]{1,0:T(8,128)S(1)}) custom-call(s32[5]{0:T(128)S(1)} %stack.32.refs_0_, bf16[208,768]{1,0:T(8,128)(2,1)} %get-tuple-element.204.refs_1_, bf16[208,768]{1,0:T(8,128)(2,1)S(1)} %collective-permute-done.7.refs_11_.refs_2_, ...), custom_call_target="tpu_custom_call" | custom-call | flops 1200000000 | bytes 1000 | tf_op jit(solution)/shard_map/late_grad_body/pallas_call | solution.py:86
  71.4 1.6 %collective-permute-start.16 = (bf16[1,4,96,384]{3,2,1,0:T(8,128)(2,1)S(1)}, bf16[1,4,96,384]{3,2,1,0:T(8,128)(2,1)S(1)}, u32[]{:S(2)}, u32[]{:S(2)}) collective-permute-start(bf16[1,4,96,384]{3,2,1,0:T(8,128)(2,1)S(1)} %get-tuple-element.211), channel_id=1, source_target_pairs={{0,4},{4,0},{8,12},{12,8},{16,20},{20,16},{24,28},{28,24},{1,5},{5... | collective-permute-start | bytes 884744 | tf_op jit(solution)/shard_map/ppermute | solution.py:825
  72.9 2.0 %late_grad_body.3 = (bf16[1,4,96,384]{3,2,1,0:T(8,128)(2,1)S(1)}, bf16[1,4,96,384]{3,2,1,0:T(8,128)(2,1)S(1)}, f32[8,128]{1,0:T(8,128)S(1)}) custom-call(s32[5]{0:T(128)S(1)} %stack.32.refs_0_, bf16[208,768]{1,0:T(8,128)(2,1)} %get-tuple-element.204.refs_1_, bf16[208,768]{1,0:T(8,128)(2,1)S(1)} %collective-permute-done.7.refs_11_.refs_2_, ...), custom_call_target="tpu_custom_call" | custom-call | flops 1200000000 | bytes 1000 | tf_op jit(solution)/shard_map/late_grad_body/pallas_call | solution.py:86
  76.1 4.4 %collective-permute-done.18 = f32[32,768]{1,0:T(8,128)S(1)} collective-permute-done((f32[32,768]{1,0:T(8,128)S(1)}, f32[32,768]{1,0:T(8,128)S(1)}, u32[]{:S(2)}, u32[]{:S(2)}) %collective-permute-start.18) | collective-permute-done | bytes 98336 | tf_op jit(solution)/shard_map/ppermute | solution.py:825
  84.0 1.7 %collective-permute-start.22 = (bf16[1,2,96,384]{3,2,1,0:T(8,128)(2,1)S(1)}, bf16[1,2,96,384]{3,2,1,0:T(8,128)(2,1)S(1)}, u32[]{:S(2)}, u32[]{:S(2)}) collective-permute-start(bf16[1,2,96,384]{3,2,1,0:T(8,128)(2,1)S(1)} %get-tuple-element.224), channel_id=1, source_target_pairs={{0,8},{4,12},{8,0},{12,4},{16,24},{20,28},{24,16},{28,20},{1,9},{5... | collective-permute-start | bytes 442376 | tf_op jit(solution)/shard_map/ppermute | solution.py:825
  85.7 2.6 %collective-permute-start.27 = (bf16[2,1,96,768]{3,2,1,0:T(8,128)(2,1)S(1)}, bf16[2,1,96,768]{3,2,1,0:T(8,128)(2,1)S(1)}, u32[]{:S(2)}, u32[]{:S(2)}) collective-permute-start(bf16[2,1,96,768]{3,2,1,0:T(8,128)(2,1)S(1)} %get-tuple-element.236), channel_id=1, source_target_pairs={{0,16},{4,20},{8,24},{12,28},{16,0},{20,4},{24,8},{28,12},{1,17},{... | collective-permute-start | bytes 884744 | tf_op jit(solution)/shard_map/ppermute | solution.py:825
  88.3 1.5 %collective-permute-start.23 = (f32[32,768]{1,0:T(8,128)S(1)}, f32[32,768]{1,0:T(8,128)S(1)}, u32[]{:S(2)}, u32[]{:S(2)}) collective-permute-start(f32[32,768]{1,0:T(8,128)S(1)} %get-tuple-element.226), channel_id=1, source_target_pairs={{0,4},{4,0},{8,12},{12,8},{16,20},{20,16},{24,28},{28,24},{1,5},{5... | collective-permute-start | bytes 294920 | tf_op jit(solution)/shard_map/ppermute | solution.py:825
  91.0 1.9 %collective-permute-done.23 = f32[32,768]{1,0:T(8,128)S(1)} collective-permute-done((f32[32,768]{1,0:T(8,128)S(1)}, f32[32,768]{1,0:T(8,128)S(1)}, u32[]{:S(2)}, u32[]{:S(2)}) %collective-permute-start.23) | collective-permute-done | bytes 98336 | tf_op jit(solution)/shard_map/ppermute | solution.py:825
  94.1 3.1 %collective-permute-start.26 = (bf16[1,1,96,384]{3,2,1,0:T(8,128)(2,1)S(1)}, bf16[1,1,96,384]{3,2,1,0:T(8,128)(2,1)S(1)}, u32[]{:S(2)}, u32[]{:S(2)}) collective-permute-start(bf16[1,1,96,384]{3,2,1,0:T(8,128)(2,1)S(1)} %get-tuple-element.234), channel_id=1, source_target_pairs={{0,16},{4,20},{8,24},{12,28},{16,0},{20,4},{24,8},{28,12},{1,17},{... | collective-permute-start | bytes 221192 | tf_op jit(solution)/shard_map/ppermute | solution.py:825
  97.2 2.2 %collective-permute-done.21.refs_2_ = bf16[1,2,96,384]{3,2,1,0:T(8,128)(2,1)S(1)} collective-permute-done((bf16[1,2,96,384]{3,2,1,0:T(8,128)(2,1)S(1)}, bf16[1,2,96,384]{3,2,1,0:T(8,128)(2,1)S(1)}, u32[]{:S(2)}, u32[]{:S(2)}) %collective-permute-start.21) | collective-permute-done | bytes 147488 | tf_op jit(solution)/shard_map/ppermute | solution.py:825
  100.0 3.2 %collective-permute-start.28 = (bf16[1,1,96,384]{3,2,1,0:T(8,128)(2,1)S(1)}, bf16[1,1,96,384]{3,2,1,0:T(8,128)(2,1)S(1)}, u32[]{:S(2)}, u32[]{:S(2)}) collective-permute-start(bf16[1,1,96,384]{3,2,1,0:T(8,128)(2,1)S(1)} %get-tuple-element.241), channel_id=1, source_target_pairs={{0,16},{4,20},{8,24},{12,28},{16,0},{20,4},{24,8},{28,12},{1,17},{... | collective-permute-start | bytes 221192 | tf_op jit(solution)/shard_map/ppermute | solution.py:825
  103.2 2.1 %layer_end_body.1 = (bf16[1,197,768]{2,1,0:T(8,128)(2,1)}, f32[8,128]{1,0:T(8,128)S(1)}, f32[32,768]{1,0:T(8,128)S(1)}) custom-call(f32[208,768]{1,0:T(8,128)} %get-tuple-element.134.refs_3_.refs_0_, f32[208,768]{1,0:T(8,128)} %get-tuple-element.142.refs_1_, bf16[208,768]{1,0:T(8,128)(2,1)S(1)} %collective-permute-done.19.refs_2_, ...), custom_call_target="tpu_custom_call", output_to_operand_aliasing={{2}: (5, {})} | custom-call | flops 200000000 | bytes 1000 | tf_op jit(solution)/shard_map/layer_end_body/pallas_call | solution.py:86
  107.7 2.2 %collective-permute-start.25 = (f32[32,768]{1,0:T(8,128)S(1)}, f32[32,768]{1,0:T(8,128)S(1)}, u32[]{:S(2)}, u32[]{:S(2)}) collective-permute-start(f32[32,768]{1,0:T(8,128)S(1)} %get-tuple-element.232), channel_id=1, source_target_pairs={{0,16},{4,20},{8,24},{12,28},{16,0},{20,4},{24,8},{28,12},{1,17},{... | collective-permute-start | bytes 294920 | tf_op jit(solution)/shard_map/ppermute | solution.py:825
  111.3 1.9 %collective-permute-done.25 = f32[32,768]{1,0:T(8,128)S(1)} collective-permute-done((f32[32,768]{1,0:T(8,128)S(1)}, f32[32,768]{1,0:T(8,128)S(1)}, u32[]{:S(2)}, u32[]{:S(2)}) %collective-permute-start.25) | collective-permute-done | bytes 98336 | tf_op jit(solution)/shard_map/ppermute | solution.py:825
  114.9 1.6 %assemble_body.1 = (f32[96,2304]{1,0:T(8,128)}, f32[96,768]{1,0:T(8,128)}, f32[8,128]{1,0:T(8,128)}) custom-call(s32[5]{0:T(128)S(1)} %stack.32.refs_0_, bf16[96,768]{1,0:T(8,128)(2,1)S(1)} %get-tuple-element.243.refs_1_, bf16[96,768]{1,0:T(8,128)(2,1)S(1)} %collective-permute-done.29.refs_2_, bf16[2,96,768]{2,1,0:T(8,128)(2,1)S(1)} %collective-permute-done.30.refs_3_, ...), custom_call_target="tpu_custom_call" | custom-call | flops 1000000000 | bytes 1000 | tf_op jit(solution)/shard_map/assemble_body/pallas_call | solution.py:86
  (72 shorter events, 21.1 us)
Async XLA Ops:
  0.7 14.8 %collective-permute-start.1 = (bf16[768,768]{1,0:T(8,128)(2,1)}, bf16[768,768]{1,0:T(8,128)(2,1)S(1)}, u32[]{:S(2)}, u32[]{:S(2)}) collective-permute-start(bf16[768,768]{1,0:T(8,128)(2,1)} %refs_3_.7), channel_id=1, source_target_pairs={{0,1},{1,0},{2,3},{3,2},{4,5},{5,4},{6,7},{7,6},{8,9},{9,8},{10,11... | collective-permute-start | bytes 3538952 | tf_op jit(solution)/shard_map/ppermute | solution.py:825
  1.2 14.3 %collective-permute-start.2 = (bf16[768,768]{1,0:T(8,128)(2,1)}, bf16[768,768]{1,0:T(8,128)(2,1)S(1)}, u32[]{:S(2)}, u32[]{:S(2)}) collective-permute-start(bf16[768,768]{1,0:T(8,128)(2,1)} %refs_2_.4), channel_id=1, source_target_pairs={{0,1},{1,0},{2,3},{3,2},{4,5},{5,4},{6,7},{7,6},{8,9},{9,8},{10,11... | collective-permute-start | bytes 3538952 | tf_op jit(solution)/shard_map/ppermute | solution.py:825
  1.3 14.2 %collective-permute-start.3 = (bf16[1,197,768]{2,1,0:T(8,128)(2,1)}, bf16[1,197,768]{2,1,0:T(8,128)(2,1)S(1)}, u32[]{:S(2)}, u32[]{:S(2)}) collective-permute-start(bf16[1,197,768]{2,1,0:T(8,128)(2,1)} %refs_5_.8), channel_id=1, source_target_pairs={{0,2},{1,3},{2,0},{3,1},{4,6},{5,7},{6,4},{7,5},{8,10},{9,11},{10,... | collective-permute-start | bytes 907784 | tf_op jit(solution)/shard_map/ppermute | solution.py:825
  4.2 9.2 %collective-permute-start.4 = (s32[1,197]{1,0:T(1,128)}, s32[1,197]{1,0:T(1,128)S(1)}, u32[]{:S(2)}, u32[]{:S(2)}) collective-permute-start(s32[1,197]{1,0:T(1,128)} %refs_10_.3), channel_id=1, source_target_pairs={{0,2},{1,3},{2,0},{3,1},{4,6},{5,7},{6,4},{7,5},{8,10},{9,11},{10,... | collective-permute-start | bytes 2372 | tf_op jit(solution)/shard_map/ppermute | solution.py:825
  4.2 11.3 %collective-permute-start = (bf16[768]{0:T(1024)(128)(2,1)}, bf16[768]{0:T(1024)(128)(2,1)S(1)}, u32[]{:S(2)}, u32[]{:S(2)}) collective-permute-start(bf16[768]{0:T(1024)(128)(2,1)} %refs_1_.6), channel_id=1, source_target_pairs={{0,1},{1,0},{2,3},{3,2},{4,5},{5,4},{6,7},{7,6},{8,9},{9,8},{10,11... | collective-permute-start | bytes 4616 | tf_op jit(solution)/shard_map/ppermute | solution.py:825
  4.3 11.8 %copy-start.1 = (bf16[768,768]{1,0:T(8,128)(2,1)S(1)}, bf16[768,768]{1,0:T(8,128)(2,1)}, u32[]{:S(2)}) copy-start(bf16[768,768]{1,0:T(8,128)(2,1)} %refs_2_.4) | copy-start | bytes 3538948
  13.4 10.3 %collective-permute-start.5 = (bf16[208,768]{1,0:T(8,128)(2,1)S(1)}, bf16[208,768]{1,0:T(8,128)(2,1)S(1)}, u32[]{:S(2)}, u32[]{:S(2)}) collective-permute-start(bf16[208,768]{1,0:T(8,128)(2,1)S(1)} %get-tuple-element.135.refs_0_.refs_1_), channel_id=1, source_target_pairs={{0,2},{1,3},{2,0},{3,1},{4,6},{5,7},{6,4},{7,5},{8,10},{9,11},{10,... | collective-permute-start | bytes 958472 | tf_op jit(solution)/shard_map/ppermute | solution.py:825
  20.7 10.7 %collective-permute-start.7 = (bf16[208,768]{1,0:T(8,128)(2,1)}, bf16[208,768]{1,0:T(8,128)(2,1)S(1)}, u32[]{:S(2)}, u32[]{:S(2)}) collective-permute-start(bf16[208,768]{1,0:T(8,128)(2,1)} %get-tuple-element.171), channel_id=1, source_target_pairs={{0,1},{1,0},{2,3},{3,2},{4,5},{5,4},{6,7},{7,6},{8,9},{9,8},{10,11... | collective-permute-start | bytes 958472 | tf_op jit(solution)/shard_map/ppermute | solution.py:825
  26.7 13.0 %collective-permute-start.9 = (bf16[208,768]{1,0:T(8,128)(2,1)S(1)}, bf16[208,768]{1,0:T(8,128)(2,1)S(1)}, u32[]{:S(2)}, u32[]{:S(2)}) collective-permute-start(bf16[208,768]{1,0:T(8,128)(2,1)S(1)} %get-tuple-element.181), channel_id=1, source_target_pairs={{0,2},{1,3},{2,0},{3,1},{4,6},{5,7},{6,4},{7,5},{8,10},{9,11},{10,... | collective-permute-start | bytes 958472 | tf_op jit(solution)/shard_map/ppermute | solution.py:825
  30.0 4.6 %collective-permute-start.6 = (bf16[2,768,768]{2,1,0:T(8,128)(2,1)S(1)}, bf16[2,768,768]{2,1,0:T(8,128)(2,1)S(1)}, u32[]{:S(2)}, u32[]{:S(2)}) collective-permute-start(bf16[2,768,768]{2,1,0:T(8,128)(2,1)S(1)} %get-tuple-element.163), channel_id=1, source_target_pairs={{0,1},{1,0},{2,3},{3,2},{4,5},{5,4},{6,7},{7,6},{8,9},{9,8},{10,11... | collective-permute-start | bytes 7077896 | tf_op jit(solution)/shard_map/ppermute | solution.py:825
  36.7 12.1 %collective-permute-start.10 = (bf16[208,768]{1,0:T(8,128)(2,1)}, bf16[208,768]{1,0:T(8,128)(2,1)S(1)}, u32[]{:S(2)}, u32[]{:S(2)}) collective-permute-start(bf16[208,768]{1,0:T(8,128)(2,1)} %get-tuple-element.194), channel_id=1, source_target_pairs={{0,2},{1,3},{2,0},{3,1},{4,6},{5,7},{6,4},{7,5},{8,10},{9,11},{10,... | collective-permute-start | bytes 958472 | tf_op jit(solution)/shard_map/ppermute | solution.py:825
  37.0 15.5 %collective-permute-start.11 = (bf16[208,768]{1,0:T(8,128)(2,1)}, bf16[208,768]{1,0:T(8,128)(2,1)S(1)}, u32[]{:S(2)}, u32[]{:S(2)}) collective-permute-start(bf16[208,768]{1,0:T(8,128)(2,1)} %get-tuple-element.195), channel_id=1, source_target_pairs={{0,3},{1,2},{2,1},{3,0},{4,7},{5,6},{6,5},{7,4},{8,11},{9,10},{10,... | collective-permute-start | bytes 958472 | tf_op jit(solution)/shard_map/ppermute | solution.py:825
  38.2 28.5 %collective-permute-start.8 = (bf16[2,4,96,768]{3,2,1,0:T(8,128)(2,1)S(1)}, bf16[2,4,96,768]{3,2,1,0:T(8,128)(2,1)S(1)}, u32[]{:S(2)}, u32[]{:S(2)}) collective-permute-start(bf16[2,4,96,768]{3,2,1,0:T(8,128)(2,1)S(1)} %get-tuple-element.179), channel_id=1, source_target_pairs={{0,4},{4,0},{8,12},{12,8},{16,20},{20,16},{24,28},{28,24},{1,5},{5... | collective-permute-start | bytes 3538952 | tf_op jit(solution)/shard_map/ppermute | solution.py:825
  47.1 22.2 %collective-permute-start.13 = (bf16[208,768]{1,0:T(8,128)(2,1)S(1)}, bf16[208,768]{1,0:T(8,128)(2,1)S(1)}, u32[]{:S(2)}, u32[]{:S(2)}) collective-permute-start(bf16[208,768]{1,0:T(8,128)(2,1)S(1)} %get-tuple-element.206), channel_id=1, source_target_pairs={{0,1},{1,0},{2,3},{3,2},{4,5},{5,4},{6,7},{7,6},{8,9},{9,8},{10,11... | collective-permute-start | bytes 958472 | tf_op jit(solution)/shard_map/ppermute | solution.py:825
  47.6 21.8 %collective-permute-start.14 = (bf16[208,768]{1,0:T(8,128)(2,1)S(1)}, bf16[208,768]{1,0:T(8,128)(2,1)S(1)}, u32[]{:S(2)}, u32[]{:S(2)}) collective-permute-start(bf16[208,768]{1,0:T(8,128)(2,1)S(1)} %get-tuple-element.207), channel_id=1, source_target_pairs={{0,2},{1,3},{2,0},{3,1},{4,6},{5,7},{6,4},{7,5},{8,10},{9,11},{10,... | collective-permute-start | bytes 958472 | tf_op jit(solution)/shard_map/ppermute | solution.py:825
  48.8 20.6 %collective-permute-start.15 = (bf16[208,768]{1,0:T(8,128)(2,1)S(1)}, bf16[208,768]{1,0:T(8,128)(2,1)S(1)}, u32[]{:S(2)}, u32[]{:S(2)}) collective-permute-start(bf16[208,768]{1,0:T(8,128)(2,1)S(1)} %get-tuple-element.208), channel_id=1, source_target_pairs={{0,3},{1,2},{2,1},{3,0},{4,7},{5,6},{6,5},{7,4},{8,11},{9,10},{10,... | collective-permute-start | bytes 958472 | tf_op jit(solution)/shard_map/ppermute | solution.py:825
  67.6 15.1 %collective-permute-start.12 = (bf16[2,2,96,768]{3,2,1,0:T(8,128)(2,1)S(1)}, bf16[2,2,96,768]{3,2,1,0:T(8,128)(2,1)S(1)}, u32[]{:S(2)}, u32[]{:S(2)}) collective-permute-start(bf16[2,2,96,768]{3,2,1,0:T(8,128)(2,1)S(1)} %get-tuple-element.203), channel_id=1, source_target_pairs={{0,8},{4,12},{8,0},{12,4},{16,24},{20,28},{24,16},{28,20},{1,9},{5... | collective-permute-start | bytes 1769480 | tf_op jit(solution)/shard_map/ppermute | solution.py:825
  71.4 10.0 %collective-permute-start.16 = (bf16[1,4,96,384]{3,2,1,0:T(8,128)(2,1)S(1)}, bf16[1,4,96,384]{3,2,1,0:T(8,128)(2,1)S(1)}, u32[]{:S(2)}, u32[]{:S(2)}) collective-permute-start(bf16[1,4,96,384]{3,2,1,0:T(8,128)(2,1)S(1)} %get-tuple-element.211), channel_id=1, source_target_pairs={{0,4},{4,0},{8,12},{12,8},{16,20},{20,16},{24,28},{28,24},{1,5},{5... | collective-permute-start | bytes 884744 | tf_op jit(solution)/shard_map/ppermute | solution.py:825
  72.9 2.6 %collective-permute-start.17 = (f32[32,768]{1,0:T(8,128)S(1)}, f32[32,768]{1,0:T(8,128)S(1)}, u32[]{:S(2)}, u32[]{:S(2)}) collective-permute-start(f32[32,768]{1,0:T(8,128)S(1)} %get-tuple-element.215), channel_id=1, source_target_pairs={{0,1},{1,0},{2,3},{3,2},{4,5},{5,4},{6,7},{7,6},{8,9},{9,8},{10,11... | collective-permute-start | bytes 294920 | tf_op jit(solution)/shard_map/ppermute | solution.py:825
  74.9 14.9 %collective-permute-start.20 = (bf16[1,4,96,384]{3,2,1,0:T(8,128)(2,1)S(1)}, bf16[1,4,96,384]{3,2,1,0:T(8,128)(2,1)S(1)}, u32[]{:S(2)}, u32[]{:S(2)}) collective-permute-start(bf16[1,4,96,384]{3,2,1,0:T(8,128)(2,1)S(1)} %get-tuple-element.219), channel_id=1, source_target_pairs={{0,4},{4,0},{8,12},{12,8},{16,20},{20,16},{24,28},{28,24},{1,5},{5... | collective-permute-start | bytes 884744 | tf_op jit(solution)/shard_map/ppermute | solution.py:825
  75.6 5.0 %collective-permute-start.18 = (f32[32,768]{1,0:T(8,128)S(1)}, f32[32,768]{1,0:T(8,128)S(1)}, u32[]{:S(2)}, u32[]{:S(2)}) collective-permute-start(f32[32,768]{1,0:T(8,128)S(1)} %add.29), channel_id=1, source_target_pairs={{0,2},{1,3},{2,0},{3,1},{4,6},{5,7},{6,4},{7,5},{8,10},{9,11},{10,... | collective-permute-start | bytes 294920 | tf_op jit(solution)/shard_map/ppermute | solution.py:825
  83.5 19.7 %collective-permute-start.19 = (bf16[208,768]{1,0:T(8,128)(2,1)}, bf16[208,768]{1,0:T(8,128)(2,1)S(1)}, u32[]{:S(2)}, u32[]{:S(2)}) collective-permute-start(bf16[208,768]{1,0:T(8,128)(2,1)} %get-tuple-element.217), channel_id=1, source_target_pairs={{0,2},{1,3},{2,0},{3,1},{4,6},{5,7},{6,4},{7,5},{8,10},{9,11},{10,... | collective-permute-start | bytes 958472 | tf_op jit(solution)/shard_map/ppermute | solution.py:825
  84.0 9.0 %collective-permute-start.22 = (bf16[1,2,96,384]{3,2,1,0:T(8,128)(2,1)S(1)}, bf16[1,2,96,384]{3,2,1,0:T(8,128)(2,1)S(1)}, u32[]{:S(2)}, u32[]{:S(2)}) collective-permute-start(bf16[1,2,96,384]{3,2,1,0:T(8,128)(2,1)S(1)} %get-tuple-element.224), channel_id=1, source_target_pairs={{0,8},{4,12},{8,0},{12,4},{16,24},{20,28},{24,16},{28,20},{1,9},{5... | collective-permute-start | bytes 442376 | tf_op jit(solution)/shard_map/ppermute | solution.py:825
  85.7 19.6 %collective-permute-start.27 = (bf16[2,1,96,768]{3,2,1,0:T(8,128)(2,1)S(1)}, bf16[2,1,96,768]{3,2,1,0:T(8,128)(2,1)S(1)}, u32[]{:S(2)}, u32[]{:S(2)}) collective-permute-start(bf16[2,1,96,768]{3,2,1,0:T(8,128)(2,1)S(1)} %get-tuple-element.236), channel_id=1, source_target_pairs={{0,16},{4,20},{8,24},{12,28},{16,0},{20,4},{24,8},{28,12},{1,17},{... | collective-permute-start | bytes 884744 | tf_op jit(solution)/shard_map/ppermute | solution.py:825
  88.3 4.6 %collective-permute-start.23 = (f32[32,768]{1,0:T(8,128)S(1)}, f32[32,768]{1,0:T(8,128)S(1)}, u32[]{:S(2)}, u32[]{:S(2)}) collective-permute-start(f32[32,768]{1,0:T(8,128)S(1)} %get-tuple-element.226), channel_id=1, source_target_pairs={{0,4},{4,0},{8,12},{12,8},{16,20},{20,16},{24,28},{28,24},{1,5},{5... | collective-permute-start | bytes 294920 | tf_op jit(solution)/shard_map/ppermute | solution.py:825
  90.5 8.9 %collective-permute-start.21 = (bf16[1,2,96,384]{3,2,1,0:T(8,128)(2,1)S(1)}, bf16[1,2,96,384]{3,2,1,0:T(8,128)(2,1)S(1)}, u32[]{:S(2)}, u32[]{:S(2)}) collective-permute-start(bf16[1,2,96,384]{3,2,1,0:T(8,128)(2,1)S(1)} %get-tuple-element.222), channel_id=1, source_target_pairs={{0,8},{4,12},{8,0},{12,4},{16,24},{20,28},{24,16},{28,20},{1,9},{5... | collective-permute-start | bytes 442376 | tf_op jit(solution)/shard_map/ppermute | solution.py:825
  93.5 9.6 %collective-permute-start.24 = (f32[32,768]{1,0:T(8,128)S(1)}, f32[32,768]{1,0:T(8,128)S(1)}, u32[]{:S(2)}, u32[]{:S(2)}) collective-permute-start(f32[32,768]{1,0:T(8,128)S(1)} %get-tuple-element.229), channel_id=1, source_target_pairs={{0,8},{4,12},{8,0},{12,4},{16,24},{20,28},{24,16},{28,20},{1,9},{5... | collective-permute-start | bytes 294920 | tf_op jit(solution)/shard_map/ppermute | solution.py:825
  94.1 12.1 %collective-permute-start.26 = (bf16[1,1,96,384]{3,2,1,0:T(8,128)(2,1)S(1)}, bf16[1,1,96,384]{3,2,1,0:T(8,128)(2,1)S(1)}, u32[]{:S(2)}, u32[]{:S(2)}) collective-permute-start(bf16[1,1,96,384]{3,2,1,0:T(8,128)(2,1)S(1)} %get-tuple-element.234), channel_id=1, source_target_pairs={{0,16},{4,20},{8,24},{12,28},{16,0},{20,4},{24,8},{28,12},{1,17},{... | collective-permute-start | bytes 221192 | tf_op jit(solution)/shard_map/ppermute | solution.py:825
  100.0 6.2 %collective-permute-start.28 = (bf16[1,1,96,384]{3,2,1,0:T(8,128)(2,1)S(1)}, bf16[1,1,96,384]{3,2,1,0:T(8,128)(2,1)S(1)}, u32[]{:S(2)}, u32[]{:S(2)}) collective-permute-start(bf16[1,1,96,384]{3,2,1,0:T(8,128)(2,1)S(1)} %get-tuple-element.241), channel_id=1, source_target_pairs={{0,16},{4,20},{8,24},{12,28},{16,0},{20,4},{24,8},{28,12},{1,17},{... | collective-permute-start | bytes 221192 | tf_op jit(solution)/shard_map/ppermute | solution.py:825
  106.2 7.0 %collective-permute-start.29 = (bf16[96,768]{1,0:T(8,128)(2,1)S(1)}, bf16[96,768]{1,0:T(8,128)(2,1)S(1)}, u32[]{:S(2)}, u32[]{:S(2)}) collective-permute-start(bf16[96,768]{1,0:T(8,128)(2,1)S(1)} %get-tuple-element.243.refs_1_), channel_id=1, source_target_pairs={{0,2},{1,3},{2,0},{3,1},{4,6},{5,7},{6,4},{7,5},{8,10},{9,11},{10,... | collective-permute-start | bytes 442376 | tf_op jit(solution)/shard_map/ppermute | solution.py:825
  107.7 5.5 %collective-permute-start.25 = (f32[32,768]{1,0:T(8,128)S(1)}, f32[32,768]{1,0:T(8,128)S(1)}, u32[]{:S(2)}, u32[]{:S(2)}) collective-permute-start(f32[32,768]{1,0:T(8,128)S(1)} %get-tuple-element.232), channel_id=1, source_target_pairs={{0,16},{4,20},{8,24},{12,28},{16,0},{20,4},{24,8},{28,12},{1,17},{... | collective-permute-start | bytes 294920 | tf_op jit(solution)/shard_map/ppermute | solution.py:825
  113.3 1.6 %collective-permute-start.30 = (bf16[2,96,768]{2,1,0:T(8,128)(2,1)S(1)}, bf16[2,96,768]{2,1,0:T(8,128)(2,1)S(1)}, u32[]{:S(2)}, u32[]{:S(2)}) collective-permute-start(bf16[2,96,768]{2,1,0:T(8,128)(2,1)S(1)} %pad_maximum_fusion), channel_id=1, source_target_pairs={{0,1},{1,0},{2,3},{3,2},{4,5},{5,4},{6,7},{7,6},{8,9},{9,8},{10,11... | collective-permute-start | bytes 884744 | tf_op jit(solution)/shard_map/ppermute | solution.py:825
  (3 other events, 16.0 us)

commit v5 on v4

--- a/solution.py
+++ b/solution.py
@@ -14,7 +14,7 @@
 SCALE = 1
 COST = dict(fwd=1, mlp=5, far=30, pair=0.42, keep=0.6, back=5, norm=5, table=3.2, late=1.2, fold=0.4, last=0.4, end=0.2, join=1)
 ORDER = (
-    "N", "T", "f1", "A", "B", "x", "a1", "f2@%", "h", "y", "b1", "a2@", "z", "b2", "E@", "w", "F", "S", "J",
+    "N", "T", "f1", "A", "B", "a1", "x", "f2@%", "h", "y", "b1", "a2@", "z", "b2", "E@", "w", "S", "F", "J",
 )
 UNROLL_F = 6
 UNROLL_B = 6

time: 117 us -> 117 us (level)
  no operation moved by 1% of the time
where the time goes in v5:
time: 117 us
  Pallas kernels  52.7 us (45%)
  starting transfers between devices  34.6 us (30%)
  waiting for transfers between devices  24.1 us (21%)
  local copies, waits for them, and re-layouts  4.07 us (3%)
    pallas_call x22, Pallas kernels, call(): pl.pallas_call(inner, name=getattr(body, 'func', body).__name__, out_shap...  52.7 us
    ppermute x31, starting transfers between devices, swap(): return lambda value: lax.ppermute(value, axis, pairs)  34.6 us
    ppermute x31, waiting for transfers between devices, swap(): return lambda value: lax.ppermute(value, axis, pairs)  24.1 us
  transfers between devices with their start and end apart: 31, of which 11 were waited for; matrix products, arithmetic and copies ran while one was open for 3% of the time, Pallas kernels for 44%

profile of v5, /device:TPU:0, one launch (start us, length us, event | category | flops | bytes accessed | tf_op | source)
XLA Modules:
  0.0 116.5 jit_solution(9905104372271432208)
XLA Ops:
  1.3 2.9 %collective-permute-start.3 = (bf16[1,197,768]{2,1,0:T(8,128)(2,1)}, bf16[1,197,768]{2,1,0:T(8,128)(2,1)S(1)}, u32[]{:S(2)}, u32[]{:S(2)}) collective-permute-start(bf16[1,197,768]{2,1,0:T(8,128)(2,1)} %refs_5_.8), channel_id=1, source_target_pairs={{0,2},{1,3},{2,0},{3,1},{4,6},{5,7},{6,4},{7,5},{8,10},{9,11},{10,... | collective-permute-start | bytes 907784 | tf_op jit(solution)/shard_map/ppermute | solution.py:825
  4.3 9.1 %forward_body.1 = (f32[208,128]{1,0:T(8,128)}, bf16[208,768]{1,0:T(8,128)(2,1)}, bf16[208,768]{1,0:T(8,128)(2,1)}, bf16[208,768]{1,0:T(8,128)(2,1)}, bf16[208,76...) custom-call(s32[5]{0:T(128)S(1)} %stack.32.refs_0_, ...), custom_call_target="tpu_custom_call" | custom-call | flops 1000000000 | bytes 1000 | tf_op jit(solution)/shard_map/forward_body/pallas_call | solution.py:86
  13.4 2.1 %collective-permute-start.5 = (bf16[208,768]{1,0:T(8,128)(2,1)S(1)}, bf16[208,768]{1,0:T(8,128)(2,1)S(1)}, u32[]{:S(2)}, u32[]{:S(2)}) collective-permute-start(bf16[208,768]{1,0:T(8,128)(2,1)S(1)} %get-tuple-element.135.refs_0_.refs_1_), channel_id=1, source_target_pairs={{0,2},{1,3},{2,0},{3,1},{4,6},{5,7},{6,4},{7,5},{8,10},{9,11},{10,... | collective-permute-start | bytes 958472 | tf_op jit(solution)/shard_map/ppermute | solution.py:825
  16.1 4.7 %mlp_body.2 = (bf16[208,768]{1,0:T(8,128)(2,1)S(1)}, bf16[208,768]{1,0:T(8,128)(2,1)S(1)}, f32[208,768]{1,0:T(8,128)S(1)}, bf16[208,768]{1,0:T(8,128)(2,1)S(1)},...) custom-call(bf16[208,768]{1,0:T(8,128)(2,1)S(1)} %get-tuple-element., ...), custom_call_target="tpu_custom_call", output_to_operand_aliasing={{11}: (14, {}), {12}: (15, {}), {13}: (16, {}), {14}: (17, ... | custom-call | flops 5000000000 | bytes 1000 | tf_op jit(solution)/shard_map/mlp_body/pallas_call | solution.py:86
  21.0 2.7 %collective-permute-done.5.refs_0_.refs_1_.refs_2_ = bf16[208,768]{1,0:T(8,128)(2,1)S(1)} collective-permute-done((bf16[208,768]{1,0:T(8,128)(2,1)S(1)}, bf16[208,768]{1,0:T(8,128)(2,1)S(1)}, u32[]{:S(2)}, u32[]{:S(2)}) %collective-permute-start.5) | collective-permute-done | bytes 319520 | tf_op jit(solution)/shard_map/ppermute | solution.py:825
  23.7 3.0 %mlp_body.3 = (bf16[208,768]{1,0:T(8,128)(2,1)S(1)}, bf16[208,768]{1,0:T(8,128)(2,1)S(1)}, bf16[208,768]{1,0:T(8,128)(2,1)S(1)}, bf16[208,768]{1,0:T(8,128)(2,1)...) custom-call(bf16[208,768]{1,0:T(8,128)(2,1)S(1)} %collective-permute, ...), custom_call_target="tpu_custom_call", output_to_operand_aliasing={{7}: (10, {}), {8}: (11, {}), {9}: (12, {}), {10}: (13, {})} | custom-call | flops 5000000000 | bytes 1000 | tf_op jit(solution)/shard_map/mlp_body/pallas_call | solution.py:86
  26.7 1.8 %collective-permute-start.9 = (bf16[208,768]{1,0:T(8,128)(2,1)S(1)}, bf16[208,768]{1,0:T(8,128)(2,1)S(1)}, u32[]{:S(2)}, u32[]{:S(2)}) collective-permute-start(bf16[208,768]{1,0:T(8,128)(2,1)S(1)} %get-tuple-element.181), channel_id=1, source_target_pairs={{0,2},{1,3},{2,0},{3,1},{4,6},{5,7},{6,4},{7,5},{8,10},{9,11},{10,... | collective-permute-start | bytes 958472 | tf_op jit(solution)/shard_map/ppermute | solution.py:825
  28.5 1.4 %pair_grad_body.1 = (bf16[2,768,768]{2,1,0:T(8,128)(2,1)S(1)}, f32[8,128]{1,0:T(8,128)S(1)}, bf16[256,768]{1,0:T(8,128)(2,1)S(1)}, bf16[256,768]{1,0:T(8,128)(2,...) custom-call(bf16[208,768]{1,0:T(8,128)(2,1)S(1)} %get-tuple-element., ...), custom_call_target="tpu_custom_call", output_to_operand_aliasing={{2}: (9, {}), {3}: (10, {}), {4}: (11, {}), {5}: (12, {})} | custom-call | flops 420000000 | bytes 1000 | tf_op jit(solution)/shard_map/pair_grad_body/pallas_call | solution.py:86
  31.5 3.1 %collective-permute-done.6.refs_9_ = bf16[2,768,768]{2,1,0:T(8,128)(2,1)S(1)} collective-permute-done((bf16[2,768,768]{2,1,0:T(8,128)(2,1)S(1)}, bf16[2,768,768]{2,1,0:T(8,128)(2,1)S(1)}, u32[]{:S(2)}, u32[]{:S(2)}) %collective-permute-start.6) | collective-permute-done | bytes 2359328 | tf_op jit(solution)/shard_map/ppermute | solution.py:825
  34.6 2.0 %fc_keep_body.1 = (bf16[2,4,96,768]{3,2,1,0:T(8,128)(2,1)S(1)}, bf16[2,4,96,768]{3,2,1,0:T(8,128)(2,1)S(1)}, f32[8,128]{1,0:T(8,128)S(1)}, bf16[208,768]{1,0:T(8...) custom-call(s32[5]{0:T(128)S(1)} %stack.32.refs_0_, ...), custom_call_target="tpu_custom_call", output_to_operand_aliasing={{3}: (12, {}), {4}: (13, {}), {5}: (14, {}), {6}: (15, {}),... | custom-call | flops 600000000 | bytes 1000 | tf_op jit(solution)/shard_map/fc_keep_body/pallas_call | solution.py:86
  38.2 1.5 %collective-permute-start.8 = (bf16[2,4,96,768]{3,2,1,0:T(8,128)(2,1)S(1)}, bf16[2,4,96,768]{3,2,1,0:T(8,128)(2,1)S(1)}, u32[]{:S(2)}, u32[]{:S(2)}) collective-permute-start(bf16[2,4,96,768]{3,2,1,0:T(8,128)(2,1)S(1)} %get-tuple-element.179), channel_id=1, source_target_pairs={{0,4},{4,0},{8,12},{12,8},{16,20},{20,16},{24,28},{28,24},{1,5},{5... | collective-permute-start | bytes 3538952 | tf_op jit(solution)/shard_map/ppermute | solution.py:825
  39.7 7.4 %backward_body.1 = (f32[208,768]{1,0:T(8,128)S(1)}, bf16[208,2304]{1,0:T(8,128)(2,1)S(1)}, bf16[208,768]{1,0:T(8,128)(2,1)S(1)}, bf16[208,768]{1,0:T(8,128)(2,1)...) custom-call(s32[5]{0:T(128)S(1)} %stack.32.refs_0_, ...), custom_call_target="tpu_custom_call" | custom-call | flops 5000000000 | bytes 1000 | tf_op jit(solution)/shard_map/backward_body/pallas_call | solution.py:86
  49.8 2.8 %collective-permute-done.11.refs_9_.refs_4_ = bf16[208,768]{1,0:T(8,128)(2,1)S(1)} collective-permute-done((bf16[208,768]{1,0:T(8,128)(2,1)}, bf16[208,768]{1,0:T(8,128)(2,1)S(1)}, u32[]{:S(2)}, u32[]{:S(2)}) %collective-permute-start.11) | collective-permute-done | bytes 319520 | tf_op jit(solution)/shard_map/ppermute | solution.py:825
  52.5 4.6 %first_norm_body.1 = (f32[1,197,768]{2,1,0:T(8,128)}, f32[8,768]{1,0:T(8,128)S(1)}, f32[8,128]{1,0:T(8,128)S(1)}) custom-call(bf16[1,197,768]{2,1,0:T(8,128)(2,1)} %refs_0_.1, f32[208,128]{1,0:T(8,128)} %get-tuple-element.183.refs_6_.refs_1_, f32[768]{0:T(1024)} %refs_2_.5, f32[768]{0:T(1024)} %refs_3_.8, bf16[208,2304]{1,0:T(8,128)(2,1)S(1)} %get-tuple-element.191.refs_4_, ...), custom_call_target="tpu_custom_call" | custom-call | flops 5000000000 | bytes 1000 | tf_op jit(solution)/shard_map/first_norm_body/pallas_call | solution.py:86
  57.1 6.3 %table_grad_body.1 = (f32[32,768]{1,0:T(8,128)S(1)}, f32[8,128]{1,0:T(8,128)S(1)}) custom-call(s32[5]{0:T(128)S(1)} %stack.32.refs_0_, s32[197,197]{1,0:T(8,128)} %refs_1_.7, bf16[208,16,256]{2,1,0:T(8,128)(2,1)S(1)} %pad.4.refs_2_, f32[8,768]{1,0:T(8,128)S(1)} %get-tuple-element.190.refs_3_, f32[8,768]{1,0:T(8,128)S(1)} %get-tuple-element.196.refs_4_, ...), custom_call_target="tpu_custom_call" | custom-call | flops 3200000000 | bytes 1000 | tf_op jit(solution)/shard_map/table_grad_body/pallas_call | solution.py:86
  63.4 3.3 %collective-permute-done.8.refs_2_ = bf16[2,4,96,768]{3,2,1,0:T(8,128)(2,1)S(1)} collective-permute-done((bf16[2,4,96,768]{3,2,1,0:T(8,128)(2,1)S(1)}, bf16[2,4,96,768]{3,2,1,0:T(8,128)(2,1)S(1)}, u32[]{:S(2)}, u32[]{:S(2)}) %collective-permute-start.8) | collective-permute-done | bytes 1179680 | tf_op jit(solution)/shard_map/ppermute | solution.py:825
  67.6 1.7 %collective-permute-start.12 = (bf16[2,2,96,768]{3,2,1,0:T(8,128)(2,1)S(1)}, bf16[2,2,96,768]{3,2,1,0:T(8,128)(2,1)S(1)}, u32[]{:S(2)}, u32[]{:S(2)}) collective-permute-start(bf16[2,2,96,768]{3,2,1,0:T(8,128)(2,1)S(1)} %get-tuple-element.203), channel_id=1, source_target_pairs={{0,8},{4,12},{8,0},{12,4},{16,24},{20,28},{24,16},{28,20},{1,9},{5... | collective-permute-start | bytes 1769480 | tf_op jit(solution)/shard_map/ppermute | solution.py:825
  69.3 2.0 %late_grad_body.2 = (bf16[1,4,96,384]{3,2,1,0:T(8,128)(2,1)S(1)}, bf16[1,4,96,384]{3,2,1,0:T(8,128)(2,1)S(1)}, f32[8,128]{1,0:T(8,128)S(1)}) custom-call(s32[5]{0:T(128)S(1)} %stack.32.refs_0_, bf16[208,768]{1,0:T(8,128)(2,1)} %get-tuple-element.204.refs_1_, bf16[208,768]{1,0:T(8,128)(2,1)S(1)} %collective-permute-done.7.refs_11_.refs_2_, ...), custom_call_target="tpu_custom_call" | custom-call | flops 1200000000 | bytes 1000 | tf_op jit(solution)/shard_map/late_grad_body/pallas_call | solution.py:86
  71.4 1.6 %collective-permute-start.16 = (bf16[1,4,96,384]{3,2,1,0:T(8,128)(2,1)S(1)}, bf16[1,4,96,384]{3,2,1,0:T(8,128)(2,1)S(1)}, u32[]{:S(2)}, u32[]{:S(2)}) collective-permute-start(bf16[1,4,96,384]{3,2,1,0:T(8,128)(2,1)S(1)} %get-tuple-element.211), channel_id=1, source_target_pairs={{0,4},{4,0},{8,12},{12,8},{16,20},{20,16},{24,28},{28,24},{1,5},{5... | collective-permute-start | bytes 884744 | tf_op jit(solution)/shard_map/ppermute | solution.py:825
  72.9 2.0 %late_grad_body.3 = (bf16[1,4,96,384]{3,2,1,0:T(8,128)(2,1)S(1)}, bf16[1,4,96,384]{3,2,1,0:T(8,128)(2,1)S(1)}, f32[8,128]{1,0:T(8,128)S(1)}) custom-call(s32[5]{0:T(128)S(1)} %stack.32.refs_0_, bf16[208,768]{1,0:T(8,128)(2,1)} %get-tuple-element.204.refs_1_, bf16[208,768]{1,0:T(8,128)(2,1)S(1)} %collective-permute-done.7.refs_11_.refs_2_, ...), custom_call_target="tpu_custom_call" | custom-call | flops 1200000000 | bytes 1000 | tf_op jit(solution)/shard_map/late_grad_body/pallas_call | solution.py:86
  76.1 4.4 %collective-permute-done.18 = f32[32,768]{1,0:T(8,128)S(1)} collective-permute-done((f32[32,768]{1,0:T(8,128)S(1)}, f32[32,768]{1,0:T(8,128)S(1)}, u32[]{:S(2)}, u32[]{:S(2)}) %collective-permute-start.18) | collective-permute-done | bytes 98336 | tf_op jit(solution)/shard_map/ppermute | solution.py:825
  84.0 1.7 %collective-permute-start.22 = (bf16[1,2,96,384]{3,2,1,0:T(8,128)(2,1)S(1)}, bf16[1,2,96,384]{3,2,1,0:T(8,128)(2,1)S(1)}, u32[]{:S(2)}, u32[]{:S(2)}) collective-permute-start(bf16[1,2,96,384]{3,2,1,0:T(8,128)(2,1)S(1)} %get-tuple-element.224), channel_id=1, source_target_pairs={{0,8},{4,12},{8,0},{12,4},{16,24},{20,28},{24,16},{28,20},{1,9},{5... | collective-permute-start | bytes 442376 | tf_op jit(solution)/shard_map/ppermute | solution.py:825
  85.7 2.6 %collective-permute-start.28 = (bf16[2,1,96,768]{3,2,1,0:T(8,128)(2,1)S(1)}, bf16[2,1,96,768]{3,2,1,0:T(8,128)(2,1)S(1)}, u32[]{:S(2)}, u32[]{:S(2)}) collective-permute-start(bf16[2,1,96,768]{3,2,1,0:T(8,128)(2,1)S(1)} %get-tuple-element.240), channel_id=1, source_target_pairs={{0,16},{4,20},{8,24},{12,28},{16,0},{20,4},{24,8},{28,12},{1,17},{... | collective-permute-start | bytes 884744 | tf_op jit(solution)/shard_map/ppermute | solution.py:825
  88.3 1.5 %collective-permute-start.23 = (f32[32,768]{1,0:T(8,128)S(1)}, f32[32,768]{1,0:T(8,128)S(1)}, u32[]{:S(2)}, u32[]{:S(2)}) collective-permute-start(f32[32,768]{1,0:T(8,128)S(1)} %get-tuple-element.226), channel_id=1, source_target_pairs={{0,4},{4,0},{8,12},{12,8},{16,20},{20,16},{24,28},{28,24},{1,5},{5... | collective-permute-start | bytes 294920 | tf_op jit(solution)/shard_map/ppermute | solution.py:825
  91.0 1.9 %collective-permute-done.23 = f32[32,768]{1,0:T(8,128)S(1)} collective-permute-done((f32[32,768]{1,0:T(8,128)S(1)}, f32[32,768]{1,0:T(8,128)S(1)}, u32[]{:S(2)}, u32[]{:S(2)}) %collective-permute-start.23) | collective-permute-done | bytes 98336 | tf_op jit(solution)/shard_map/ppermute | solution.py:825
  94.1 3.1 %collective-permute-start.26 = (bf16[1,1,96,384]{3,2,1,0:T(8,128)(2,1)S(1)}, bf16[1,1,96,384]{3,2,1,0:T(8,128)(2,1)S(1)}, u32[]{:S(2)}, u32[]{:S(2)}) collective-permute-start(bf16[1,1,96,384]{3,2,1,0:T(8,128)(2,1)S(1)} %get-tuple-element.234), channel_id=1, source_target_pairs={{0,16},{4,20},{8,24},{12,28},{16,0},{20,4},{24,8},{28,12},{1,17},{... | collective-permute-start | bytes 221192 | tf_op jit(solution)/shard_map/ppermute | solution.py:825
  97.2 2.2 %collective-permute-done.21.refs_2_ = bf16[1,2,96,384]{3,2,1,0:T(8,128)(2,1)S(1)} collective-permute-done((bf16[1,2,96,384]{3,2,1,0:T(8,128)(2,1)S(1)}, bf16[1,2,96,384]{3,2,1,0:T(8,128)(2,1)S(1)}, u32[]{:S(2)}, u32[]{:S(2)}) %collective-permute-start.21) | collective-permute-done | bytes 147488 | tf_op jit(solution)/shard_map/ppermute | solution.py:825
  100.0 3.2 %collective-permute-start.27 = (bf16[1,1,96,384]{3,2,1,0:T(8,128)(2,1)S(1)}, bf16[1,1,96,384]{3,2,1,0:T(8,128)(2,1)S(1)}, u32[]{:S(2)}, u32[]{:S(2)}) collective-permute-start(bf16[1,1,96,384]{3,2,1,0:T(8,128)(2,1)S(1)} %get-tuple-element.238), channel_id=1, source_target_pairs={{0,16},{4,20},{8,24},{12,28},{16,0},{20,4},{24,8},{28,12},{1,17},{... | collective-permute-start | bytes 221192 | tf_op jit(solution)/shard_map/ppermute | solution.py:825
  103.2 2.1 %layer_end_body.1 = (bf16[1,197,768]{2,1,0:T(8,128)(2,1)}, f32[8,128]{1,0:T(8,128)S(1)}, f32[32,768]{1,0:T(8,128)S(1)}) custom-call(f32[208,768]{1,0:T(8,128)} %get-tuple-element.134.refs_3_.refs_0_, f32[208,768]{1,0:T(8,128)} %get-tuple-element.142.refs_1_, bf16[208,768]{1,0:T(8,128)(2,1)S(1)} %collective-permute-done.19.refs_2_, ...), custom_call_target="tpu_custom_call", output_to_operand_aliasing={{2}: (5, {})} | custom-call | flops 200000000 | bytes 1000 | tf_op jit(solution)/shard_map/layer_end_body/pallas_call | solution.py:86
  107.7 2.2 %collective-permute-start.25 = (f32[32,768]{1,0:T(8,128)S(1)}, f32[32,768]{1,0:T(8,128)S(1)}, u32[]{:S(2)}, u32[]{:S(2)}) collective-permute-start(f32[32,768]{1,0:T(8,128)S(1)} %get-tuple-element.232), channel_id=1, source_target_pairs={{0,16},{4,20},{8,24},{12,28},{16,0},{20,4},{24,8},{28,12},{1,17},{... | collective-permute-start | bytes 294920 | tf_op jit(solution)/shard_map/ppermute | solution.py:825
  111.3 1.8 %collective-permute-done.25 = f32[32,768]{1,0:T(8,128)S(1)} collective-permute-done((f32[32,768]{1,0:T(8,128)S(1)}, f32[32,768]{1,0:T(8,128)S(1)}, u32[]{:S(2)}, u32[]{:S(2)}) %collective-permute-start.25) | collective-permute-done | bytes 98336 | tf_op jit(solution)/shard_map/ppermute | solution.py:825
  114.9 1.6 %assemble_body.1 = (f32[96,2304]{1,0:T(8,128)}, f32[96,768]{1,0:T(8,128)}, f32[8,128]{1,0:T(8,128)}) custom-call(s32[5]{0:T(128)S(1)} %stack.32.refs_0_, bf16[96,768]{1,0:T(8,128)(2,1)S(1)} %get-tuple-element.243.refs_1_, bf16[96,768]{1,0:T(8,128)(2,1)S(1)} %collective-permute-done.29.refs_2_, bf16[2,96,768]{2,1,0:T(8,128)(2,1)S(1)} %collective-permute-done.30.refs_3_, ...), custom_call_target="tpu_custom_call" | custom-call | flops 1000000000 | bytes 1000 | tf_op jit(solution)/shard_map/assemble_body/pallas_call | solution.py:86
  (72 shorter events, 21.1 us)
Async XLA Ops:
  0.7 14.8 %collective-permute-start.1 = (bf16[768,768]{1,0:T(8,128)(2,1)}, bf16[768,768]{1,0:T(8,128)(2,1)S(1)}, u32[]{:S(2)}, u32[]{:S(2)}) collective-permute-start(bf16[768,768]{1,0:T(8,128)(2,1)} %refs_3_.7), channel_id=1, source_target_pairs={{0,1},{1,0},{2,3},{3,2},{4,5},{5,4},{6,7},{7,6},{8,9},{9,8},{10,11... | collective-permute-start | bytes 3538952 | tf_op jit(solution)/shard_map/ppermute | solution.py:825
  1.2 14.3 %collective-permute-start.2 = (bf16[768,768]{1,0:T(8,128)(2,1)}, bf16[768,768]{1,0:T(8,128)(2,1)S(1)}, u32[]{:S(2)}, u32[]{:S(2)}) collective-permute-start(bf16[768,768]{1,0:T(8,128)(2,1)} %refs_2_.4), channel_id=1, source_target_pairs={{0,1},{1,0},{2,3},{3,2},{4,5},{5,4},{6,7},{7,6},{8,9},{9,8},{10,11... | collective-permute-start | bytes 3538952 | tf_op jit(solution)/shard_map/ppermute | solution.py:825
  1.3 14.2 %collective-permute-start.3 = (bf16[1,197,768]{2,1,0:T(8,128)(2,1)}, bf16[1,197,768]{2,1,0:T(8,128)(2,1)S(1)}, u32[]{:S(2)}, u32[]{:S(2)}) collective-permute-start(bf16[1,197,768]{2,1,0:T(8,128)(2,1)} %refs_5_.8), channel_id=1, source_target_pairs={{0,2},{1,3},{2,0},{3,1},{4,6},{5,7},{6,4},{7,5},{8,10},{9,11},{10,... | collective-permute-start | bytes 907784 | tf_op jit(solution)/shard_map/ppermute | solution.py:825
  4.2 9.2 %collective-permute-start.4 = (s32[1,197]{1,0:T(1,128)}, s32[1,197]{1,0:T(1,128)S(1)}, u32[]{:S(2)}, u32[]{:S(2)}) collective-permute-start(s32[1,197]{1,0:T(1,128)} %refs_10_.3), channel_id=1, source_target_pairs={{0,2},{1,3},{2,0},{3,1},{4,6},{5,7},{6,4},{7,5},{8,10},{9,11},{10,... | collective-permute-start | bytes 2372 | tf_op jit(solution)/shard_map/ppermute | solution.py:825
  4.2 11.3 %collective-permute-start = (bf16[768]{0:T(1024)(128)(2,1)}, bf16[768]{0:T(1024)(128)(2,1)S(1)}, u32[]{:S(2)}, u32[]{:S(2)}) collective-permute-start(bf16[768]{0:T(1024)(128)(2,1)} %refs_1_.6), channel_id=1, source_target_pairs={{0,1},{1,0},{2,3},{3,2},{4,5},{5,4},{6,7},{7,6},{8,9},{9,8},{10,11... | collective-permute-start | bytes 4616 | tf_op jit(solution)/shard_map/ppermute | solution.py:825
  4.3 11.8 %copy-start.1 = (bf16[768,768]{1,0:T(8,128)(2,1)S(1)}, bf16[768,768]{1,0:T(8,128)(2,1)}, u32[]{:S(2)}) copy-start(bf16[768,768]{1,0:T(8,128)(2,1)} %refs_2_.4) | copy-start | bytes 3538948
  13.4 10.3 %collective-permute-start.5 = (bf16[208,768]{1,0:T(8,128)(2,1)S(1)}, bf16[208,768]{1,0:T(8,128)(2,1)S(1)}, u32[]{:S(2)}, u32[]{:S(2)}) collective-permute-start(bf16[208,768]{1,0:T(8,128)(2,1)S(1)} %get-tuple-element.135.refs_0_.refs_1_), channel_id=1, source_target_pairs={{0,2},{1,3},{2,0},{3,1},{4,6},{5,7},{6,4},{7,5},{8,10},{9,11},{10,... | collective-permute-start | bytes 958472 | tf_op jit(solution)/shard_map/ppermute | solution.py:825
  20.7 10.7 %collective-permute-start.7 = (bf16[208,768]{1,0:T(8,128)(2,1)}, bf16[208,768]{1,0:T(8,128)(2,1)S(1)}, u32[]{:S(2)}, u32[]{:S(2)}) collective-permute-start(bf16[208,768]{1,0:T(8,128)(2,1)} %get-tuple-element.171), channel_id=1, source_target_pairs={{0,1},{1,0},{2,3},{3,2},{4,5},{5,4},{6,7},{7,6},{8,9},{9,8},{10,11... | collective-permute-start | bytes 958472 | tf_op jit(solution)/shard_map/ppermute | solution.py:825
  26.7 13.0 %collective-permute-start.9 = (bf16[208,768]{1,0:T(8,128)(2,1)S(1)}, bf16[208,768]{1,0:T(8,128)(2,1)S(1)}, u32[]{:S(2)}, u32[]{:S(2)}) collective-permute-start(bf16[208,768]{1,0:T(8,128)(2,1)S(1)} %get-tuple-element.181), channel_id=1, source_target_pairs={{0,2},{1,3},{2,0},{3,1},{4,6},{5,7},{6,4},{7,5},{8,10},{9,11},{10,... | collective-permute-start | bytes 958472 | tf_op jit(solution)/shard_map/ppermute | solution.py:825
  30.0 4.6 %collective-permute-start.6 = (bf16[2,768,768]{2,1,0:T(8,128)(2,1)S(1)}, bf16[2,768,768]{2,1,0:T(8,128)(2,1)S(1)}, u32[]{:S(2)}, u32[]{:S(2)}) collective-permute-start(bf16[2,768,768]{2,1,0:T(8,128)(2,1)S(1)} %get-tuple-element.163), channel_id=1, source_target_pairs={{0,1},{1,0},{2,3},{3,2},{4,5},{5,4},{6,7},{7,6},{8,9},{9,8},{10,11... | collective-permute-start | bytes 7077896 | tf_op jit(solution)/shard_map/ppermute | solution.py:825
  36.7 12.1 %collective-permute-start.10 = (bf16[208,768]{1,0:T(8,128)(2,1)}, bf16[208,768]{1,0:T(8,128)(2,1)S(1)}, u32[]{:S(2)}, u32[]{:S(2)}) collective-permute-start(bf16[208,768]{1,0:T(8,128)(2,1)} %get-tuple-element.194), channel_id=1, source_target_pairs={{0,2},{1,3},{2,0},{3,1},{4,6},{5,7},{6,4},{7,5},{8,10},{9,11},{10,... | collective-permute-start | bytes 958472 | tf_op jit(solution)/shard_map/ppermute | solution.py:825
  37.0 15.5 %collective-permute-start.11 = (bf16[208,768]{1,0:T(8,128)(2,1)}, bf16[208,768]{1,0:T(8,128)(2,1)S(1)}, u32[]{:S(2)}, u32[]{:S(2)}) collective-permute-start(bf16[208,768]{1,0:T(8,128)(2,1)} %get-tuple-element.195), channel_id=1, source_target_pairs={{0,3},{1,2},{2,1},{3,0},{4,7},{5,6},{6,5},{7,4},{8,11},{9,10},{10,... | collective-permute-start | bytes 958472 | tf_op jit(solution)/shard_map/ppermute | solution.py:825
  38.2 28.5 %collective-permute-start.8 = (bf16[2,4,96,768]{3,2,1,0:T(8,128)(2,1)S(1)}, bf16[2,4,96,768]{3,2,1,0:T(8,128)(2,1)S(1)}, u32[]{:S(2)}, u32[]{:S(2)}) collective-permute-start(bf16[2,4,96,768]{3,2,1,0:T(8,128)(2,1)S(1)} %get-tuple-element.179), channel_id=1, source_target_pairs={{0,4},{4,0},{8,12},{12,8},{16,20},{20,16},{24,28},{28,24},{1,5},{5... | collective-permute-start | bytes 3538952 | tf_op jit(solution)/shard_map/ppermute | solution.py:825
  47.1 22.2 %collective-permute-start.13 = (bf16[208,768]{1,0:T(8,128)(2,1)S(1)}, bf16[208,768]{1,0:T(8,128)(2,1)S(1)}, u32[]{:S(2)}, u32[]{:S(2)}) collective-permute-start(bf16[208,768]{1,0:T(8,128)(2,1)S(1)} %get-tuple-element.206), channel_id=1, source_target_pairs={{0,1},{1,0},{2,3},{3,2},{4,5},{5,4},{6,7},{7,6},{8,9},{9,8},{10,11... | collective-permute-start | bytes 958472 | tf_op jit(solution)/shard_map/ppermute | solution.py:825
  47.6 21.8 %collective-permute-start.14 = (bf16[208,768]{1,0:T(8,128)(2,1)S(1)}, bf16[208,768]{1,0:T(8,128)(2,1)S(1)}, u32[]{:S(2)}, u32[]{:S(2)}) collective-permute-start(bf16[208,768]{1,0:T(8,128)(2,1)S(1)} %get-tuple-element.207), channel_id=1, source_target_pairs={{0,2},{1,3},{2,0},{3,1},{4,6},{5,7},{6,4},{7,5},{8,10},{9,11},{10,... | collective-permute-start | bytes 958472 | tf_op jit(solution)/shard_map/ppermute | solution.py:825
  48.8 20.6 %collective-permute-start.15 = (bf16[208,768]{1,0:T(8,128)(2,1)S(1)}, bf16[208,768]{1,0:T(8,128)(2,1)S(1)}, u32[]{:S(2)}, u32[]{:S(2)}) collective-permute-start(bf16[208,768]{1,0:T(8,128)(2,1)S(1)} %get-tuple-element.208), channel_id=1, source_target_pairs={{0,3},{1,2},{2,1},{3,0},{4,7},{5,6},{6,5},{7,4},{8,11},{9,10},{10,... | collective-permute-start | bytes 958472 | tf_op jit(solution)/shard_map/ppermute | solution.py:825
  67.6 15.1 %collective-permute-start.12 = (bf16[2,2,96,768]{3,2,1,0:T(8,128)(2,1)S(1)}, bf16[2,2,96,768]{3,2,1,0:T(8,128)(2,1)S(1)}, u32[]{:S(2)}, u32[]{:S(2)}) collective-permute-start(bf16[2,2,96,768]{3,2,1,0:T(8,128)(2,1)S(1)} %get-tuple-element.203), channel_id=1, source_target_pairs={{0,8},{4,12},{8,0},{12,4},{16,24},{20,28},{24,16},{28,20},{1,9},{5... | collective-permute-start | bytes 1769480 | tf_op jit(solution)/shard_map/ppermute | solution.py:825
  71.4 10.0 %collective-permute-start.16 = (bf16[1,4,96,384]{3,2,1,0:T(8,128)(2,1)S(1)}, bf16[1,4,96,384]{3,2,1,0:T(8,128)(2,1)S(1)}, u32[]{:S(2)}, u32[]{:S(2)}) collective-permute-start(bf16[1,4,96,384]{3,2,1,0:T(8,128)(2,1)S(1)} %get-tuple-element.211), channel_id=1, source_target_pairs={{0,4},{4,0},{8,12},{12,8},{16,20},{20,16},{24,28},{28,24},{1,5},{5... | collective-permute-start | bytes 884744 | tf_op jit(solution)/shard_map/ppermute | solution.py:825
  72.9 2.6 %collective-permute-start.17 = (f32[32,768]{1,0:T(8,128)S(1)}, f32[32,768]{1,0:T(8,128)S(1)}, u32[]{:S(2)}, u32[]{:S(2)}) collective-permute-start(f32[32,768]{1,0:T(8,128)S(1)} %get-tuple-element.215), channel_id=1, source_target_pairs={{0,1},{1,0},{2,3},{3,2},{4,5},{5,4},{6,7},{7,6},{8,9},{9,8},{10,11... | collective-permute-start | bytes 294920 | tf_op jit(solution)/shard_map/ppermute | solution.py:825
  74.9 14.9 %collective-permute-start.20 = (bf16[1,4,96,384]{3,2,1,0:T(8,128)(2,1)S(1)}, bf16[1,4,96,384]{3,2,1,0:T(8,128)(2,1)S(1)}, u32[]{:S(2)}, u32[]{:S(2)}) collective-permute-start(bf16[1,4,96,384]{3,2,1,0:T(8,128)(2,1)S(1)} %get-tuple-element.219), channel_id=1, source_target_pairs={{0,4},{4,0},{8,12},{12,8},{16,20},{20,16},{24,28},{28,24},{1,5},{5... | collective-permute-start | bytes 884744 | tf_op jit(solution)/shard_map/ppermute | solution.py:825
  75.6 5.0 %collective-permute-start.18 = (f32[32,768]{1,0:T(8,128)S(1)}, f32[32,768]{1,0:T(8,128)S(1)}, u32[]{:S(2)}, u32[]{:S(2)}) collective-permute-start(f32[32,768]{1,0:T(8,128)S(1)} %add.29), channel_id=1, source_target_pairs={{0,2},{1,3},{2,0},{3,1},{4,6},{5,7},{6,4},{7,5},{8,10},{9,11},{10,... | collective-permute-start | bytes 294920 | tf_op jit(solution)/shard_map/ppermute | solution.py:825
  83.5 19.7 %collective-permute-start.19 = (bf16[208,768]{1,0:T(8,128)(2,1)}, bf16[208,768]{1,0:T(8,128)(2,1)S(1)}, u32[]{:S(2)}, u32[]{:S(2)}) collective-permute-start(bf16[208,768]{1,0:T(8,128)(2,1)} %get-tuple-element.217), channel_id=1, source_target_pairs={{0,2},{1,3},{2,0},{3,1},{4,6},{5,7},{6,4},{7,5},{8,10},{9,11},{10,... | collective-permute-start | bytes 958472 | tf_op jit(solution)/shard_map/ppermute | solution.py:825
  84.0 9.0 %collective-permute-start.22 = (bf16[1,2,96,384]{3,2,1,0:T(8,128)(2,1)S(1)}, bf16[1,2,96,384]{3,2,1,0:T(8,128)(2,1)S(1)}, u32[]{:S(2)}, u32[]{:S(2)}) collective-permute-start(bf16[1,2,96,384]{3,2,1,0:T(8,128)(2,1)S(1)} %get-tuple-element.224), channel_id=1, source_target_pairs={{0,8},{4,12},{8,0},{12,4},{16,24},{20,28},{24,16},{28,20},{1,9},{5... | collective-permute-start | bytes 442376 | tf_op jit(solution)/shard_map/ppermute | solution.py:825
  85.7 19.7 %collective-permute-start.28 = (bf16[2,1,96,768]{3,2,1,0:T(8,128)(2,1)S(1)}, bf16[2,1,96,768]{3,2,1,0:T(8,128)(2,1)S(1)}, u32[]{:S(2)}, u32[]{:S(2)}) collective-permute-start(bf16[2,1,96,768]{3,2,1,0:T(8,128)(2,1)S(1)} %get-tuple-element.240), channel_id=1, source_target_pairs={{0,16},{4,20},{8,24},{12,28},{16,0},{20,4},{24,8},{28,12},{1,17},{... | collective-permute-start | bytes 884744 | tf_op jit(solution)/shard_map/ppermute | solution.py:825
  88.3 4.6 %collective-permute-start.23 = (f32[32,768]{1,0:T(8,128)S(1)}, f32[32,768]{1,0:T(8,128)S(1)}, u32[]{:S(2)}, u32[]{:S(2)}) collective-permute-start(f32[32,768]{1,0:T(8,128)S(1)} %get-tuple-element.226), channel_id=1, source_target_pairs={{0,4},{4,0},{8,12},{12,8},{16,20},{20,16},{24,28},{28,24},{1,5},{5... | collective-permute-start | bytes 294920 | tf_op jit(solution)/shard_map/ppermute | solution.py:825
  90.5 8.9 %collective-permute-start.21 = (bf16[1,2,96,384]{3,2,1,0:T(8,128)(2,1)S(1)}, bf16[1,2,96,384]{3,2,1,0:T(8,128)(2,1)S(1)}, u32[]{:S(2)}, u32[]{:S(2)}) collective-permute-start(bf16[1,2,96,384]{3,2,1,0:T(8,128)(2,1)S(1)} %get-tuple-element.222), channel_id=1, source_target_pairs={{0,8},{4,12},{8,0},{12,4},{16,24},{20,28},{24,16},{28,20},{1,9},{5... | collective-permute-start | bytes 442376 | tf_op jit(solution)/shard_map/ppermute | solution.py:825
  93.5 9.6 %collective-permute-start.24 = (f32[32,768]{1,0:T(8,128)S(1)}, f32[32,768]{1,0:T(8,128)S(1)}, u32[]{:S(2)}, u32[]{:S(2)}) collective-permute-start(f32[32,768]{1,0:T(8,128)S(1)} %get-tuple-element.229), channel_id=1, source_target_pairs={{0,8},{4,12},{8,0},{12,4},{16,24},{20,28},{24,16},{28,20},{1,9},{5... | collective-permute-start | bytes 294920 | tf_op jit(solution)/shard_map/ppermute | solution.py:825
  94.1 11.3 %collective-permute-start.26 = (bf16[1,1,96,384]{3,2,1,0:T(8,128)(2,1)S(1)}, bf16[1,1,96,384]{3,2,1,0:T(8,128)(2,1)S(1)}, u32[]{:S(2)}, u32[]{:S(2)}) collective-permute-start(bf16[1,1,96,384]{3,2,1,0:T(8,128)(2,1)S(1)} %get-tuple-element.234), channel_id=1, source_target_pairs={{0,16},{4,20},{8,24},{12,28},{16,0},{20,4},{24,8},{28,12},{1,17},{... | collective-permute-start | bytes 221192 | tf_op jit(solution)/shard_map/ppermute | solution.py:825
  100.0 6.2 %collective-permute-start.27 = (bf16[1,1,96,384]{3,2,1,0:T(8,128)(2,1)S(1)}, bf16[1,1,96,384]{3,2,1,0:T(8,128)(2,1)S(1)}, u32[]{:S(2)}, u32[]{:S(2)}) collective-permute-start(bf16[1,1,96,384]{3,2,1,0:T(8,128)(2,1)S(1)} %get-tuple-element.238), channel_id=1, source_target_pairs={{0,16},{4,20},{8,24},{12,28},{16,0},{20,4},{24,8},{28,12},{1,17},{... | collective-permute-start | bytes 221192 | tf_op jit(solution)/shard_map/ppermute | solution.py:825
  106.2 7.0 %collective-permute-start.29 = (bf16[96,768]{1,0:T(8,128)(2,1)S(1)}, bf16[96,768]{1,0:T(8,128)(2,1)S(1)}, u32[]{:S(2)}, u32[]{:S(2)}) collective-permute-start(bf16[96,768]{1,0:T(8,128)(2,1)S(1)} %get-tuple-element.243.refs_1_), channel_id=1, source_target_pairs={{0,2},{1,3},{2,0},{3,1},{4,6},{5,7},{6,4},{7,5},{8,10},{9,11},{10,... | collective-permute-start | bytes 442376 | tf_op jit(solution)/shard_map/ppermute | solution.py:825
  107.7 5.5 %collective-permute-start.25 = (f32[32,768]{1,0:T(8,128)S(1)}, f32[32,768]{1,0:T(8,128)S(1)}, u32[]{:S(2)}, u32[]{:S(2)}) collective-permute-start(f32[32,768]{1,0:T(8,128)S(1)} %get-tuple-element.232), channel_id=1, source_target_pairs={{0,16},{4,20},{8,24},{12,28},{16,0},{20,4},{24,8},{28,12},{1,17},{... | collective-permute-start | bytes 294920 | tf_op jit(solution)/shard_map/ppermute | solution.py:825
  113.3 1.6 %collective-permute-start.30 = (bf16[2,96,768]{2,1,0:T(8,128)(2,1)S(1)}, bf16[2,96,768]{2,1,0:T(8,128)(2,1)S(1)}, u32[]{:S(2)}, u32[]{:S(2)}) collective-permute-start(bf16[2,96,768]{2,1,0:T(8,128)(2,1)S(1)} %pad_maximum_fusion), channel_id=1, source_target_pairs={{0,1},{1,0},{2,3},{3,2},{4,5},{5,4},{6,7},{7,6},{8,9},{9,8},{10,11... | collective-permute-start | bytes 884744 | tf_op jit(solution)/shard_map/ppermute | solution.py:825
  (3 other events, 16.0 us)
